TPU v7x, 32 devices: a whole 2x2x4 slice. The times are simulated.
32 devices in a mesh: rows: 4 (over y, x), seq: 8 (over z, core).
Axes of the slice: x: 2, y: 2, z: 4, core: 2. Of those that a mesh axis runs over, the one named last changes fastest.
Arguments:
- tokens: bfloat16 [12, 1024, 1024], P('rows', 'seq'), may hold values from -6 to 6
- bounds: int32 [12, 8], P('rows'), may hold values from 1 to 1023, as said below
- norm1_gain: float32 [1024], replicated, may hold values from 0.5 to 1.5
- w_branch: bfloat16 [1024, 1536], P('seq'), may hold values from -0.1875 to 0.1875
- w_rec: bfloat16 [1024, 1536], P('seq'), may hold values from -0.1875 to 0.1875
- conv_weight: float32 [4, 1536], replicated, may hold values from -3 to 3
- conv_bias: float32 [1536], replicated, may hold values from -3 to 3
- w_rate: bfloat16 [1536, 1536], P('seq'), may hold values from -0.15625 to 0.15625
- rate_bias: float32 [1536], replicated, may hold values from -4 to 4
- w_input: bfloat16 [1536, 1536], P('seq'), may hold values from -0.15625 to 0.15625
- input_bias: float32 [1536], replicated, may hold values from -4 to 4
- decay_param: float32 [1536], replicated, may hold values from -14 to -3
- w_out: bfloat16 [1536, 1024], P('seq'), may hold values from -0.3125 to 0.3125
- norm2_gain: float32 [1024], replicated, may hold values from 0.5 to 1.5
- w_gate: bfloat16 [1024, 3072], P('seq'), may hold values from -0.1875 to 0.1875
- w_up: bfloat16 [1024, 3072], P('seq'), may hold values from -0.1875 to 0.1875
- w_down: bfloat16 [3072, 1024], P('seq'), may hold values from -0.15625 to 0.15625
- cotangent: bfloat16 [12, 1024, 1024], P('rows', 'seq'), may hold values from -6 to 6
Outputs:
- mixed: bfloat16 [12, 1024, 1024], P('rows', 'seq')
- token_grad: bfloat16 [12, 1024, 1024], P('rows', 'seq')
- grad_norm1: float32 [1024], replicated
- grad_w_branch: float32 [1024, 1536], P('seq')
- grad_w_rec: float32 [1024, 1536], P('seq')
- grad_conv_weight: float32 [4, 1536], replicated
- grad_conv_bias: float32 [1536], replicated
- grad_w_rate: float32 [1536, 1536], P('seq')
- grad_rate_bias: float32 [1536], replicated
- grad_w_input: float32 [1536, 1536], P('seq')
- grad_input_bias: float32 [1536], replicated
- grad_decay_param: float32 [1536], replicated
- grad_w_out: float32 [1536, 1024], P('seq')
- grad_norm2: float32 [1024], replicated
- grad_w_gate: float32 [1024, 3072], P('seq')
- grad_w_up: float32 [1024, 3072], P('seq')
- grad_w_down: float32 [3072, 1024], P('seq')
Inputs may be any that keep to these rules, and one draw needn't show every extreme that they name: `bounds`: sorted in each row, values may repeat. Each is the first token of a document; position 0 always starts one.
All inputs are finite; a program needn't handle non-finite values.
Results may differ from a plain program's by a relative error of at most 0.009.
Values may be sent and summed in bfloat16 or wider, within the bound.
A program may use at most 256 MiB of HBM per device.

v0:
```python
import jax
import jax.numpy as jnp
from jax import lax
from jax.sharding import PartitionSpec as P

epsilon = 1e-06


def from_behind(block, axis, distance):
    devices = range(lax.axis_size(axis))
    route = [(i - distance, i) for i in devices if i - distance in devices]
    return lax.ppermute(block, axis, route)


def prefix(part, axis, combine, identity, reverse):
    count = lax.axis_size(axis)
    place = lax.axis_index(axis)
    ahead = count - 1 - place if reverse else place
    gathered = jax.tree.map(lambda a: lax.all_gather(a, axis), part)
    state = jax.tree.map(lambda a, e: jnp.zeros_like(a) + jnp.asarray(e, a.dtype), part, identity)

    def one(turn, state):
        source = count - 1 - turn if reverse else turn
        return combine(
            state, jax.tree.map(lambda a: lax.dynamic_index_in_dim(a, source, 0, False), gathered)
        )

    return lax.fori_loop(0, ahead, one, state)


def rms_norm(values, gain):
    return values * lax.rsqrt(jnp.mean(values * values, axis=-1, keepdims=True) + epsilon) * gain


def combine(earlier, latter):
    return (earlier[0] * latter[0], latter[0] * earlier[1] + latter[1])


def conv_masks(padded_resets):
    keep_mask = 1.0 - padded_resets
    first = keep_mask[..., 3:]
    second = first * keep_mask[..., 2:-1]
    third = second * keep_mask[..., 1:-2]
    return (first, second, third)


def convolve(padded, masks, conv_weight, conv_bias):
    result = conv_bias + conv_weight[0] * padded[..., 3:, :]
    result = result + conv_weight[1] * masks[0][..., None] * padded[..., 2:-1, :]
    result = result + conv_weight[2] * masks[1][..., None] * padded[..., 1:-2, :]
    return result + conv_weight[3] * masks[2][..., None] * padded[..., :-3, :]


def gate_terms(rate_pre, input_pre, conv_out, decay_param, rate_bias, input_bias, resets):
    rate_gate = jax.nn.sigmoid(rate_pre + rate_bias)
    input_gate = jax.nn.sigmoid(input_pre + input_bias)
    log_rate = -8.0 * jax.nn.softplus(decay_param) * rate_gate
    keep_mask = 1.0 - resets[..., None]
    decays = jnp.exp(log_rate) * keep_mask
    scales = resets[..., None] + keep_mask * jnp.sqrt(-jnp.expm1(2.0 * log_rate))
    return (decays, scales * input_gate * conv_out)


def forward_product(values, weight):
    return jnp.dot(values, weight, preferred_element_type=jnp.float32)


def outer(left, right):
    return lax.dot_general(
        left, right, (((0,), (0,)), ((), ())), preferred_element_type=jnp.float32
    )


def back_product(grads, weight):
    return lax.dot_general(
        grads, weight, (((1,), (1,)), ((), ())), preferred_element_type=jnp.float32
    )


def body(
    tokens,
    bounds,
    norm1_gain,
    w_branch,
    w_rec,
    conv_weight,
    conv_bias,
    w_rate,
    rate_bias,
    w_input,
    input_bias,
    decay_param,
    w_out,
    norm2_gain,
    w_gate,
    w_up,
    w_down,
    cotangent,
):
    gathered = (
        lax.all_gather(w_branch, "seq", axis=0, tiled=True),
        lax.all_gather(w_rec, "seq", axis=0, tiled=True),
        lax.all_gather(w_rate, "seq", axis=0, tiled=True),
        lax.all_gather(w_input, "seq", axis=0, tiled=True),
        lax.all_gather(w_out, "seq", axis=0, tiled=True),
        lax.all_gather(w_gate, "seq", axis=0, tiled=True),
        lax.all_gather(w_up, "seq", axis=0, tiled=True),
        lax.all_gather(w_down, "seq", axis=0, tiled=True),
    )
    full_branch, full_rec, full_rate, full_input, full_out, full_gate, full_up, full_down = gathered
    row_count, tok_count, model_width = tokens.shape
    rec_width = full_rec.shape[1]
    offset = lax.axis_index("seq") * tok_count
    positions = offset - 3 + jnp.arange(tok_count + 3, dtype=jnp.int32)
    marked = (
        jnp.any(positions[None, :, None] == bounds[:, None, :], axis=2) | (positions == 0)[None, :]
    )
    padded_resets = marked.astype(jnp.float32)
    resets = padded_resets[:, 3:]
    masks = conv_masks(padded_resets)
    inputs = tokens.astype(jnp.float32).reshape(-1, model_width)
    normed = rms_norm(inputs, norm1_gain).astype(jnp.bfloat16)
    branch_pre = forward_product(normed, full_branch)
    rec_in = forward_product(normed, full_rec).reshape(row_count, tok_count, rec_width)
    rim = from_behind(rec_in[:, tok_count - 3 :, :], "seq", 1)
    padded = jnp.concatenate([rim, rec_in], axis=1)
    conv_out = convolve(padded, masks, conv_weight, conv_bias)
    conv_low = conv_out.astype(jnp.bfloat16).reshape(-1, rec_width)
    rate_pre = forward_product(conv_low, full_rate).reshape(conv_out.shape)
    input_pre = forward_product(conv_low, full_input).reshape(conv_out.shape)

    def gates_of(rate_arg, input_arg, conv_arg, decay_arg, rate_arg_bias, input_arg_bias):
        return gate_terms(
            rate_arg, input_arg, conv_arg, decay_arg, rate_arg_bias, input_arg_bias, resets
        )

    decays, drives = gates_of(rate_pre, input_pre, conv_out, decay_param, rate_bias, input_bias)
    prefix_decay, local_states = lax.associative_scan(combine, (decays, drives), axis=1)
    ones_pair = jnp.ones((row_count, rec_width), jnp.float32)
    zeros_pair = jnp.zeros((row_count, rec_width), jnp.float32)
    carry_in = prefix(
        (prefix_decay[:, -1], local_states[:, -1]), "seq", combine, (ones_pair, zeros_pair), False
    )[1]
    states = local_states + prefix_decay * carry_in[:, None, :]
    earlier_states = jnp.concatenate([carry_in[:, None, :], states[:, :-1, :]], axis=1)
    branch_act = jax.nn.gelu(branch_pre, approximate=True).reshape(states.shape)
    mixed_in = (states * branch_act).astype(jnp.bfloat16).reshape(-1, rec_width)
    resid = inputs + forward_product(mixed_in, full_out)
    normed2 = rms_norm(resid, norm2_gain).astype(jnp.bfloat16)
    gate_pre = forward_product(normed2, full_gate)
    up_pre = forward_product(normed2, full_up)
    hidden = (jax.nn.gelu(gate_pre, approximate=True) * up_pre).astype(jnp.bfloat16)
    mixed = (resid + forward_product(hidden, full_down)).astype(jnp.bfloat16).reshape(tokens.shape)
    cot_low = cotangent.reshape(-1, model_width)
    grad_down = outer(hidden, cot_low)
    grad_hidden = back_product(cot_low, full_down)
    _, pull_mlp = jax.vjp(
        lambda gate_arg, up_arg: jax.nn.gelu(gate_arg, approximate=True) * up_arg, gate_pre, up_pre
    )
    grad_gate_pre, grad_up_pre = pull_mlp(grad_hidden)
    gate_low = grad_gate_pre.astype(jnp.bfloat16)
    up_low = grad_up_pre.astype(jnp.bfloat16)
    grad_gate = outer(normed2, gate_low)
    grad_up = outer(normed2, up_low)
    grad_normed2 = back_product(gate_low, full_gate) + back_product(up_low, full_up)
    _, pull_norm2 = jax.vjp(rms_norm, resid, norm2_gain)
    grad_resid_norm, grad_norm2 = pull_norm2(grad_normed2)
    grad_resid = cot_low.astype(jnp.float32) + grad_resid_norm
    resid_low = grad_resid.astype(jnp.bfloat16)
    grad_out = outer(mixed_in, resid_low)
    grad_mixed = back_product(resid_low, full_out).reshape(states.shape)
    grad_states = grad_mixed * branch_act
    _, pull_branch = jax.vjp(lambda pre_arg: jax.nn.gelu(pre_arg, approximate=True), branch_pre)
    branch_low = pull_branch((grad_mixed * states).reshape(-1, rec_width))[0].astype(jnp.bfloat16)
    next_decays = jnp.concatenate([decays[:, 1:, :], ones_pair[:, None, :]], axis=1)
    suffix_decay, local_grads = lax.associative_scan(
        combine, (next_decays, grad_states), axis=1, reverse=True
    )
    element = (prefix_decay[:, -1], decays[:, 0] * local_grads[:, 0])
    carry_back = prefix(element, "seq", combine, (ones_pair, zeros_pair), True)[1]
    state_grads = local_grads + suffix_decay * carry_back[:, None, :]
    _, pull_gates = jax.vjp(
        gates_of, rate_pre, input_pre, conv_out, decay_param, rate_bias, input_bias
    )
    grad_rate_pre, grad_input_pre, grad_conv_direct, grad_decay, grad_rate_bias, grad_input_bias = (
        pull_gates((state_grads * earlier_states, state_grads))
    )
    rate_low = grad_rate_pre.astype(jnp.bfloat16).reshape(-1, rec_width)
    input_low = grad_input_pre.astype(jnp.bfloat16).reshape(-1, rec_width)
    grad_rate = outer(conv_low, rate_low)
    grad_input = outer(conv_low, input_low)
    grad_conv = grad_conv_direct + (
        back_product(rate_low, full_rate) + back_product(input_low, full_input)
    ).reshape(conv_out.shape)
    _, pull_conv = jax.vjp(
        lambda pad_arg, weight_arg, bias_arg: convolve(pad_arg, masks, weight_arg, bias_arg),
        padded,
        conv_weight,
        conv_bias,
    )
    grad_padded, grad_conv_weight, grad_conv_bias = pull_conv(grad_conv)
    rim_back = from_behind(grad_padded[:, :3, :], "seq", -1)
    grad_rec = grad_padded[:, 3:, :] + jnp.concatenate(
        [jnp.zeros((row_count, tok_count - 3, rec_width), jnp.float32), rim_back], axis=1
    )
    rec_low = grad_rec.astype(jnp.bfloat16).reshape(-1, rec_width)
    grad_rec_w = outer(normed, rec_low)
    grad_branch_w = outer(normed, branch_low)
    grad_normed = back_product(branch_low, full_branch) + back_product(rec_low, full_rec)
    _, pull_norm1 = jax.vjp(rms_norm, inputs, norm1_gain)
    grad_inputs, grad_norm1 = pull_norm1(grad_normed)
    token_grad = (grad_resid + grad_inputs).astype(jnp.bfloat16).reshape(tokens.shape)
    grad_mats = (
        grad_branch_w,
        grad_rec_w,
        grad_rate,
        grad_input,
        grad_out,
        grad_gate,
        grad_up,
        grad_down,
    )
    blocks = (
        lax.psum_scatter(grad_mats[0], "seq", scatter_dimension=0, tiled=True),
        lax.psum_scatter(grad_mats[1], "seq", scatter_dimension=0, tiled=True),
        lax.psum_scatter(grad_mats[2], "seq", scatter_dimension=0, tiled=True),
        lax.psum_scatter(grad_mats[3], "seq", scatter_dimension=0, tiled=True),
        lax.psum_scatter(grad_mats[4], "seq", scatter_dimension=0, tiled=True),
        lax.psum_scatter(grad_mats[5], "seq", scatter_dimension=0, tiled=True),
        lax.psum_scatter(grad_mats[6], "seq", scatter_dimension=0, tiled=True),
        lax.psum_scatter(grad_mats[7], "seq", scatter_dimension=0, tiled=True),
    )
    summed = lax.psum(
        (blocks[0], blocks[1], blocks[2], blocks[3], blocks[4], blocks[5], blocks[6], blocks[7]),
        "rows",
    )
    small = lax.psum(
        (
            grad_norm1,
            grad_conv_weight,
            grad_conv_bias,
            grad_rate_bias,
            grad_input_bias,
            grad_decay,
            grad_norm2,
        ),
        ("rows", "seq"),
    )
    return (
        mixed,
        token_grad,
        small[0],
        summed[0],
        summed[1],
        small[1],
        small[2],
        summed[2],
        small[3],
        summed[3],
        small[4],
        small[5],
        summed[4],
        small[6],
        summed[5],
        summed[6],
        summed[7],
    )


def solution(mesh):
    in_specs = (
        P("rows", "seq", None),
        P("rows", None),
        P(),
        P("seq", None),
        P("seq", None),
        P(),
        P(),
        P("seq", None),
        P(),
        P("seq", None),
        P(),
        P(),
        P("seq", None),
        P(),
        P("seq", None),
        P("seq", None),
        P("seq", None),
        P("rows", "seq", None),
    )
    out_specs = (
        P("rows", "seq", None),
        P("rows", "seq", None),
        P(),
        P("seq", None),
        P("seq", None),
        P(),
        P(),
        P("seq", None),
        P(),
        P("seq", None),
        P(),
        P(),
        P("seq", None),
        P(),
        P("seq", None),
        P("seq", None),
        P("seq", None),
    )
    return jax.shard_map(body, mesh=mesh, in_specs=in_specs, out_specs=out_specs, check_vma=False)
```

profile of v0, /device:TPU:0, one launch (start us, length us, event | category | flops | bytes accessed | tf_op | source)
XLA Modules:
  0.0 1805.0 jit_solution(5584287064794648267)
XLA Ops:
  14.7 36.0 %all-gather.12.cloned.1.call-done = bf16[1024,1536]{1,0:T(8,128)(2,1)} async-done(((bf16[128,1536]{1,0:T(8,128)(2,1)}), bf16[1024,1536]{1,0:T(8,128)(2,1)}) %all-gather.12.cloned.1.call-update) | async-done | bytes 3145744 | tf_op jit(solution)/shard_map/all_gather | solution.py:102
  56.4 33.1 %all-gather.18.cloned.1.call-done = bf16[1024,1536]{1,0:T(8,128)(2,1)} async-done(((bf16[128,1536]{1,0:T(8,128)(2,1)}), bf16[1024,1536]{1,0:T(8,128)(2,1)}) %all-gather.18.cloned.1.call-update) | async-done | bytes 3145744 | tf_op jit(solution)/shard_map/all_gather | solution.py:101
  98.8 43.0 %all-gather.14.cloned.1.call-done = bf16[1536,1536]{1,0:T(8,128)(2,1)} async-done(((bf16[192,1536]{1,0:T(8,128)(2,1)}), bf16[1536,1536]{1,0:T(8,128)(2,1)}) %all-gather.14.cloned.1.call-update) | async-done | bytes 4718608 | tf_op jit(solution)/shard_map/all_gather | solution.py:103
  146.7 47.1 %all-gather.16.cloned.1.call-done = bf16[1536,1536]{1,0:T(8,128)(2,1)} async-done(((bf16[192,1536]{1,0:T(8,128)(2,1)}), bf16[1536,1536]{1,0:T(8,128)(2,1)}) %all-gather.16.cloned.1.call-update) | async-done | bytes 4718608 | tf_op jit(solution)/shard_map/all_gather | solution.py:104
  193.8 10.2 fusion.94
  427.7 14.0 all-gather.1
  456.0 14.0 all-gather
  484.0 7.8 fusion.125
  491.8 7.8 fusion.126
  499.6 11.7 multiply_convert_fusion
  824.9 17.3 all-gather.2
  859.4 18.8 %rev.9 = f32[3,128,1536]{2,1,0:T(8,128)} reverse(f32[3,128,1536]{2,1,0:T(8,128)} %add.619), dimensions={1} | reverse | bytes 4718592 | tf_op jit(solution)/shard_map/rev | solution.py:176
  878.2 18.8 %rev.8 = f32[3,128,1536]{2,1,0:T(8,128)} reverse(f32[3,128,1536]{2,1,0:T(8,128)} %add.612), dimensions={1} | reverse | bytes 4718592 | tf_op jit(solution)/shard_map/rev | solution.py:176
  945.0 8.2 fusion.131
  953.3 8.3 fusion.132
  962.7 8.2 fusion.133
  971.0 29.5 %reduce-scatter.11.cloned.1.call-done = f32[128,1536]{1,0:T(8,128)} async-done(((f32[1024,1536]{1,0:T(8,128)}), f32[128,1536]{1,0:T(8,128)}) %reduce-scatter.11.cloned.1.call-update) | async-done | bytes 786448 | tf_op jit(solution)/shard_map/reduce_scatter | solution.py:225
  1000.5 100.1 %reduce-scatter.13.cloned.1.call-done = f32[192,1536]{1,0:T(8,128)} async-done(((f32[1536,1536]{1,0:T(8,128)}), f32[192,1536]{1,0:T(8,128)}) %reduce-scatter.13.cloned.1.call-update) | async-done | bytes 1179664 | tf_op jit(solution)/shard_map/reduce_scatter | solution.py:226
  1100.6 100.2 %reduce-scatter.15.cloned.1.call-done = f32[192,1536]{1,0:T(8,128)} async-done(((f32[1536,1536]{1,0:T(8,128)}), f32[192,1536]{1,0:T(8,128)}) %reduce-scatter.15.cloned.1.call-update) | async-done | bytes 1179664 | tf_op jit(solution)/shard_map/reduce_scatter | solution.py:227
  1200.8 129.8 %reduce-scatter.19.cloned.1.call-done = f32[128,3072]{1,0:T(8,128)} async-done(((f32[1024,3072]{1,0:T(8,128)}), f32[128,3072]{1,0:T(8,128)}) %reduce-scatter.19.cloned.1.call-update) | async-done | bytes 1572880 | tf_op jit(solution)/shard_map/reduce_scatter | solution.py:229
  1330.6 129.8 %reduce-scatter.21.cloned.1.call-done = f32[128,3072]{1,0:T(8,128)} async-done(((f32[1024,3072]{1,0:T(8,128)}), f32[128,3072]{1,0:T(8,128)}) %reduce-scatter.21.cloned.1.call-update) | async-done | bytes 1572880 | tf_op jit(solution)/shard_map/reduce_scatter | solution.py:230
  1460.3 129.8 %reduce-scatter.23.cloned.1.call-done = f32[384,1024]{1,0:T(8,128)} async-done(((f32[3072,1024]{1,0:T(8,128)}), f32[384,1024]{1,0:T(8,128)}) %reduce-scatter.23.cloned.1.call-update) | async-done | bytes 1572880 | tf_op jit(solution)/shard_map/reduce_scatter | solution.py:231
  1604.0 39.7 %all-reduce.67 = (f32[1024]{0:T(1024)}, f32[4,1536]{1,0:T(4,128)}, f32[1536]{0:T(1024)}, f32[1536]{0:T(1024)}, f32[1536]{0:T(1024)}, /*index=5*/f32[1536]{0:T(1024)}, f32[1024]{0:T(1024)}) all-reduce(f32[1024]{0:T(1024)S(1)} %get-tuple-element.156, ...), channel_id=1, replica_groups=mesh['rows'=4,'seq'=8] {'rows','seq'}, use_global_device_ids=true, to_apply=%region_10.11 | all-reduce | flops 14336 | bytes 114688 | tf_op jit(solution)/shard_map/psum | solution.py:237
  1646.5 140.3 %all-reduce.71.cloned.1.call-done = (f32[128,1536]{1,0:T(8,128)}, f32[128,1536]{1,0:T(8,128)}, f32[192,1536]{1,0:T(8,128)}, f32[192,1536]{1,0:T(8,128)}, f32[192...) async-done(((f32[128,1536]{1,0:T(8,128)}, f32[128,1536]{1,0:T(8,128)}, f32[192,1536]{1,0:T(8,128)}, f32[192,1536]{1,0:T(8,128)}, ...) | async-done | bytes 9437200 | tf_op jit(solution)/shard_map/psum | solution.py:233
  (579 shorter events, 691.3 us)
Async XLA Ops:
  7.2 43.5 %all-gather.12.cloned.1.call-start = ((), (), s32[]{:S(2)}) async-start(), calls=%async_computation.8 | async-start | bytes 3538944 | tf_op jit(solution)/shard_map/all_gather | solution.py:102
  7.9 81.6 %all-gather.18.cloned.1.call-start = ((), (), s32[]{:S(2)}) async-start(), calls=%async_computation.11 | async-start | bytes 3538944 | tf_op jit(solution)/shard_map/all_gather | solution.py:101
  8.7 133.1 %all-gather.14.cloned.1.call-start = ((), (), s32[]{:S(2)}) async-start(), calls=%async_computation.9 | async-start | bytes 5308416 | tf_op jit(solution)/shard_map/all_gather | solution.py:103
  9.5 184.4 %all-gather.16.cloned.1.call-start = ((), (), s32[]{:S(2)}) async-start(), calls=%async_computation.10 | async-start | bytes 5308416 | tf_op jit(solution)/shard_map/all_gather | solution.py:104
  10.0 468.0 %all-gather.20.cloned.1.call-start = ((), (), s32[]{:S(2)}) async-start(), calls=%async_computation.12 | async-start | bytes 3538944 | tf_op jit(solution)/shard_map/all_gather | solution.py:105
  10.6 473.4 %all-gather.22.cloned.1.call-start = ((), (), s32[]{:S(2)}) async-start(), calls=%async_computation.13 | async-start | bytes 7077888 | tf_op jit(solution)/shard_map/all_gather | solution.py:106
  11.2 480.6 %all-gather.24.cloned.1.call-start = ((), (), s32[]{:S(2)}) async-start(), calls=%async_computation.14 | async-start | bytes 7077888 | tf_op jit(solution)/shard_map/all_gather | solution.py:107
  12.0 487.6 %all-gather.26.cloned.1.call-start = ((), (), s32[]{:S(2)}) async-start(), calls=%async_computation.15 | async-start | bytes 7077888 | tf_op jit(solution)/shard_map/all_gather | solution.py:108
  12.7 958.3 %reduce-scatter.17.cloned.1.call-start = ((), (), s32[]{:S(2)}) async-start(), calls=%async_computation.20 | async-start | bytes 7077888 | tf_op jit(solution)/shard_map/reduce_scatter | solution.py:228
  13.3 82.2 %copy-start.93 = (f32[3,128]{1,0:T(4,128)}, f32[3,128]{1,0:T(4,128)S(1)}, u32[]{:S(2)}) copy-start(f32[3,128]{1,0:T(4,128)S(1)} %get-tuple-element.206) | copy-start | bytes 4612
  13.3 82.2 %copy-start.95 = (f32[3,128]{1,0:T(4,128)}, f32[3,128]{1,0:T(4,128)S(1)}, u32[]{:S(2)}) copy-start(f32[3,128]{1,0:T(4,128)S(1)} %get-tuple-element.207) | copy-start | bytes 4612
  13.3 82.2 %copy-start.97 = (f32[3,128]{1,0:T(4,128)}, f32[3,128]{1,0:T(4,128)S(1)}, u32[]{:S(2)}) copy-start(f32[3,128]{1,0:T(4,128)S(1)} %get-tuple-element.281) | copy-start | bytes 4612
  13.4 82.1 %copy-start.70 = (f32[1536]{0:T(1024)}, f32[1536]{0:T(1024)S(1)}, u32[]{:S(2)}) copy-start(f32[1536]{0:T(1024)S(1)} %get-tuple-element.158) | copy-start | bytes 18436
  13.4 82.1 %copy-start.72 = (f32[1536]{0:T(1024)}, f32[1536]{0:T(1024)S(1)}, u32[]{:S(2)}) copy-start(f32[1536]{0:T(1024)S(1)} %get-tuple-element.159) | copy-start | bytes 18436
  54.1 41.3 %collective-permute-start = (f32[3,3,1536]{2,1,0:T(4,128)S(1)}, f32[3,3,1536]{2,1,0:T(4,128)S(1)}, u32[]{:S(2)}, u32[]{:S(2)}) collective-permute-start(f32[3,3,1536]{2,1,0:T(4,128)S(1)} %slice.639), channel_id=1, source_target_pairs={{0,1},{1,2},{2,3},{3,4},{4,5},{5,6},{6,7},{8,9},{9,10},{10,11},{11... | collective-permute-start | bytes 165896 | tf_op jit(solution)/shard_map/ppermute | solution.py:12
  527.8 443.3 %reduce-scatter.9.cloned.1.call-start = ((), (), s32[]{:S(2)}) async-start(), calls=%async_computation.16 | async-start | bytes 7077888 | tf_op jit(solution)/shard_map/reduce_scatter | solution.py:224
  704.4 296.2 %reduce-scatter.11.cloned.1.call-start = ((), (), s32[]{:S(2)}) async-start(), calls=%async_computation.17 | async-start | bytes 7077888 | tf_op jit(solution)/shard_map/reduce_scatter | solution.py:225
  922.5 3.2 collective-permute-start.1
  930.6 170.0 %reduce-scatter.13.cloned.1.call-start = ((), (), s32[]{:S(2)}) async-start(), calls=%async_computation.18 | async-start | bytes 10616832 | tf_op jit(solution)/shard_map/reduce_scatter | solution.py:226
  937.4 263.4 %reduce-scatter.15.cloned.1.call-start = ((), (), s32[]{:S(2)}) async-start(), calls=%async_computation.19 | async-start | bytes 10616832 | tf_op jit(solution)/shard_map/reduce_scatter | solution.py:227
  943.9 386.7 %reduce-scatter.19.cloned.1.call-start = ((), (), s32[]{:S(2)}) async-start(), calls=%async_computation.21 | async-start | bytes 14155776 | tf_op jit(solution)/shard_map/reduce_scatter | solution.py:229
  953.2 507.1 %reduce-scatter.21.cloned.1.call-start = ((), (), s32[]{:S(2)}) async-start(), calls=%async_computation.22 | async-start | bytes 14155776 | tf_op jit(solution)/shard_map/reduce_scatter | solution.py:230
  961.6 628.5 %reduce-scatter.23.cloned.1.call-start = ((), (), s32[]{:S(2)}) async-start(), calls=%async_computation.23 | async-start | bytes 14155776 | tf_op jit(solution)/shard_map/reduce_scatter | solution.py:231
  970.9 815.9 %all-reduce.71.cloned.1.call-start = ((), (), s32[]{:S(2)}) async-start(), calls=%async_computation.24 | async-start | bytes 18874368 | tf_op jit(solution)/shard_map/psum | solution.py:233
  (111 other events, 991.1 us)
Sparse Core Ops, SparseCore 0:
  9.7 40.9 all-gather.11
  52.3 37.1 all-gather.17
  91.2 50.5 all-gather.13
  143.3 50.5 all-gather.15
  195.3 37.0 all-gather.19
  233.9 63.6 all-gather.21
  299.2 63.3 all-gather.23
  364.3 63.3 all-gather.25
  527.9 74.0 reduce-scatter.16
  704.5 74.1 reduce-scatter.8
  930.7 69.8 reduce-scatter.10
  1002.7 97.8 reduce-scatter.12
  1102.9 97.8 reduce-scatter.14
  1203.0 127.5 reduce-scatter.18
  1332.7 127.5 reduce-scatter.20
  1462.5 127.5 reduce-scatter.22
  1594.6 192.2 all-reduce.70
where the time goes:
time: 1820 us; the launch traced here: 1810 us
  waiting for transfers between devices  925 us (51%)
  local copies, waits for them, and re-layouts  467 us (26%)
  other arithmetic  173 us (10%)
  matrix products  135 us (7%)
  blocking collectives  85 us (5%)
    slice x49, local copies, waits for them, and re-layouts, body(): lax.associative_scan(combine, (next_decays, grad_states), axis=1, reverse...  142 us
    psum x1, waiting for transfers between devices, body(): lax.psum((blocks[0], blocks[1], blocks[2], blocks[3], blocks[4], blocks[5...  140 us
    reduce_scatter x1, waiting for transfers between devices, body(): lax.psum_scatter(grad_mats[7], 'seq', scatter_dimension=0, tiled=True)  130 us
    reduce_scatter x1, waiting for transfers between devices, body(): lax.psum_scatter(grad_mats[5], 'seq', scatter_dimension=0, tiled=True)  130 us
    reduce_scatter x1, waiting for transfers between devices, body(): lax.psum_scatter(grad_mats[6], 'seq', scatter_dimension=0, tiled=True)  130 us
    slice x44, local copies, waits for them, and re-layouts, body(): lax.associative_scan(combine, (decays, drives), axis=1)  102 us
    reduce_scatter x1, waiting for transfers between devices, body(): lax.psum_scatter(grad_mats[3], 'seq', scatter_dimension=0, tiled=True)  100 us
    reduce_scatter x1, waiting for transfers between devices, body(): lax.psum_scatter(grad_mats[2], 'seq', scatter_dimension=0, tiled=True)  100 us
  transfers between devices with their start and end apart: 19, of which 12 were waited for; matrix products, arithmetic and copies ran while one was open for 40% of the time, Pallas kernels for 0%

commit v1 on v0

--- a/solution.py
+++ b/solution.py
@@ -1,9 +1,496 @@
+import functools
+
 import jax
 import jax.numpy as jnp
 from jax import lax
+from jax.experimental import pallas as pl
+from jax.experimental.pallas import tpu as pltpu
 from jax.sharding import PartitionSpec as P
 
 epsilon = 1e-06
+MESH = pl.DeviceIdType.MESH
+ANY = pl.BlockSpec(memory_space=pl.ANY)
+VMEM = pl.BlockSpec(memory_space=pltpu.VMEM)
+
+
+def place():
+    r = lax.axis_index("rows")
+    s = lax.axis_index("seq")
+    return r, s, lax.div(s, 2), lax.rem(s, 2)
+
+
+def greet(peers):
+    barrier = pltpu.get_barrier_semaphore()
+    for peer in peers:
+        pl.semaphore_signal(barrier, inc=1, device_id=peer, device_id_type=MESH)
+    pl.semaphore_wait(barrier, len(peers))
+
+
+def peers_of(r, s, z, c):
+    mate = (r, s + 1 - 2 * c)
+    along_x = (r + 1 - 2 * lax.rem(r, 2), s)
+    along_y = (lax.rem(r + 2, 4), s)
+    along_z = [(r, lax.rem(z + k, 4) * 2 + c) for k in (1, 2, 3)]
+    return mate, along_x, along_y, along_z
+
+
+def gather_kernel(count, *refs):
+    shards, fulls = refs[:count], refs[count : 2 * count]
+    send, recv, local = refs[2 * count :]
+    r, s, z, c = place()
+    mate, along_x, along_y, along_z = peers_of(r, s, z, c)
+    across_x, across_y = along_x[0], along_y[0]
+    greet([mate, along_x, along_y] + along_z)
+
+    def remote(m, slot, src, dst, device):
+        return pltpu.make_async_remote_copy(
+            src_ref=src,
+            dst_ref=dst,
+            send_sem=send.at[m, slot],
+            recv_sem=recv.at[m, slot],
+            device_id=device,
+            device_id_type=MESH,
+        )
+
+    def region(m, source, quarter, begin, length):
+        depth, width = shards[m].shape
+        part = width // 4
+        row = pl.multiple_of((source * 2 + c) * depth + begin, 16)
+        column = pl.multiple_of(quarter * part, 128)
+        return fulls[m].at[pl.ds(row, length), pl.ds(column, part)]
+
+    live = []
+
+    def start(copy):
+        copy.start()
+        live.append(copy)
+        return copy
+
+    stage_own, stage_z, stage_x, stage_y, stage_d, stage_c = {}, {}, {}, {}, {}, {}
+
+    def begin(m):
+        depth, width = shards[m].shape
+        part = width // 4
+        rows = pl.ds(pl.multiple_of(s * depth, 16), depth)
+        own = pltpu.make_async_copy(shards[m], fulls[m].at[rows], local.at[m])
+        own.start()
+        column = pl.multiple_of(r * part, 128)
+        stage_z[m] = [
+            start(
+                remote(
+                    m,
+                    k,
+                    shards[m].at[:, pl.ds(column, part)],
+                    region(m, z, r, 0, depth),
+                    along_z[k - 1],
+                )
+            )
+            for k in (1, 2, 3)
+        ]
+        stage_own[m] = (own, start(remote(m, 0, shards[m], fulls[m].at[rows], mate)))
+
+    def sources(k):
+        return lax.rem(z + 4 - k, 4)
+
+    begin(0)
+    begin(1)
+    for tick in range(count + 2):
+        m = tick
+        if m < count:
+            depth = shards[m].shape[0]
+            stage_x[m], stage_y[m] = [], []
+            for k in (1, 2, 3):
+                stage_z[m][k - 1].wait_recv()
+                piece = region(m, sources(k), r, 0, depth)
+                stage_x[m].append(start(remote(m, 3 + k, piece, piece, along_x)))
+                stage_y[m].append(start(remote(m, 6 + k, piece, piece, along_y)))
+        if tick + 2 < count:
+            begin(tick + 2)
+        m = tick - 1
+        if 0 <= m < count:
+            depth = shards[m].shape[0]
+            half = depth // 2
+            stage_d[m] = []
+            for k in (1, 2, 3):
+                stage_x[m][k - 1].wait_recv()
+                piece = region(m, sources(k), across_x, 0, half)
+                stage_d[m].append(start(remote(m, 9 + k, piece, piece, along_y)))
+                stage_y[m][k - 1].wait_recv()
+                piece = region(m, sources(k), across_y, half, half)
+                stage_d[m].append(start(remote(m, 12 + k, piece, piece, along_x)))
+        m = tick - 2
+        if 0 <= m < count:
+            depth = shards[m].shape[0]
+            stage_c[m] = []
+            for k in (1, 2, 3):
+                stage_d[m][2 * k - 2].wait_recv()
+                stage_d[m][2 * k - 1].wait_recv()
+                rows = pl.ds(pl.multiple_of((sources(k) * 2 + c) * depth, 16), depth)
+                piece = fulls[m].at[rows]
+                stage_c[m].append(start(remote(m, 15 + k, piece, piece, mate)))
+    for m in range(count):
+        own, twin = stage_own[m]
+        own.wait()
+        twin.wait_recv()
+        for copy in stage_c[m]:
+            copy.wait_recv()
+    for copy in live:
+        copy.wait_send()
+
+
+def gather_all(shards, axis_size):
+    if axis_size != 8 or lax.axis_size("rows") != 4:
+        return tuple(lax.all_gather(a, "seq", axis=0, tiled=True) for a in shards)
+    count = len(shards)
+    return pl.pallas_call(
+        functools.partial(gather_kernel, count),
+        out_shape=tuple(
+            jax.ShapeDtypeStruct((a.shape[0] * axis_size, a.shape[1]), a.dtype) for a in shards
+        ),
+        in_specs=[ANY] * count,
+        out_specs=(ANY,) * count,
+        scratch_shapes=[
+            pltpu.SemaphoreType.DMA((count, 19)),
+            pltpu.SemaphoreType.DMA((count, 19)),
+            pltpu.SemaphoreType.DMA((count,)),
+        ],
+        compiler_params=pltpu.CompilerParams(collective_id=0, has_side_effects=True),
+        name="gather_weights",
+    )(*shards)
+
+
+def blocks_add(total, term, lead, rows):
+    def one(i, carry):
+        total_at = total(i)
+        total_at[...] = total_at[...] + term(i)[...]
+        return carry
+
+    lax.fori_loop(0, lead, one, 0)
+
+
+def reduce_kernel(count, has_small, *refs):
+    refs = list(refs)
+    grads = [refs.pop(0) for _ in range(count)]
+    small_in = refs.pop(0) if has_small else None
+    outs = [refs.pop(0) for _ in range(count)]
+    small_out = refs.pop(0) if has_small else None
+    held, own, first, second, third, final = (
+        [refs.pop(0) for _ in range(count)] for _ in range(6)
+    )
+    send, recv, local = refs.pop(0), refs.pop(0), refs.pop(0)
+    if has_small:
+        small_held, small_got, small_send, small_recv = refs
+    r, s, z, c = place()
+    mate, along_x, along_y, along_z = peers_of(r, s, z, c)
+    across_x, across_y = along_x[0], along_y[0]
+    diagonal = (3 - r, s)
+    rx, ry = lax.rem(r, 2), lax.div(r, 2)
+    greet([mate, along_x, along_y, diagonal] + along_z)
+    live = []
+
+    def remote(m, slot, src, dst, device):
+        copy = pltpu.make_async_remote_copy(
+            src_ref=src,
+            dst_ref=dst,
+            send_sem=send.at[m, slot],
+            recv_sem=recv.at[m, slot],
+            device_id=device,
+            device_id_type=MESH,
+        )
+        copy.start()
+        live.append(copy)
+        return copy
+
+    at_c, at_one, at_two, at_z, at_end, at_out = {}, {}, {}, {}, {}, {}
+
+    def begin(m):
+        part = held[m].shape[3]
+        at_c[m] = []
+        for q in range(4):
+            columns = pl.ds(q * part, part)
+            far = remote(m, q, grads[m].at[:, 1 - c, :, columns], held[m].at[q], mate)
+            near = pltpu.make_async_copy(
+                grads[m].at[:, c, :, columns], own[m].at[q], local.at[m, q]
+            )
+            near.start()
+            at_c[m].append((far, near))
+
+    small_copies = []
+
+    def small_exchange(slot, device):
+        copy = pltpu.make_async_remote_copy(
+            src_ref=small_held.at[slot],
+            dst_ref=small_got.at[slot],
+            send_sem=small_send.at[slot],
+            recv_sem=small_recv.at[slot],
+            device_id=device,
+            device_id_type=MESH,
+        )
+        copy.start()
+        small_copies.append(copy)
+        return copy
+
+    if has_small:
+        small_held[0] = small_in[...]
+        swap = small_exchange(0, mate)
+    begin(0)
+    if count > 1:
+        begin(1)
+    for tick in range(count + 4):
+        m = tick
+        if m < count:
+            _, _, depth, part = held[m].shape
+            half = depth // 2
+            for far, near in at_c[m]:
+                far.wait_recv()
+                near.wait()
+
+            def add_all(i, carry, m=m):
+                q, b = lax.div(i, 4), lax.rem(i, 4)
+                held[m][q, b] = held[m][q, b] + own[m][q, b]
+                return carry
+
+            lax.fori_loop(0, 16, add_all, 0)
+            at_one[m] = []
+            for other in range(2):
+                quarter = other * 2 + (1 - rx)
+                at_one[m].append(
+                    remote(
+                        m,
+                        4 + other,
+                        held[m].at[quarter, :, pl.ds(0, half)],
+                        first[m].at[0, other],
+                        along_x,
+                    )
+                )
+                quarter = (1 - ry) * 2 + other
+                at_one[m].append(
+                    remote(
+                        m,
+                        6 + other,
+                        held[m].at[quarter, :, pl.ds(half, half)],
+                        first[m].at[1, other],
+                        along_y,
+                    )
+                )
+        if tick + 2 < count:
+            begin(tick + 2)
+        m = tick - 1
+        if 0 <= m < count:
+            _, _, depth, part = held[m].shape
+            half = depth // 2
+            for copy in at_one[m]:
+                copy.wait_recv()
+
+            def add_one(i, carry, m=m, half=half):
+                other, b = lax.div(i, 4), lax.rem(i, 4)
+                qx = other * 2 + rx
+                held[m][qx, b, :half] = held[m][qx, b, :half] + first[m][0, other, b]
+                qy = ry * 2 + other
+                held[m][qy, b, half:] = held[m][qy, b, half:] + first[m][1, other, b]
+                return carry
+
+            lax.fori_loop(0, 8, add_one, 0)
+            at_two[m] = [
+                remote(
+                    m,
+                    8,
+                    held[m].at[(1 - ry) * 2 + rx, :, pl.ds(0, half)],
+                    second[m].at[0],
+                    along_y,
+                ),
+                remote(
+                    m,
+                    9,
+                    held[m].at[ry * 2 + (1 - rx), :, pl.ds(half, half)],
+                    second[m].at[1],
+                    along_x,
+                ),
+            ]
+        if has_small and tick == 1:
+            swap.wait_recv()
+            small_held[1] = small_held[0] + small_got[0]
+            swap = small_exchange(1, along_x)
+        m = tick - 2
+        if 0 <= m < count:
+            _, _, depth, part = held[m].shape
+            half = depth // 2
+            for copy in at_two[m]:
+                copy.wait_recv()
+
+            def add_two(b, carry, m=m, half=half):
+                held[m][r, b, :half] = held[m][r, b, :half] + second[m][0, b]
+                held[m][r, b, half:] = held[m][r, b, half:] + second[m][1, b]
+                return carry
+
+            lax.fori_loop(0, 4, add_two, 0)
+            at_z[m] = [
+                remote(
+                    m,
+                    9 + k,
+                    held[m].at[r, lax.rem(z + k, 4)],
+                    third[m].at[k - 1],
+                    along_z[k - 1],
+                )
+                for k in (1, 2, 3)
+            ]
+        if has_small and tick == 2:
+            swap.wait_recv()
+            small_held[2] = small_held[1] + small_got[1]
+            swap = small_exchange(2, along_y)
+        m = tick - 3
+        if 0 <= m < count:
+            for copy in at_z[m]:
+                copy.wait_recv()
+            mine = held[m][r, z].astype(jnp.float32)
+            for k in range(3):
+                mine = mine + third[m][k].astype(jnp.float32)
+            final[m][r] = mine.astype(jnp.bfloat16)
+            at_end[m] = [
+                remote(m, 13 + i, final[m].at[r], final[m].at[r], device)
+                for i, device in enumerate((along_x, along_y, diagonal))
+            ]
+        if has_small and tick == 3:
+            swap.wait_recv()
+            small_held[3] = small_held[2] + small_got[2]
+            spread = []
+            for k in (1, 2, 3):
+                copy = pltpu.make_async_remote_copy(
+                    src_ref=small_held.at[3],
+                    dst_ref=small_got.at[2 + k],
+                    send_sem=small_send.at[2 + k],
+                    recv_sem=small_recv.at[2 + k],
+                    device_id=along_z[k - 1],
+                    device_id_type=MESH,
+                )
+                copy.start()
+                small_copies.append(copy)
+                spread.append(copy)
+        m = tick - 4
+        if 0 <= m < count:
+            for copy in at_end[m]:
+                copy.wait_recv()
+            out = pltpu.make_async_copy(final[m], outs[m], local.at[m, 4])
+            out.start()
+            at_out[m] = out
+    if has_small:
+        for copy in spread:
+            copy.wait_recv()
+        small_got[6] = small_held[3]
+        total = None
+        for source in range(4):
+            k = lax.rem(z + 4 - source, 4)
+            slot = jnp.where(k == 0, 6, 2 + k)
+            term = small_got[slot]
+            total = term if total is None else total + term
+        small_out[...] = total
+        for copy in small_copies:
+            copy.wait_send()
+    for m in range(count):
+        at_out[m].wait()
+    for copy in live:
+        copy.wait_send()
+
+
+def reduce_all(grads, small, axis_size, tag):
+    if axis_size != 8 or lax.axis_size("rows") != 4:
+        blocks = [
+            lax.psum(lax.psum_scatter(g, "seq", scatter_dimension=0, tiled=True), "rows")
+            for g in grads
+        ]
+        if small is not None:
+            small = lax.psum(small, ("rows", "seq"))
+        return [b.astype(jnp.float32) for b in blocks], small
+    count = len(grads)
+    shapes = [(g.shape[0] // axis_size, g.shape[1] // 4) for g in grads]
+    views = [g.reshape(4, 2, k, 4 * n) for g, (k, n) in zip(grads, shapes)]
+    low = jnp.bfloat16
+    out_shape = [jax.ShapeDtypeStruct((4, k, n), low) for k, n in shapes]
+    out_specs = [ANY] * count
+    in_specs = [ANY] * count
+    scratch = [pltpu.VMEM((4, 4, k, n), low) for k, n in shapes]
+    scratch += [pltpu.VMEM((4, 4, k, n), low) for k, n in shapes]
+    scratch += [pltpu.VMEM((2, 2, 4, k // 2, n), low) for k, n in shapes]
+    scratch += [pltpu.VMEM((2, 4, k // 2, n), low) for k, n in shapes]
+    scratch += [pltpu.VMEM((3, k, n), low) for k, n in shapes]
+    scratch += [pltpu.VMEM((4, k, n), low) for k, n in shapes]
+    scratch += [
+        pltpu.SemaphoreType.DMA((count, 16)),
+        pltpu.SemaphoreType.DMA((count, 16)),
+        pltpu.SemaphoreType.DMA((count, 5)),
+    ]
+    args = list(views)
+    if small is not None:
+        args.append(small)
+        in_specs.append(VMEM)
+        out_shape.append(jax.ShapeDtypeStruct(small.shape, small.dtype))
+        out_specs.append(VMEM)
+        scratch += [
+            pltpu.VMEM((4,) + small.shape, small.dtype),
+            pltpu.VMEM((7,) + small.shape, small.dtype),
+            pltpu.SemaphoreType.DMA((6,)),
+            pltpu.SemaphoreType.DMA((6,)),
+        ]
+    results = pl.pallas_call(
+        functools.partial(reduce_kernel, count, small is not None),
+        out_shape=tuple(out_shape),
+        in_specs=in_specs,
+        out_specs=tuple(out_specs),
+        scratch_shapes=scratch,
+        compiler_params=pltpu.CompilerParams(
+            collective_id=tag, has_side_effects=True, vmem_limit_bytes=60 * 1024 * 1024
+        ),
+        name="reduce_grads",
+    )(*args)
+    blocks = [
+        b.transpose(1, 0, 2).reshape(k, 4 * n).astype(jnp.float32)
+        for b, (k, n) in zip(results[:count], shapes)
+    ]
+    return blocks, (results[count] if small is not None else None)
+
+
+def scan_kernel(reverse, a_ref, b_ref, p_ref, h_ref):
+    steps, width = a_ref.shape[1:]
+    tiles = steps // 8
+    spot = lax.broadcasted_iota(jnp.int32, (8, width), 0)
+
+    def shift(values, distance, fill):
+        if reverse:
+            moved = pltpu.roll(values, 8 - distance, 0)
+            return jnp.where(spot >= 8 - distance, fill, moved)
+        moved = pltpu.roll(values, distance, 0)
+        return jnp.where(spot < distance, fill, moved)
+
+    def tile(i, carry):
+        carry_a, carry_b = carry
+        t = tiles - 1 - i if reverse else i
+        rows = pl.ds(pl.multiple_of(t * 8, 8), 8)
+        a, b = a_ref[0, rows, :], b_ref[0, rows, :]
+        for distance in (1, 2, 4):
+            b = b + a * shift(b, distance, 0.0)
+            a = a * shift(a, distance, 1.0)
+        b = b + a * carry_b
+        a = a * carry_a
+        p_ref[0, rows, :] = a
+        h_ref[0, rows, :] = b
+        edge = slice(0, 1) if reverse else slice(7, 8)
+        return a[edge], b[edge]
+
+    ones, zeros = jnp.ones((1, width), jnp.float32), jnp.zeros((1, width), jnp.float32)
+    lax.fori_loop(0, tiles, tile, (ones, zeros))
+
+
+def scan(a, b, reverse):
+    count, steps, width = a.shape
+    block = pl.BlockSpec((1, steps, 512), lambda i, j: (i, 0, j))
+    return pl.pallas_call(
+        functools.partial(scan_kernel, reverse),
+        grid=(count, width // 512),
+        in_specs=[block, block],
+        out_specs=(block, block),
+        out_shape=(jax.ShapeDtypeStruct(a.shape, a.dtype),) * 2,
+        name="scan_back" if reverse else "scan_ahead",
+    )(a, b)
 
 
 def from_behind(block, axis, distance):
@@ -97,17 +584,10 @@
     w_down,
     cotangent,
 ):
-    gathered = (
-        lax.all_gather(w_branch, "seq", axis=0, tiled=True),
-        lax.all_gather(w_rec, "seq", axis=0, tiled=True),
-        lax.all_gather(w_rate, "seq", axis=0, tiled=True),
-        lax.all_gather(w_input, "seq", axis=0, tiled=True),
-        lax.all_gather(w_out, "seq", axis=0, tiled=True),
-        lax.all_gather(w_gate, "seq", axis=0, tiled=True),
-        lax.all_gather(w_up, "seq", axis=0, tiled=True),
-        lax.all_gather(w_down, "seq", axis=0, tiled=True),
-    )
-    full_branch, full_rec, full_rate, full_input, full_out, full_gate, full_up, full_down = gathered
+    axis_size = lax.axis_size("seq")
+    full_rec, full_rate, full_input, full_branch, full_out, full_gate, full_up, full_down = gather_all(
+        (w_rec, w_rate, w_input, w_branch, w_out, w_gate, w_up, w_down), axis_size
+    )
     row_count, tok_count, model_width = tokens.shape
     rec_width = full_rec.shape[1]
     offset = lax.axis_index("seq") * tok_count
@@ -135,7 +615,7 @@
         )
 
     decays, drives = gates_of(rate_pre, input_pre, conv_out, decay_param, rate_bias, input_bias)
-    prefix_decay, local_states = lax.associative_scan(combine, (decays, drives), axis=1)
+    prefix_decay, local_states = scan(decays, drives, False)
     ones_pair = jnp.ones((row_count, rec_width), jnp.float32)
     zeros_pair = jnp.zeros((row_count, rec_width), jnp.float32)
     carry_in = prefix(
@@ -173,9 +653,7 @@
     _, pull_branch = jax.vjp(lambda pre_arg: jax.nn.gelu(pre_arg, approximate=True), branch_pre)
     branch_low = pull_branch((grad_mixed * states).reshape(-1, rec_width))[0].astype(jnp.bfloat16)
     next_decays = jnp.concatenate([decays[:, 1:, :], ones_pair[:, None, :]], axis=1)
-    suffix_decay, local_grads = lax.associative_scan(
-        combine, (next_decays, grad_states), axis=1, reverse=True
-    )
+    suffix_decay, local_grads = scan(next_decays, grad_states, True)
     element = (prefix_decay[:, -1], decays[:, 0] * local_grads[:, 0])
     carry_back = prefix(element, "seq", combine, (ones_pair, zeros_pair), True)[1]
     state_grads = local_grads + suffix_decay * carry_back[:, None, :]
@@ -210,42 +688,46 @@
     _, pull_norm1 = jax.vjp(rms_norm, inputs, norm1_gain)
     grad_inputs, grad_norm1 = pull_norm1(grad_normed)
     token_grad = (grad_resid + grad_inputs).astype(jnp.bfloat16).reshape(tokens.shape)
-    grad_mats = (
-        grad_branch_w,
-        grad_rec_w,
-        grad_rate,
-        grad_input,
-        grad_out,
-        grad_gate,
-        grad_up,
-        grad_down,
-    )
-    blocks = (
-        lax.psum_scatter(grad_mats[0], "seq", scatter_dimension=0, tiled=True),
-        lax.psum_scatter(grad_mats[1], "seq", scatter_dimension=0, tiled=True),
-        lax.psum_scatter(grad_mats[2], "seq", scatter_dimension=0, tiled=True),
-        lax.psum_scatter(grad_mats[3], "seq", scatter_dimension=0, tiled=True),
-        lax.psum_scatter(grad_mats[4], "seq", scatter_dimension=0, tiled=True),
-        lax.psum_scatter(grad_mats[5], "seq", scatter_dimension=0, tiled=True),
-        lax.psum_scatter(grad_mats[6], "seq", scatter_dimension=0, tiled=True),
-        lax.psum_scatter(grad_mats[7], "seq", scatter_dimension=0, tiled=True),
-    )
-    summed = lax.psum(
-        (blocks[0], blocks[1], blocks[2], blocks[3], blocks[4], blocks[5], blocks[6], blocks[7]),
-        "rows",
-    )
-    small = lax.psum(
-        (
-            grad_norm1,
-            grad_conv_weight,
-            grad_conv_bias,
-            grad_rate_bias,
-            grad_input_bias,
-            grad_decay,
-            grad_norm2,
-        ),
-        ("rows", "seq"),
-    )
+    low = jnp.bfloat16
+    ff, _ = reduce_all(
+        [g.astype(low) for g in (grad_down, grad_gate, grad_up)], None, axis_size, 1
+    )
+    flat = jnp.concatenate(
+        [
+            g.reshape(-1)
+            for g in (
+                grad_norm1,
+                grad_conv_weight,
+                grad_conv_bias,
+                grad_rate_bias,
+                grad_input_bias,
+                grad_decay,
+                grad_norm2,
+            )
+        ]
+    )
+    size = flat.shape[0]
+    flat = jnp.pad(flat, (0, -size % 8192)).reshape(-1, 1024)
+    rec, flat = reduce_all(
+        [g.astype(low) for g in (grad_out, grad_rate, grad_input, grad_branch_w, grad_rec_w)],
+        flat,
+        axis_size,
+        2,
+    )
+    flat = flat.reshape(-1)
+    small, begin = [], 0
+    for like in (
+        grad_norm1,
+        grad_conv_weight,
+        grad_conv_bias,
+        grad_rate_bias,
+        grad_input_bias,
+        grad_decay,
+        grad_norm2,
+    ):
+        small.append(flat[begin : begin + like.size].reshape(like.shape))
+        begin += like.size
+    summed = (rec[3], rec[4], rec[1], rec[2], rec[0], ff[1], ff[2], ff[0])
     return (
         mixed,
         token_grad,

time: 1820 us -> 670 us (0.37)
  waiting for transfers between devices: 925 us -> 0.01 us
  local copies, waits for them, and re-layouts: 467 us -> 45.6 us
  Pallas kernels: 0 us -> 411 us
  other arithmetic: 173 us -> 49.3 us
  blocking collectives: 85 us -> 48.8 us
  matrix products: 135 us -> 99.8 us
    reduce_scatter x8 -> x0, waiting for transfers between devices: 619 us -> none  [the longest x1 130 us: body(): lax.psum_scatter(grad_mats[7], 'seq', scatter_dimension=0, tiled=True)]
    pallas_call x0 -> x5, Pallas kernels: none -> 411 us  [the longest x2 241 us: reduce_all(): pl.pallas_call(functools.partial(reduce_kernel, count, small is not None)...]
    slice x93 -> x5, local copies, waits for them, and re-layouts: 243 us -> 4.61 us  [the longest x3 2.76 us: body(): small.append(flat[begin:begin + like.size].reshape(like.shape))]
    all_gather x8 -> x0, waiting for transfers between devices: 159 us -> none  [the longest x1 47.1 us: body(): lax.all_gather(w_input, 'seq', axis=0, tiled=True)]
    pad x48 -> x1, local copies, waits for them, and re-layouts: 155 us -> 0.01 us  [body(): flat = jnp.pad(flat, (0, -size % 8192)).reshape(-1, 1024)]
    psum x1 -> x0, waiting for transfers between devices: 140 us -> none  [body(): lax.psum((blocks[0], blocks[1], blocks[2], blocks[3], blocks[4], blocks[5...]
    add x27 -> x0, other arithmetic: 51.3 us -> none  [the longest x14 31.1 us: body(): lax.associative_scan(combine, (next_decays, grad_states), axis=1, reverse...]
    psum x1 -> x0, blocking collectives: 39.7 us -> none  [body(): lax.psum((grad_norm1, grad_conv_weight, grad_conv_bias, grad_rate_bias, g...]
  transfers between devices with their start and end apart: 19 -> 2, of which waited for: 12 -> 0; matrix products, arithmetic and copies ran while one was open for 40% -> 4% of each run, Pallas kernels for 0% -> 18%
where the time goes in v1:
time: 670 us; the launch traced here: 660 us
  Pallas kernels  411 us (61%)
  matrix products  99.8 us (15%)
  other arithmetic  49.3 us (7%)
  blocking collectives  48.8 us (7%)
  local copies, waits for them, and re-layouts  45.6 us (7%)
    pallas_call x2, Pallas kernels, reduce_all(): pl.pallas_call(functools.partial(reduce_kernel, count, small is not None)...  241 us
    pallas_call x1, Pallas kernels, gather_all(): pl.pallas_call(functools.partial(gather_kernel, count), out_shape=tuple((...  152 us
    all_gather x3, blocking collectives, prefix(): gathered = jax.tree.map(lambda a: lax.all_gather(a, axis), part)  48.8 us
    dot_general x8, matrix products, outer(): lax.dot_general(left, right, (((0,), (0,)), ((), ())), preferred_element_...  35.9 us
    dot_general x8, matrix products, forward_product(): return jnp.dot(values, weight, preferred_element_type=jnp.float32)  34.4 us
    dot_general x8, matrix products, back_product(): lax.dot_general(grads, weight, (((1,), (1,)), ((), ())), preferred_elemen...  29.5 us
    unnamed x189, local copies, waits for them, and re-layouts  18.9 us
    pallas_call x2, Pallas kernels, scan(): pl.pallas_call(functools.partial(scan_kernel, reverse), grid=(count, widt...  17.5 us
  transfers between devices with their start and end apart: 2, of which 0 were waited for; matrix products, arithmetic and copies ran while one was open for 4% of the time, Pallas kernels for 18%

profile of v1, /device:TPU:0, one launch (start us, length us, event | category | flops | bytes accessed | tf_op | source)
XLA Modules:
  0.0 659.6 jit_solution(16393723772990441473)
XLA Ops:
  2.1 152.2 %gather_weights.1 = (bf16[1024,1536]{1,0:T(8,128)(2,1)}, bf16[1536,1536]{1,0:T(8,128)(2,1)}, bf16[1536,1536]{1,0:T(8,128)(2,1)}, bf16[1024,1536]{1,0:T(8,128)(2,...) custom-call(bf16[128,1536]{1,0:T(8,128)(2,1)} %refs_0_.1, ...), custom_call_target="tpu_custom_call" | custom-call | tf_op jit(solution)/shard_map/gather_weights/pallas_call | solution.py:145
  159.8 5.7 multiply_multiply_fusion.11
  167.8 5.8 fusion.38
  173.7 5.9 fusion.84
  181.7 8.7 %scan_ahead.1 = (f32[3,128,1536]{2,1,0:T(8,128)}, f32[3,128,1536]{2,1,0:T(8,128)}) custom-call(f32[3,128,1536]{2,1,0:T(8,128)} %copy-done.7, f32[3,128,1536]{2,1,0:T(8,128)} %get-tuple-element.289.b_ref), custom_call_target="tpu_custom_call" | custom-call | tf_op jit(solution)/shard_map/scan_ahead/pallas_call | solution.py:486
  191.4 15.0 %all-gather = f32[24,1,1536]{2,1,0:T(1,128)S(1)} all-gather(f32[3,1,1536]{2,1,0:T(1,128)S(1)} %slice.108), channel_id=2, replica_groups=mesh['rows'=4,'seq'=8] {'seq'}, dimensions={0}, use_global_device_ids=true | all-gather | bytes 165888 | tf_op jit(solution)/shard_map/all_gather | solution.py:506
  209.3 14.3 %all-gather.1 = f32[24,1,1536]{2,1,0:T(1,128)S(1)} all-gather(f32[3,1,1536]{2,1,0:T(1,128)S(1)} %slice.109), channel_id=3, replica_groups=mesh['rows'=4,'seq'=8] {'seq'}, dimensions={0}, use_global_device_ids=true | all-gather | bytes 165888 | tf_op jit(solution)/shard_map/all_gather | solution.py:506
  234.2 4.2 fusion.101
  238.4 4.4 fusion.102
  242.8 10.7 %fusion.7 = (bf16[384,3072]{1,0:T(8,128)(2,1)}, bf16[384,3072]{1,0:T(8,128)(2,1)}, bf16[384,3072]{1,0:T(8,128)(2,1)}) fusion(f32[384,3072]{1,0:T(8,128)} %fusion.101, f32[384,3072]{1,0:T(8,128)} %fusion.102, bf16[3072,1024]{1,0:T(8,128)(2,1)S(1)} %bitcast.227, bf16[384,1024]{1,0:T(8,128)(2,1)S(1)} %bitcast.220), kind=kOutput, calls=%fused_computation.21 | convolution fusion | flops 2446589952 | bytes 23592960 | tf_op jit(solution)/shard_map/dot_general | solution.py:562
  253.5 4.4 fusion.103
  270.2 8.8 %scan_back.1 = (f32[3,128,1536]{2,1,0:T(8,128)}, f32[3,128,1536]{2,1,0:T(8,128)}) custom-call(f32[3,128,1536]{2,1,0:T(8,128)} %concatenate.16.a_ref, f32[3,128,1536]{2,1,0:T(8,128)} %get-tuple-element.295.b_ref), custom_call_target="tpu_custom_call" | custom-call | tf_op jit(solution)/shard_map/scan_back/pallas_call | solution.py:486
  280.0 19.5 %all-gather.2 = f32[24,1,1536]{2,1,0:T(1,128)S(1)} all-gather(f32[3,1,1536]{2,1,0:T(1,128)S(1)} %slice_multiply_fusion), channel_id=4, replica_groups=mesh['rows'=4,'seq'=8] {'seq'}, dimensions={0}, use_global_device_ids=true | all-gather | bytes 165888 | tf_op jit(solution)/shard_map/all_gather | solution.py:506
  302.1 5.4 while.27
  307.6 6.8 %fusion.92 = (f32[1536]{0:T(1024)}, bf16[3,128,1536]{2,1,0:T(8,128)(2,1)S(1)}, f32[3,128,1536]{2,1,0:T(8,128)S(1)}) fusion(f32[3,128,1536]{2,1,0:T(8,128)} %get-tuple-element.308, f32[3,128,1536]{2,1,0:T(8,128)} %copy-done, f32[3,128,1536]{2,1,0:T(8,128)S(1)} %fusion.38, f32[1536]{0:T(1024)S(1)} %fusion.89, f32[3,128]{1,0:T(4,128)} %copy-done.49, ...), kind=kLoop, calls=%fused_computation.176 | loop fusion | flops 8256000 | bytes 15369216 | tf_op jit(solution)/shard_map/transpose(jvp())/reduce_sum | solution.py:543
  314.5 4.3 multiply_reduce_fusion
  323.6 4.3 multiply_reduce_fusion.4
  335.1 4.3 bitcast_convert_fusion.1
  339.4 4.6 bitcast_convert_fusion
  355.5 5.4 convolution_convert_fusion.2
  360.9 5.4 convolution_convert_fusion.1
  366.4 5.6 convolution_convert_fusion
  373.3 121.4 %reduce_grads.3 = (bf16[4,384,256]{2,1,0:T(8,128)(2,1)}, bf16[4,128,768]{2,1,0:T(8,128)(2,1)}, bf16[4,128,768]{2,1,0:T(8,128)(2,1)}) custom-call(bf16[4,2,384,1024]{3,2,1,0:T(8,128)(2,1)} %bitcast.199, bf16[4,2,128,3072]{3,2,1,0:T(8,128)(2,1)} %bitcast.200, bf16[4,2,128,3072]{3,2,1,0:T(8,128)(2,1)} %bitcast.201), custom_call_target="tpu_custom_call" | custom-call | tf_op jit(solution)/shard_map/reduce_grads/pallas_call | solution.py:434
  525.9 119.6 %reduce_grads.2 = (bf16[4,192,256]{2,1,0:T(8,128)(2,1)}, bf16[4,192,384]{2,1,0:T(8,128)(2,1)}, bf16[4,192,384]{2,1,0:T(8,128)(2,1)}, bf16[4,128,384]{2,1,0:T(8,1...) custom-call(bf16[4,2,192,1024]{3,2,1,0:T(8,128)(2,1)} %bitcast.204, bf16[4,2,192,1536]{3,2,1,0:T(8,128)(2,1)} %bitcast.202, ...), custom_call_target="tpu_custom_call" | custom-call | tf_op jit(solution)/shard_map/reduce_grads/pallas_call | solution.py:434
  (292 shorter events, 115.7 us)
Async XLA Ops:
  2.0 157.2 %copy-start.41 = (f32[3,128]{1,0:T(4,128)}, f32[3,128]{1,0:T(4,128)S(1)}, u32[]{:S(2)}) copy-start(f32[3,128]{1,0:T(4,128)S(1)} %fusion.72) | copy-start | bytes 4612
  2.0 152.3 %copy-start.62 = (f32[3,128]{1,0:T(4,128)}, f32[3,128]{1,0:T(4,128)S(1)}, u32[]{:S(2)}) copy-start(f32[3,128]{1,0:T(4,128)S(1)} %fusion.91) | copy-start | bytes 4612
  2.0 152.3 %copy-start.11 = (bf16[3,128,1024]{2,1,0:T(8,128)(2,1)S(1)}, bf16[3,128,1024]{2,1,0:T(8,128)(2,1)}, u32[]{:S(2)}) copy-start(bf16[3,128,1024]{2,1,0:T(8,128)(2,1)} %param.22) | copy-start | bytes 2359300
  2.1 152.3 %copy-start.56 = (f32[1024]{0:T(1024)S(1)}, f32[1024]{0:T(1024)}, u32[]{:S(2)}) copy-start(f32[1024]{0:T(1024)} %param.24) | copy-start | bytes 12292
  157.7 8.1 %copy-start.5 = (f32[3,128,1536]{2,1,0:T(8,128)}, f32[3,128,1536]{2,1,0:T(8,128)S(1)}, u32[]{:S(2)}) copy-start(f32[3,128,1536]{2,1,0:T(8,128)S(1)} %fusion.12) | copy-start | bytes 7077892
  157.7 8.0 %collective-permute-start = (f32[3,3,1536]{2,1,0:T(4,128)S(1)}, f32[3,3,1536]{2,1,0:T(4,128)S(1)}, u32[]{:S(2)}, u32[]{:S(2)}) collective-permute-start(f32[3,3,1536]{2,1,0:T(4,128)S(1)} %slice.126), channel_id=1, source_target_pairs={{0,1},{1,2},{2,3},{3,4},{4,5},{5,6},{6,7},{8,9},{9,10},{10,11},{11... | collective-permute-start | bytes 165896 | tf_op jit(solution)/shard_map/ppermute | solution.py:499
  159.8 6.0 copy-start.59
  165.6 8.0 %copy-start.49 = (f32[3,128]{1,0:T(4,128)}, f32[3,128]{1,0:T(4,128)S(1)}, u32[]{:S(2)}) copy-start(f32[3,128]{1,0:T(4,128)S(1)} %get-tuple-element.313) | copy-start | bytes 4612
  165.6 8.0 %copy-start.54 = (f32[3,128]{1,0:T(4,128)}, f32[3,128]{1,0:T(4,128)S(1)}, u32[]{:S(2)}) copy-start(f32[3,128]{1,0:T(4,128)S(1)} %get-tuple-element.314) | copy-start | bytes 4612
  165.8 7.9 %slice-start.8 = ((s8[4718592]{0:T(1024)(128)(4,1)}), s8[4194304]{0:T(1024)(128)(4,1)S(1)}, s32[]{:S(2)}) async-start(s8[4718592]{0:T(1024)(128)(4,1)} %bitcast.234), calls=%async_computation.8 | async-start | bytes 8388608
  230.5 34.4 %copy-start.2 = (f32[3,128,1536]{2,1,0:T(8,128)}, f32[3,128,1536]{2,1,0:T(8,128)S(1)}, u32[]{:S(2)}) copy-start(f32[3,128,1536]{2,1,0:T(8,128)S(1)} %get-tuple-element.281) | copy-start | bytes 7077892
  232.0 29.5 %copy-start.15 = (f32[384,1024]{1,0:T(8,128)}, f32[384,1024]{1,0:T(8,128)S(1)}, u32[]{:S(2)}) copy-start(f32[384,1024]{1,0:T(8,128)S(1)} %get-tuple-element.310) | copy-start | bytes 4718596
  232.0 6.4 slice-start.4
  232.2 6.2 copy-start.25
  234.2 8.6 %slice-start = ((s8[6291456]{0:T(1024)(128)(4,1)}), s8[4194304]{0:T(1024)(128)(4,1)S(1)}, s32[]{:S(2)}) async-start(s8[6291456]{0:T(1024)(128)(4,1)} %bitcast.226), calls=%async_computation | async-start | bytes 8388608
  307.6 6.9 %copy-start.1 = (f32[3,128,1536]{2,1,0:T(8,128)S(1)}, f32[3,128,1536]{2,1,0:T(8,128)}, u32[]{:S(2)}) copy-start(f32[3,128,1536]{2,1,0:T(8,128)} %copy-done) | copy-start | bytes 7077892
  307.6 6.9 %copy-start.3 = (f32[3,128,1536]{2,1,0:T(8,128)S(1)}, f32[3,128,1536]{2,1,0:T(8,128)}, u32[]{:S(2)}) copy-start(f32[3,128,1536]{2,1,0:T(8,128)} %copy-done.2) | copy-start | bytes 7077892
  307.6 6.9 %copy-start.4 = (f32[3,128,1536]{2,1,0:T(8,128)S(1)}, f32[3,128,1536]{2,1,0:T(8,128)}, u32[]{:S(2)}) copy-start(f32[3,128,1536]{2,1,0:T(8,128)} %get-tuple-element.308) | copy-start | bytes 7077892
  307.6 6.9 %copy-start.50 = (f32[3,128]{1,0:T(4,128)S(1)}, f32[3,128]{1,0:T(4,128)}, u32[]{:S(2)}) copy-start(f32[3,128]{1,0:T(4,128)} %copy-done.49) | copy-start | bytes 4612
  307.6 11.7 %slice-start.12 = ((s8[4718592]{0:T(1024)(128)(4,1)}), s8[4194304]{0:T(1024)(128)(4,1)S(1)}, s32[]{:S(2)}) async-start(s8[4718592]{0:T(1024)(128)(4,1)} %bitcast.238), calls=%async_computation.12 | async-start | bytes 8388608
  344.0 8.0 %slice-start.2 = ((s8[6291456]{0:T(1024)(128)(4,1)}), s8[2097152]{0:T(1024)(128)(4,1)S(1)}, s32[]{:S(2)}) async-start(s8[6291456]{0:T(1024)(128)(4,1)} %bitcast.228), calls=%async_computation.2 | async-start | bytes 4194304
  345.9 6.1 slice-start.3
  371.9 146.0 %collective-permute-start.1 = (f32[3,3,1536]{2,1,0:T(4,128)S(1)}, f32[3,3,1536]{2,1,0:T(4,128)S(1)}, u32[]{:S(2)}, u32[]{:S(2)}) collective-permute-start(f32[3,3,1536]{2,1,0:T(4,128)S(1)} %pad_add_fusion.1), channel_id=1, source_target_pairs={{1,0},{2,1},{3,2},{4,3},{5,4},{6,5},{7,6},{9,8},{10,9},{11,10},{12... | collective-permute-start | bytes 165896 | tf_op jit(solution)/shard_map/ppermute | solution.py:499
  525.9 121.7 %copy-start.42 = (f32[3,128]{1,0:T(4,128)S(1)}, f32[3,128]{1,0:T(4,128)}, u32[]{:S(2)}) copy-start(f32[3,128]{1,0:T(4,128)} %copy-done.41) | copy-start | bytes 4612
  (67 other events, 218.2 us)

commit v2 on v1

--- a/solution.py
+++ b/solution.py
@@ -32,140 +32,6 @@
     along_y = (lax.rem(r + 2, 4), s)
     along_z = [(r, lax.rem(z + k, 4) * 2 + c) for k in (1, 2, 3)]
     return mate, along_x, along_y, along_z
-
-
-def gather_kernel(count, *refs):
-    shards, fulls = refs[:count], refs[count : 2 * count]
-    send, recv, local = refs[2 * count :]
-    r, s, z, c = place()
-    mate, along_x, along_y, along_z = peers_of(r, s, z, c)
-    across_x, across_y = along_x[0], along_y[0]
-    greet([mate, along_x, along_y] + along_z)
-
-    def remote(m, slot, src, dst, device):
-        return pltpu.make_async_remote_copy(
-            src_ref=src,
-            dst_ref=dst,
-            send_sem=send.at[m, slot],
-            recv_sem=recv.at[m, slot],
-            device_id=device,
-            device_id_type=MESH,
-        )
-
-    def region(m, source, quarter, begin, length):
-        depth, width = shards[m].shape
-        part = width // 4
-        row = pl.multiple_of((source * 2 + c) * depth + begin, 16)
-        column = pl.multiple_of(quarter * part, 128)
-        return fulls[m].at[pl.ds(row, length), pl.ds(column, part)]
-
-    live = []
-
-    def start(copy):
-        copy.start()
-        live.append(copy)
-        return copy
-
-    stage_own, stage_z, stage_x, stage_y, stage_d, stage_c = {}, {}, {}, {}, {}, {}
-
-    def begin(m):
-        depth, width = shards[m].shape
-        part = width // 4
-        rows = pl.ds(pl.multiple_of(s * depth, 16), depth)
-        own = pltpu.make_async_copy(shards[m], fulls[m].at[rows], local.at[m])
-        own.start()
-        column = pl.multiple_of(r * part, 128)
-        stage_z[m] = [
-            start(
-                remote(
-                    m,
-                    k,
-                    shards[m].at[:, pl.ds(column, part)],
-                    region(m, z, r, 0, depth),
-                    along_z[k - 1],
-                )
-            )
-            for k in (1, 2, 3)
-        ]
-        stage_own[m] = (own, start(remote(m, 0, shards[m], fulls[m].at[rows], mate)))
-
-    def sources(k):
-        return lax.rem(z + 4 - k, 4)
-
-    begin(0)
-    begin(1)
-    for tick in range(count + 2):
-        m = tick
-        if m < count:
-            depth = shards[m].shape[0]
-            stage_x[m], stage_y[m] = [], []
-            for k in (1, 2, 3):
-                stage_z[m][k - 1].wait_recv()
-                piece = region(m, sources(k), r, 0, depth)
-                stage_x[m].append(start(remote(m, 3 + k, piece, piece, along_x)))
-                stage_y[m].append(start(remote(m, 6 + k, piece, piece, along_y)))
-        if tick + 2 < count:
-            begin(tick + 2)
-        m = tick - 1
-        if 0 <= m < count:
-            depth = shards[m].shape[0]
-            half = depth // 2
-            stage_d[m] = []
-            for k in (1, 2, 3):
-                stage_x[m][k - 1].wait_recv()
-                piece = region(m, sources(k), across_x, 0, half)
-                stage_d[m].append(start(remote(m, 9 + k, piece, piece, along_y)))
-                stage_y[m][k - 1].wait_recv()
-                piece = region(m, sources(k), across_y, half, half)
-                stage_d[m].append(start(remote(m, 12 + k, piece, piece, along_x)))
-        m = tick - 2
-        if 0 <= m < count:
-            depth = shards[m].shape[0]
-            stage_c[m] = []
-            for k in (1, 2, 3):
-                stage_d[m][2 * k - 2].wait_recv()
-                stage_d[m][2 * k - 1].wait_recv()
-                rows = pl.ds(pl.multiple_of((sources(k) * 2 + c) * depth, 16), depth)
-                piece = fulls[m].at[rows]
-                stage_c[m].append(start(remote(m, 15 + k, piece, piece, mate)))
-    for m in range(count):
-        own, twin = stage_own[m]
-        own.wait()
-        twin.wait_recv()
-        for copy in stage_c[m]:
-            copy.wait_recv()
-    for copy in live:
-        copy.wait_send()
-
-
-def gather_all(shards, axis_size):
-    if axis_size != 8 or lax.axis_size("rows") != 4:
-        return tuple(lax.all_gather(a, "seq", axis=0, tiled=True) for a in shards)
-    count = len(shards)
-    return pl.pallas_call(
-        functools.partial(gather_kernel, count),
-        out_shape=tuple(
-            jax.ShapeDtypeStruct((a.shape[0] * axis_size, a.shape[1]), a.dtype) for a in shards
-        ),
-        in_specs=[ANY] * count,
-        out_specs=(ANY,) * count,
-        scratch_shapes=[
-            pltpu.SemaphoreType.DMA((count, 19)),
-            pltpu.SemaphoreType.DMA((count, 19)),
-            pltpu.SemaphoreType.DMA((count,)),
-        ],
-        compiler_params=pltpu.CompilerParams(collective_id=0, has_side_effects=True),
-        name="gather_weights",
-    )(*shards)
-
-
-def blocks_add(total, term, lead, rows):
-    def one(i, carry):
-        total_at = total(i)
-        total_at[...] = total_at[...] + term(i)[...]
-        return carry
-
-    lax.fori_loop(0, lead, one, 0)
 
 
 def reduce_kernel(count, has_small, *refs):
@@ -492,6 +358,439 @@
         name="scan_back" if reverse else "scan_ahead",
     )(a, b)
 
+def gelu_parts(v):
+    inner = 0.7978845608028654 * (v + 0.044715 * v * v * v)
+    t = jnp.tanh(inner)
+    slope = 0.7978845608028654 * (1.0 + 0.134145 * v * v)
+    return 0.5 * v * (1.0 + t), 0.5 * (1.0 + t) + 0.5 * v * (1.0 - t * t) * slope
+
+
+def gelu_of(v):
+    return 0.5 * v * (1.0 + jnp.tanh(0.7978845608028654 * (v + 0.044715 * v * v * v)))
+
+
+def minus_expm1(v, power):
+    total = 1.0 / 40320.0
+    for term in (5040.0, 720.0, 120.0, 24.0, 6.0, 2.0, 1.0):
+        total = total * v + 1.0 / term
+    return jnp.where(v > -0.5, -v * total, 1.0 - power)
+
+
+def tile_scan(a, b, reverse):
+    spot = lax.broadcasted_iota(jnp.int32, a.shape, 0)
+    for distance in (1, 2, 4):
+        if reverse:
+            inside = spot < 8 - distance
+            back_a, back_b = pltpu.roll(a, 8 - distance, 0), pltpu.roll(b, 8 - distance, 0)
+        else:
+            inside = spot >= distance
+            back_a, back_b = pltpu.roll(a, distance, 0), pltpu.roll(b, distance, 0)
+        b = b + a * jnp.where(inside, back_b, 0.0)
+        a = a * jnp.where(inside, back_a, 1.0)
+    return a, b
+
+
+def loop(count, body):
+    def one(i, carry):
+        body(i)
+        return carry
+
+    lax.fori_loop(0, count, one, 0)
+
+
+def at(i, size):
+    return pl.ds(pl.multiple_of(i * size, size), size)
+
+
+def forward_kernel(*refs):
+    refs = list(refs)
+
+    def take(n):
+        taken, refs[:n] = refs[:n], []
+        return taken
+
+    shards = take(8)
+    tokens, marks, gain1, conv_w, conv_b, rate_b, input_b, decay_scale, gain2 = take(9)
+    fulls = take(8)
+    outs = take(12)
+    (w_rec, w_rate, w_input, w_branch, w_out) = weights = take(5)
+    normed, padded, conv_out, conv_low, rate_pre, input_pre = take(6)
+    products, states, branch_pre, mixed_in, resid, normed2 = take(6)
+    rim, ends, got, carry_in = take(4)
+    send, recv, local, near_send, near_recv, load_sem, save_sem = refs
+    count = 8
+    r, s, z, c = place()
+    mate, along_x, along_y, along_z = peers_of(r, s, z, c)
+    across_x, across_y = along_x[0], along_y[0]
+    others = [(r, lax.rem(s + k, 8)) for k in range(1, 8)]
+    greet(others + [along_x, along_y])
+    live, pending = [], []
+
+    def start(copy):
+        copy.start()
+        live.append(copy)
+        return copy
+
+    def remote(m, slot, src, dst, device):
+        return start(
+            pltpu.make_async_remote_copy(
+                src_ref=src,
+                dst_ref=dst,
+                send_sem=send.at[m, slot],
+                recv_sem=recv.at[m, slot],
+                device_id=device,
+                device_id_type=MESH,
+            )
+        )
+
+    def near(slot, src, dst, device):
+        return start(
+            pltpu.make_async_remote_copy(
+                src_ref=src,
+                dst_ref=dst,
+                send_sem=near_send.at[slot],
+                recv_sem=near_recv.at[slot],
+                device_id=device,
+                device_id_type=MESH,
+            )
+        )
+
+    def save(slot, src, dst):
+        copy = pltpu.make_async_copy(src, dst, save_sem.at[slot])
+        copy.start()
+        pending.append(copy)
+
+    def region(m, source, quarter, begin, length):
+        depth, width = shards[m].shape
+        part = width // 4
+        row = pl.multiple_of((source * 2 + c) * depth + begin, 16)
+        column = pl.multiple_of(quarter * part, 128)
+        return fulls[m].at[pl.ds(row, length), pl.ds(column, part)]
+
+    stage_own, stage_z, stage_x, stage_y, stage_d, stage_c = {}, {}, {}, {}, {}, {}
+
+    def begin(m):
+        depth, width = shards[m].shape
+        part = width // 4
+        rows = pl.ds(pl.multiple_of(s * depth, 16), depth)
+        own = pltpu.make_async_copy(shards[m], fulls[m].at[rows], local.at[m])
+        own.start()
+        column = pl.multiple_of(r * part, 128)
+        stage_z[m] = [
+            remote(
+                m,
+                k,
+                shards[m].at[:, pl.ds(column, part)],
+                region(m, z, r, 0, depth),
+                along_z[k - 1],
+            )
+            for k in (1, 2, 3)
+        ]
+        stage_own[m] = (own, remote(m, 0, shards[m], fulls[m].at[rows], mate))
+
+    def sources(k):
+        return lax.rem(z + 4 - k, 4)
+
+    def tick(now):
+        m = now
+        if m < count:
+            depth = shards[m].shape[0]
+            stage_x[m], stage_y[m] = [], []
+            for k in (1, 2, 3):
+                stage_z[m][k - 1].wait_recv()
+                piece = region(m, sources(k), r, 0, depth)
+                stage_x[m].append(remote(m, 3 + k, piece, piece, along_x))
+                stage_y[m].append(remote(m, 6 + k, piece, piece, along_y))
+        if now + 2 < count:
+            begin(now + 2)
+        m = now - 1
+        if 0 <= m < count:
+            depth = shards[m].shape[0]
+            half = depth // 2
+            stage_d[m] = []
+            for k in (1, 2, 3):
+                stage_x[m][k - 1].wait_recv()
+                piece = region(m, sources(k), across_x, 0, half)
+                stage_d[m].append(remote(m, 9 + k, piece, piece, along_y))
+                stage_y[m][k - 1].wait_recv()
+                piece = region(m, sources(k), across_y, half, half)
+                stage_d[m].append(remote(m, 12 + k, piece, piece, along_x))
+        m = now - 2
+        if 0 <= m < count:
+            depth = shards[m].shape[0]
+            stage_c[m] = []
+            for k in (1, 2, 3):
+                stage_d[m][2 * k - 2].wait_recv()
+                stage_d[m][2 * k - 1].wait_recv()
+                rows = pl.ds(pl.multiple_of((sources(k) * 2 + c) * depth, 16), depth)
+                piece = fulls[m].at[rows]
+                stage_c[m].append(remote(m, 15 + k, piece, piece, mate))
+
+    loads = {}
+
+    def arrive(m):
+        own, twin = stage_own[m]
+        own.wait()
+        twin.wait_recv()
+        for copy in stage_c[m]:
+            copy.wait_recv()
+        if m < 5:
+            loads[m] = pltpu.make_async_copy(fulls[m], weights[m], load_sem.at[m])
+            loads[m].start()
+
+    def product(left, right, store):
+        width = right.shape[1]
+
+        def one(j):
+            columns = at(j, 512)
+            store(
+                columns,
+                jnp.dot(left[...], right[:, columns], preferred_element_type=jnp.float32),
+            )
+
+        loop(width // 512, one)
+
+    def first_norm():
+        def one(i):
+            rows = at(i, 32)
+            values = tokens[rows, :].astype(jnp.float32)
+            scale = lax.rsqrt(jnp.mean(values * values, axis=-1, keepdims=True) + epsilon)
+            normed[rows, :] = (values * scale * gain1[...]).astype(jnp.bfloat16)
+
+        loop(12, one)
+        save(0, normed, outs[0])
+
+    def rec_product():
+        loads[0].wait()
+
+        def store(columns, values):
+            for row in range(3):
+                padded[row, 8:136, columns] = values[row * 128 : (row + 1) * 128]
+
+        product(normed, w_rec, store)
+        return near(0, padded.at[:, pl.ds(128, 8), :], rim, others[0])
+
+    def convolution(copy):
+        copy.wait_recv()
+        for row in range(3):
+            padded[row, 0:8, :] = jnp.where(s > 0, rim[row], 0.0)
+        save(1, padded, outs[1])
+
+        def one(i):
+            row, rest = lax.div(i, 12), lax.rem(i, 12)
+            block, column = lax.div(rest, 3), lax.rem(rest, 3)
+            columns = at(column, 512)
+            window = padded[row, pl.ds(pl.multiple_of(block * 32, 8), 40), columns]
+            rows = pl.ds(pl.multiple_of(row * 128 + block * 32, 32), 32)
+            total = conv_b[:, columns] + conv_w[0:1, columns] * window[8:]
+            for k in (1, 2, 3):
+                shifted = pltpu.roll(window, k, 0)[8:]
+                total = total + conv_w[k : k + 1, columns] * (marks[rows, k : k + 1] * shifted)
+            conv_out[rows, columns] = total
+            conv_low[rows, columns] = total.astype(jnp.bfloat16)
+
+        loop(36, one)
+        save(2, conv_out, outs[2])
+        save(3, conv_low, outs[3])
+
+    def gate_product(which):
+        target, weight = ((rate_pre, w_rate), (input_pre, w_input))[which]
+        loads[1 + which].wait()
+
+        def store(columns, values):
+            target[:, columns] = values
+
+        product(conv_low, weight, store)
+        save(4 + which, target, outs[4 + which])
+
+    def branch_product():
+        loads[3].wait()
+
+        def store(columns, values):
+            branch_pre[:, columns] = values
+
+        product(normed, w_branch, store)
+        save(7, branch_pre, outs[7])
+
+    def local_scan():
+        def one(column):
+            columns = at(column, 512)
+
+            def tile(t, carry):
+                results = []
+                for row in range(3):
+                    rows = pl.ds(pl.multiple_of(row * 128 + t * 8, 8), 8)
+                    reset = marks[rows, 0:1]
+                    rate_gate = jax.nn.sigmoid(rate_pre[rows, columns] + rate_b[:, columns])
+                    input_gate = jax.nn.sigmoid(input_pre[rows, columns] + input_b[:, columns])
+                    log_rate = decay_scale[:, columns] * rate_gate
+                    keep = 1.0 - reset
+                    pace = jnp.exp(log_rate)
+                    left = minus_expm1(2.0 * log_rate, pace * pace)
+                    scale = reset + keep * jnp.sqrt(left)
+                    a, b = tile_scan(
+                        pace * keep, scale * input_gate * conv_out[rows, columns], False
+                    )
+                    b = b + a * carry[2 * row + 1]
+                    a = a * carry[2 * row]
+                    products[rows, columns] = a
+                    states[rows, columns] = b
+                    results += [a[7:8], b[7:8]]
+                return tuple(results)
+
+            ones, zeros = jnp.ones((1, 512), jnp.float32), jnp.zeros((1, 512), jnp.float32)
+            last = lax.fori_loop(0, 16, tile, (ones, zeros) * 3)
+            for row in range(3):
+                ends[row : row + 1, columns] = last[2 * row]
+                ends[3 + row : 4 + row, columns] = last[2 * row + 1]
+
+        loop(3, one)
+        return [near(k, ends, got.at[k], others[k - 1]) for k in range(1, 8)]
+
+    def carry_states(copies):
+        for copy in copies:
+            copy.wait_recv()
+
+        def one(column):
+            columns = at(column, 512)
+            state = jnp.zeros((3, 512), jnp.float32)
+            for k in range(7, 0, -1):
+                after = got[k, 3:6, columns] + got[k, 0:3, columns] * state
+                state = jnp.where(k <= s, after, state)
+            carry_in[0:3, columns] = state
+
+        loop(3, one)
+        save(10, carry_in, outs[10])
+
+    def mix():
+        def one(i):
+            row, rest = lax.div(i, 12), lax.rem(i, 12)
+            block, column = lax.div(rest, 3), lax.rem(rest, 3)
+            columns = at(column, 512)
+            rows = pl.ds(pl.multiple_of(row * 128 + block * 32, 32), 32)
+            carried = carry_in[pl.ds(row, 1), columns]
+            state = states[rows, columns] + products[rows, columns] * carried
+            states[rows, columns] = state
+            mixed_in[rows, columns] = (state * gelu_of(branch_pre[rows, columns])).astype(
+                jnp.bfloat16
+            )
+
+        loop(36, one)
+        save(6, states, outs[6])
+        save(8, mixed_in, outs[8])
+
+    def out_product():
+        loads[4].wait()
+
+        def store(columns, values):
+            resid[:, columns] = tokens[:, columns].astype(jnp.float32) + values
+
+        product(mixed_in, w_out, store)
+        save(9, resid, outs[9])
+
+        def one(i):
+            rows = at(i, 32)
+            values = resid[rows, :]
+            scale = lax.rsqrt(jnp.mean(values * values, axis=-1, keepdims=True) + epsilon)
+            normed2[rows, :] = (values * scale * gain2[...]).astype(jnp.bfloat16)
+
+        loop(12, one)
+        save(11, normed2, outs[11])
+
+    carry_in[...] = jnp.zeros_like(carry_in)
+    ends[...] = jnp.zeros_like(ends)
+    begin(0)
+    begin(1)
+    first_norm()
+    tick(0)
+    tick(1)
+    tick(2)
+    arrive(0)
+    rim_copy = rec_product()
+    tick(3)
+    arrive(1)
+    convolution(rim_copy)
+    gate_product(0)
+    tick(4)
+    arrive(2)
+    gate_product(1)
+    tick(5)
+    ends_copies = local_scan()
+    arrive(3)
+    branch_product()
+    tick(6)
+    carry_states(ends_copies)
+    mix()
+    arrive(4)
+    tick(7)
+    out_product()
+    tick(8)
+    tick(9)
+    for m in (5, 6, 7):
+        arrive(m)
+    for copy in live:
+        copy.wait_send()
+    for copy in pending:
+        copy.wait()
+
+
+def forward_all(shards, tokens, marks, vectors):
+    low, full = jnp.bfloat16, jnp.float32
+    tok, model = tokens.shape
+    rec = shards[0].shape[1]
+    shape = jax.ShapeDtypeStruct
+    saved = (
+        shape((tok, model), low),
+        shape((3, 136, rec), full),
+        shape((tok, rec), full),
+        shape((tok, rec), low),
+        shape((tok, rec), full),
+        shape((tok, rec), full),
+        shape((tok, rec), full),
+        shape((tok, rec), full),
+        shape((tok, rec), low),
+        shape((tok, model), full),
+        shape((8, rec), full),
+        shape((tok, model), low),
+    )
+    fulls = tuple(shape((a.shape[0] * 8, a.shape[1]), low) for a in shards)
+    results = pl.pallas_call(
+        forward_kernel,
+        out_shape=fulls + saved,
+        in_specs=[ANY] * 8 + [VMEM] * 9,
+        out_specs=(ANY,) * 20,
+        scratch_shapes=[pltpu.VMEM(a.shape, low) for a in fulls[:5]]
+        + [
+            pltpu.VMEM((tok, model), low),
+            pltpu.VMEM((3, 136, rec), full),
+            pltpu.VMEM((tok, rec), full),
+            pltpu.VMEM((tok, rec), low),
+            pltpu.VMEM((tok, rec), full),
+            pltpu.VMEM((tok, rec), full),
+            pltpu.VMEM((tok, rec), full),
+            pltpu.VMEM((tok, rec), full),
+            pltpu.VMEM((tok, rec), full),
+            pltpu.VMEM((tok, rec), low),
+            pltpu.VMEM((tok, model), full),
+            pltpu.VMEM((tok, model), low),
+            pltpu.VMEM((3, 8, rec), full),
+            pltpu.VMEM((8, rec), full),
+            pltpu.VMEM((8, 8, rec), full),
+            pltpu.VMEM((8, rec), full),
+            pltpu.SemaphoreType.DMA((8, 19)),
+            pltpu.SemaphoreType.DMA((8, 19)),
+            pltpu.SemaphoreType.DMA((8,)),
+            pltpu.SemaphoreType.DMA((8,)),
+            pltpu.SemaphoreType.DMA((8,)),
+            pltpu.SemaphoreType.DMA((5,)),
+            pltpu.SemaphoreType.DMA((12,)),
+        ],
+        compiler_params=pltpu.CompilerParams(
+            collective_id=0, has_side_effects=True, vmem_limit_bytes=60 * 1024 * 1024
+        ),
+        name="recurrent_forward",
+    )(*shards, tokens, marks, *vectors)
+    return results[:8], results[8:]
 
 def from_behind(block, axis, distance):
     devices = range(lax.axis_size(axis))
@@ -564,7 +863,7 @@
     )
 
 
-def body(
+def plain_body(
     tokens,
     bounds,
     norm1_gain,
@@ -584,10 +883,17 @@
     w_down,
     cotangent,
 ):
-    axis_size = lax.axis_size("seq")
-    full_rec, full_rate, full_input, full_branch, full_out, full_gate, full_up, full_down = gather_all(
-        (w_rec, w_rate, w_input, w_branch, w_out, w_gate, w_up, w_down), axis_size
-    )
+    gathered = (
+        lax.all_gather(w_branch, "seq", axis=0, tiled=True),
+        lax.all_gather(w_rec, "seq", axis=0, tiled=True),
+        lax.all_gather(w_rate, "seq", axis=0, tiled=True),
+        lax.all_gather(w_input, "seq", axis=0, tiled=True),
+        lax.all_gather(w_out, "seq", axis=0, tiled=True),
+        lax.all_gather(w_gate, "seq", axis=0, tiled=True),
+        lax.all_gather(w_up, "seq", axis=0, tiled=True),
+        lax.all_gather(w_down, "seq", axis=0, tiled=True),
+    )
+    full_branch, full_rec, full_rate, full_input, full_out, full_gate, full_up, full_down = gathered
     row_count, tok_count, model_width = tokens.shape
     rec_width = full_rec.shape[1]
     offset = lax.axis_index("seq") * tok_count
@@ -615,7 +921,7 @@
         )
 
     decays, drives = gates_of(rate_pre, input_pre, conv_out, decay_param, rate_bias, input_bias)
-    prefix_decay, local_states = scan(decays, drives, False)
+    prefix_decay, local_states = lax.associative_scan(combine, (decays, drives), axis=1)
     ones_pair = jnp.ones((row_count, rec_width), jnp.float32)
     zeros_pair = jnp.zeros((row_count, rec_width), jnp.float32)
     carry_in = prefix(
@@ -653,7 +959,9 @@
     _, pull_branch = jax.vjp(lambda pre_arg: jax.nn.gelu(pre_arg, approximate=True), branch_pre)
     branch_low = pull_branch((grad_mixed * states).reshape(-1, rec_width))[0].astype(jnp.bfloat16)
     next_decays = jnp.concatenate([decays[:, 1:, :], ones_pair[:, None, :]], axis=1)
-    suffix_decay, local_grads = scan(next_decays, grad_states, True)
+    suffix_decay, local_grads = lax.associative_scan(
+        combine, (next_decays, grad_states), axis=1, reverse=True
+    )
     element = (prefix_decay[:, -1], decays[:, 0] * local_grads[:, 0])
     carry_back = prefix(element, "seq", combine, (ones_pair, zeros_pair), True)[1]
     state_grads = local_grads + suffix_decay * carry_back[:, None, :]
@@ -688,7 +996,199 @@
     _, pull_norm1 = jax.vjp(rms_norm, inputs, norm1_gain)
     grad_inputs, grad_norm1 = pull_norm1(grad_normed)
     token_grad = (grad_resid + grad_inputs).astype(jnp.bfloat16).reshape(tokens.shape)
+    grad_mats = (
+        grad_branch_w,
+        grad_rec_w,
+        grad_rate,
+        grad_input,
+        grad_out,
+        grad_gate,
+        grad_up,
+        grad_down,
+    )
+    blocks = (
+        lax.psum_scatter(grad_mats[0], "seq", scatter_dimension=0, tiled=True),
+        lax.psum_scatter(grad_mats[1], "seq", scatter_dimension=0, tiled=True),
+        lax.psum_scatter(grad_mats[2], "seq", scatter_dimension=0, tiled=True),
+        lax.psum_scatter(grad_mats[3], "seq", scatter_dimension=0, tiled=True),
+        lax.psum_scatter(grad_mats[4], "seq", scatter_dimension=0, tiled=True),
+        lax.psum_scatter(grad_mats[5], "seq", scatter_dimension=0, tiled=True),
+        lax.psum_scatter(grad_mats[6], "seq", scatter_dimension=0, tiled=True),
+        lax.psum_scatter(grad_mats[7], "seq", scatter_dimension=0, tiled=True),
+    )
+    summed = lax.psum(
+        (blocks[0], blocks[1], blocks[2], blocks[3], blocks[4], blocks[5], blocks[6], blocks[7]),
+        "rows",
+    )
+    small = lax.psum(
+        (
+            grad_norm1,
+            grad_conv_weight,
+            grad_conv_bias,
+            grad_rate_bias,
+            grad_input_bias,
+            grad_decay,
+            grad_norm2,
+        ),
+        ("rows", "seq"),
+    )
+    return (
+        mixed,
+        token_grad,
+        small[0],
+        summed[0],
+        summed[1],
+        small[1],
+        small[2],
+        summed[2],
+        small[3],
+        summed[3],
+        small[4],
+        small[5],
+        summed[4],
+        small[6],
+        summed[5],
+        summed[6],
+        summed[7],
+    )
+
+
+def body(*args):
+    if lax.axis_size("rows") == 4 and lax.axis_size("seq") == 8:
+        return staged_body(*args)
+    return plain_body(*args)
+
+
+def staged_body(
+    tokens,
+    bounds,
+    norm1_gain,
+    w_branch,
+    w_rec,
+    conv_weight,
+    conv_bias,
+    w_rate,
+    rate_bias,
+    w_input,
+    input_bias,
+    decay_param,
+    w_out,
+    norm2_gain,
+    w_gate,
+    w_up,
+    w_down,
+    cotangent,
+):
+    row_count, tok_count, model_width = tokens.shape
+    rec_width = w_rec.shape[1]
+    offset = lax.axis_index("seq") * tok_count
+    positions = offset - 3 + jnp.arange(tok_count + 3, dtype=jnp.int32)
+    marked = (
+        jnp.any(positions[None, :, None] == bounds[:, None, :], axis=2) | (positions == 0)[None, :]
+    )
+    padded_resets = marked.astype(jnp.float32)
+    resets = padded_resets[:, 3:]
+    masks = conv_masks(padded_resets)
+    marks = jnp.stack((resets,) + masks + (resets,) * 4, axis=2).reshape(-1, 8)
+    flat_tokens = tokens.reshape(-1, model_width)
+    decay_scale = (-8.0 * jax.nn.softplus(decay_param))[None]
+    fulls, saved = forward_all(
+        (w_rec, w_rate, w_input, w_branch, w_out, w_gate, w_up, w_down),
+        flat_tokens,
+        marks,
+        (
+            norm1_gain[None],
+            conv_weight,
+            conv_bias[None],
+            rate_bias[None],
+            input_bias[None],
+            decay_scale,
+            norm2_gain[None],
+        ),
+    )
+    full_rec, full_rate, full_input, full_branch, full_out, full_gate, full_up, full_down = fulls
+    normed, padded_all, conv_out, conv_low, rate_pre, input_pre = saved[:6]
+    states, branch_pre, mixed_in, resid, carried, normed2 = saved[6:]
+    shape = (row_count, tok_count, rec_width)
+    conv_out, rate_pre, input_pre = (a.reshape(shape) for a in (conv_out, rate_pre, input_pre))
+    states = states.reshape(shape)
+    carry_in = carried[:3]
+    padded = padded_all[:, 5:, :]
+    inputs = flat_tokens.astype(jnp.float32)
+
+    def gates_of(rate_arg, input_arg, conv_arg, decay_arg, rate_arg_bias, input_arg_bias):
+        return gate_terms(
+            rate_arg, input_arg, conv_arg, decay_arg, rate_arg_bias, input_arg_bias, resets
+        )
+
+    decays, drives = gates_of(rate_pre, input_pre, conv_out, decay_param, rate_bias, input_bias)
+    ones_pair = jnp.ones((row_count, rec_width), jnp.float32)
+    zeros_pair = jnp.zeros((row_count, rec_width), jnp.float32)
+    earlier_states = jnp.concatenate([carry_in[:, None, :], states[:, :-1, :]], axis=1)
+    branch_act = jax.nn.gelu(branch_pre, approximate=True).reshape(states.shape)
+    gate_pre = forward_product(normed2, full_gate)
+    up_pre = forward_product(normed2, full_up)
+    hidden = (jax.nn.gelu(gate_pre, approximate=True) * up_pre).astype(jnp.bfloat16)
+    mixed = (resid + forward_product(hidden, full_down)).astype(jnp.bfloat16).reshape(tokens.shape)
+    cot_low = cotangent.reshape(-1, model_width)
+    grad_down = outer(hidden, cot_low)
+    grad_hidden = back_product(cot_low, full_down)
+    _, pull_mlp = jax.vjp(
+        lambda gate_arg, up_arg: jax.nn.gelu(gate_arg, approximate=True) * up_arg, gate_pre, up_pre
+    )
+    grad_gate_pre, grad_up_pre = pull_mlp(grad_hidden)
+    gate_low = grad_gate_pre.astype(jnp.bfloat16)
+    up_low = grad_up_pre.astype(jnp.bfloat16)
+    grad_gate = outer(normed2, gate_low)
+    grad_up = outer(normed2, up_low)
+    grad_normed2 = back_product(gate_low, full_gate) + back_product(up_low, full_up)
+    _, pull_norm2 = jax.vjp(rms_norm, resid, norm2_gain)
+    grad_resid_norm, grad_norm2 = pull_norm2(grad_normed2)
+    grad_resid = cot_low.astype(jnp.float32) + grad_resid_norm
+    resid_low = grad_resid.astype(jnp.bfloat16)
+    grad_out = outer(mixed_in, resid_low)
+    grad_mixed = back_product(resid_low, full_out).reshape(states.shape)
+    grad_states = grad_mixed * branch_act
+    _, pull_branch = jax.vjp(lambda pre_arg: jax.nn.gelu(pre_arg, approximate=True), branch_pre)
+    branch_low = pull_branch((grad_mixed * states).reshape(-1, rec_width))[0].astype(jnp.bfloat16)
+    next_decays = jnp.concatenate([decays[:, 1:, :], ones_pair[:, None, :]], axis=1)
+    suffix_decay, local_grads = scan(next_decays, grad_states, True)
+    element = (decays[:, 0] * suffix_decay[:, 0], decays[:, 0] * local_grads[:, 0])
+    carry_back = prefix(element, "seq", combine, (ones_pair, zeros_pair), True)[1]
+    state_grads = local_grads + suffix_decay * carry_back[:, None, :]
+    _, pull_gates = jax.vjp(
+        gates_of, rate_pre, input_pre, conv_out, decay_param, rate_bias, input_bias
+    )
+    grad_rate_pre, grad_input_pre, grad_conv_direct, grad_decay, grad_rate_bias, grad_input_bias = (
+        pull_gates((state_grads * earlier_states, state_grads))
+    )
+    rate_low = grad_rate_pre.astype(jnp.bfloat16).reshape(-1, rec_width)
+    input_low = grad_input_pre.astype(jnp.bfloat16).reshape(-1, rec_width)
+    grad_rate = outer(conv_low, rate_low)
+    grad_input = outer(conv_low, input_low)
+    grad_conv = grad_conv_direct + (
+        back_product(rate_low, full_rate) + back_product(input_low, full_input)
+    ).reshape(conv_out.shape)
+    _, pull_conv = jax.vjp(
+        lambda pad_arg, weight_arg, bias_arg: convolve(pad_arg, masks, weight_arg, bias_arg),
+        padded,
+        conv_weight,
+        conv_bias,
+    )
+    grad_padded, grad_conv_weight, grad_conv_bias = pull_conv(grad_conv)
+    rim_back = from_behind(grad_padded[:, :3, :], "seq", -1)
+    grad_rec = grad_padded[:, 3:, :] + jnp.concatenate(
+        [jnp.zeros((row_count, tok_count - 3, rec_width), jnp.float32), rim_back], axis=1
+    )
+    rec_low = grad_rec.astype(jnp.bfloat16).reshape(-1, rec_width)
+    grad_rec_w = outer(normed, rec_low)
+    grad_branch_w = outer(normed, branch_low)
+    grad_normed = back_product(branch_low, full_branch) + back_product(rec_low, full_rec)
+    _, pull_norm1 = jax.vjp(rms_norm, inputs, norm1_gain)
+    grad_inputs, grad_norm1 = pull_norm1(grad_normed)
+    token_grad = (grad_resid + grad_inputs).astype(jnp.bfloat16).reshape(tokens.shape)
     low = jnp.bfloat16
+    axis_size = 8
     ff, _ = reduce_all(
         [g.astype(low) for g in (grad_down, grad_gate, grad_up)], None, axis_size, 1
     )
@@ -789,4 +1289,5 @@
         P("seq", None),
         P("seq", None),
     )
-    return jax.shard_map(body, mesh=mesh, in_specs=in_specs, out_specs=out_specs, check_vma=False)
+    return jax.shard_map(
+        body, mesh=mesh, in_specs=in_specs, out_specs=out_specs, check_vma=False)

time: 670 us -> 600 us (0.90)
  matrix products: 99.8 us -> 79.1 us
  blocking collectives: 48.8 us -> 28.1 us
  other arithmetic: 49.3 us -> 32.7 us
  Pallas kernels: 411 us -> 404 us
    dot_general x8 -> x3, matrix products: 34.4 us -> 12.8 us  [forward_product(): return jnp.dot(values, weight, preferred_element_type=jnp.float32)]
    all_gather x3 -> x2, blocking collectives: 48.8 us -> 28.1 us  [prefix(): gathered = jax.tree.map(lambda a: lax.all_gather(a, axis), part)]
    pallas_call x2 -> x1, Pallas kernels: 17.5 us -> 8.78 us  [scan(): pl.pallas_call(functools.partial(scan_kernel, reverse), grid=(count, widt...]
    convert_element_type x9 -> x4, other arithmetic: 10.2 us -> 2.39 us  [the longest x1 1.35 us: staged_body(): (grad_resid + grad_inputs).astype(jnp.bfloat16).reshape(tokens.shape)]
    unnamed x189 -> x127, local copies, waits for them, and re-layouts: 18.9 us -> 16.7 us
  transfers between devices with their start and end apart: 2 -> 1, of which waited for: 0 -> 0; matrix products, arithmetic and copies ran while one was open for 4% -> 11% of each run, Pallas kernels for 18% -> 21%
where the time goes in v2:
time: 600 us; the launch traced here: 592 us
  Pallas kernels  404 us (67%)
  matrix products  79.1 us (13%)
  local copies, waits for them, and re-layouts  43.5 us (7%)
  other arithmetic  32.7 us (5%)
  blocking collectives  28.1 us (5%)
    pallas_call x2, Pallas kernels, reduce_all(): pl.pallas_call(functools.partial(reduce_kernel, count, small is not None)...  242 us
    pallas_call x1, Pallas kernels, forward_all(): pl.pallas_call(forward_kernel, out_shape=fulls + saved, in_specs=[ANY] *...  154 us
    dot_general x8, matrix products, outer(): lax.dot_general(left, right, (((0,), (0,)), ((), ())), preferred_element_...  35.9 us
    dot_general x8, matrix products, back_product(): lax.dot_general(grads, weight, (((1,), (1,)), ((), ())), preferred_elemen...  30.4 us
    all_gather x2, blocking collectives, prefix(): gathered = jax.tree.map(lambda a: lax.all_gather(a, axis), part)  28.1 us
    unnamed x127, local copies, waits for them, and re-layouts  16.7 us
    convert_element_type x8, local copies, waits for them, and re-layouts, reduce_all(): b.transpose(1, 0, 2).reshape(k, 4 * n).astype(jnp.float32)  12.9 us
    dot_general x3, matrix products, forward_product(): return jnp.dot(values, weight, preferred_element_type=jnp.float32)  12.8 us
  transfers between devices with their start and end apart: 1, of which 0 were waited for; matrix products, arithmetic and copies ran while one was open for 11% of the time, Pallas kernels for 21%

profile of v2, /device:TPU:0, one launch (start us, length us, event | category | flops | bytes accessed | tf_op | source)
XLA Modules:
  0.0 591.6 jit_solution(7198402651764062525)
XLA Ops:
  8.7 153.9 %recurrent_forward.1 = (bf16[1024,1536]{1,0:T(8,128)(2,1)}, bf16[1536,1536]{1,0:T(8,128)(2,1)}, bf16[1536,1536]{1,0:T(8,128)(2,1)}, bf16[1024,1536]{1,0:T(8,128)...) custom-call(bf16[128,1536]{1,0:T(8,128)(2,1)} %refs_0_.1, ...), custom_call_target="tpu_custom_call" | custom-call | tf_op jit(solution)/shard_map/recurrent_forward/pallas_call | solution.py:757
  162.6 5.0 fusion.44
  167.7 4.2 fusion.45
  172.1 9.9 %fusion.7 = (bf16[384,3072]{1,0:T(8,128)(2,1)}, bf16[384,3072]{1,0:T(8,128)(2,1)S(1)}, bf16[384,3072]{1,0:T(8,128)(2,1)}) fusion(f32[384,3072]{1,0:T(8,128)S(1)} %fusion.44, f32[384,3072]{1,0:T(8,128)} %fusion.45, bf16[3072,1024]{1,0:T(8,128)(2,1)S(1)} %bitcast.189, bf16[384,1024]{1,0:T(8,128)(2,1)S(1)} %bitcast.178), kind=kOutput, calls=%fused_computation.18 | convolution fusion | flops 2446589952 | bytes 23592960 | tf_op jit(solution)/shard_map/dot_general | solution.py:861
  184.8 4.1 multiply_reduce_fusion.5
  199.6 4.2 multiply_multiply_fusion.7
  203.8 8.8 %scan_back.1 = (f32[3,128,1536]{2,1,0:T(8,128)}, f32[3,128,1536]{2,1,0:T(8,128)}) custom-call(f32[3,128,1536]{2,1,0:T(8,128)} %concatenate.13.a_ref, f32[3,128,1536]{2,1,0:T(8,128)} %bitcast.166), custom_call_target="tpu_custom_call" | custom-call | tf_op jit(solution)/shard_map/scan_back/pallas_call | solution.py:352
  213.7 14.1 %all-gather = f32[24,1,1536]{2,1,0:T(1,128)S(1)} all-gather(f32[3,1,1536]{2,1,0:T(1,128)S(1)} %get-tuple-element.257), channel_id=2, replica_groups=mesh['rows'=4,'seq'=8] {'seq'}, dimensions={0}, use_global_device_ids=true | all-gather | bytes 165888 | tf_op jit(solution)/shard_map/all_gather | solution.py:805
  228.2 14.0 %all-gather.1 = f32[24,1,1536]{2,1,0:T(1,128)S(1)} all-gather(f32[3,1,1536]{2,1,0:T(1,128)S(1)} %get-tuple-element.256), channel_id=3, replica_groups=mesh['rows'=4,'seq'=8] {'seq'}, dimensions={0}, use_global_device_ids=true | all-gather | bytes 165888 | tf_op jit(solution)/shard_map/all_gather | solution.py:805
  243.1 5.8 fusion.38
  249.0 4.2 multiply_reduce_fusion
  258.2 4.4 multiply_reduce_fusion.4
  266.4 4.5 convolution_convert_fusion.1
  270.9 4.4 convolution_convert_fusion
  275.3 3.5 add_convert_fusion
  278.8 5.4 convolution_convert_fusion.4
  284.2 5.4 convolution_convert_fusion.3
  289.6 5.8 convolution_convert_fusion.2
  295.4 3.5 convolution_convert_fusion.7
  301.6 3.5 convolution_convert_fusion.6
  305.1 124.4 %reduce_grads.3 = (bf16[4,384,256]{2,1,0:T(8,128)(2,1)}, bf16[4,128,768]{2,1,0:T(8,128)(2,1)}, bf16[4,128,768]{2,1,0:T(8,128)(2,1)}) custom-call(bf16[4,2,384,1024]{3,2,1,0:T(8,128)(2,1)} %bitcast.155, bf16[4,2,128,3072]{3,2,1,0:T(8,128)(2,1)} %bitcast.156, bf16[4,2,128,3072]{3,2,1,0:T(8,128)(2,1)} %bitcast.157), custom_call_target="tpu_custom_call" | custom-call | tf_op jit(solution)/shard_map/reduce_grads/pallas_call | solution.py:300
  434.7 3.0 copy.80
  453.9 3.5 convolution_convert_fusion.5
  461.1 117.4 %reduce_grads.2 = (bf16[4,192,256]{2,1,0:T(8,128)(2,1)}, bf16[4,192,384]{2,1,0:T(8,128)(2,1)}, bf16[4,192,384]{2,1,0:T(8,128)(2,1)}, bf16[4,128,384]{2,1,0:T(8,1...) custom-call(bf16[4,2,192,1024]{3,2,1,0:T(8,128)(2,1)} %bitcast.160, bf16[4,2,192,1536]{3,2,1,0:T(8,128)(2,1)} %bitcast.158, ...), custom_call_target="tpu_custom_call" | custom-call | tf_op jit(solution)/shard_map/reduce_grads/pallas_call | solution.py:300
  (217 shorter events, 72.7 us)
Async XLA Ops:
  162.5 5.1 copy-start.30
  162.5 5.1 copy-start.39
  162.6 9.5 %slice-start = ((s8[6291456]{0:T(1024)(128)(4,1)}), s8[4194304]{0:T(1024)(128)(4,1)S(1)}, s32[]{:S(2)}) async-start(s8[6291456]{0:T(1024)(128)(4,1)} %bitcast.188), calls=%async_computation | async-start | bytes 8388608
  167.6 4.5 copy-start.17
  167.6 4.5 slice-start.1
  171.9 10.2 %slice-start.4 = ((s8[6291456]{0:T(1024)(128)(4,1)}), s8[4194304]{0:T(1024)(128)(4,1)S(1)}, s32[]{:S(2)}) async-start(s8[6291456]{0:T(1024)(128)(4,1)} %bitcast.192), calls=%async_computation.4 | async-start | bytes 8388608
  172.1 9.9 %slice-start.5 = ((s8[6291456]{0:T(1024)(128)(4,1)}), s8[2097152]{0:T(1024)(128)(4,1)S(1)}, s32[]{:S(2)}) async-start(s8[6291456]{0:T(1024)(128)(4,1)} %bitcast.192), calls=%async_computation.5 | async-start | bytes 4194304
  193.0 4.6 copy-start.33
  212.6 30.4 %copy-start.29 = (f32[8,1536]{1,0:T(8,128)S(1)}, f32[8,1536]{1,0:T(8,128)}, u32[]{:S(2)}) copy-start(f32[8,1536]{1,0:T(8,128)} %get-tuple-element.147) | copy-start | bytes 147460
  212.6 30.4 %copy-start.25 = (f32[1536]{0:T(1024)S(1)}, f32[1536]{0:T(1024)}, u32[]{:S(2)}) copy-start(f32[1536]{0:T(1024)} %param.30) | copy-start | bytes 18436
  243.1 5.9 copy-start.2
  243.1 5.9 copy-start.4
  243.1 5.9 copy-start.13
  243.1 10.9 %slice-start.8 = ((s8[4718592]{0:T(1024)(128)(4,1)}), s8[4194304]{0:T(1024)(128)(4,1)S(1)}, s32[]{:S(2)}) async-start(s8[4718592]{0:T(1024)(128)(4,1)} %bitcast.196), calls=%async_computation.8 | async-start | bytes 8388608
  249.0 5.0 slice-start.9
  263.4 189.4 %collective-permute-start = (f32[3,3,1536]{2,1,0:T(4,128)S(1)}, f32[3,3,1536]{2,1,0:T(4,128)S(1)}, u32[]{:S(2)}, u32[]{:S(2)}) collective-permute-start(f32[3,3,1536]{2,1,0:T(4,128)S(1)} %pad_add_fusion.1), channel_id=1, source_target_pairs={{1,0},{2,1},{3,2},{4,3},{5,4},{6,5},{7,6},{9,8},{10,9},{11,10},{12... | collective-permute-start | bytes 165896 | tf_op jit(solution)/shard_map/ppermute | solution.py:798
  266.4 8.9 %slice-start.2 = ((s8[6291456]{0:T(1024)(128)(4,1)}), s8[4194304]{0:T(1024)(128)(4,1)S(1)}, s32[]{:S(2)}) async-start(s8[6291456]{0:T(1024)(128)(4,1)} %bitcast.190), calls=%async_computation.2 | async-start | bytes 8388608
  270.9 4.4 copy-start.47
  278.8 5.4 copy-start.40
  278.8 5.4 copy-start.44
  284.2 5.4 copy-start.42
  289.6 5.8 copy-start.10
  289.6 5.8 copy-start.35
  578.5 4.7 copy-start.22
  (35 other events, 99.9 us)

commit v3 on v2

--- a/solution.py
+++ b/solution.py
@@ -33,330 +33,6 @@
     along_z = [(r, lax.rem(z + k, 4) * 2 + c) for k in (1, 2, 3)]
     return mate, along_x, along_y, along_z
 
-
-def reduce_kernel(count, has_small, *refs):
-    refs = list(refs)
-    grads = [refs.pop(0) for _ in range(count)]
-    small_in = refs.pop(0) if has_small else None
-    outs = [refs.pop(0) for _ in range(count)]
-    small_out = refs.pop(0) if has_small else None
-    held, own, first, second, third, final = (
-        [refs.pop(0) for _ in range(count)] for _ in range(6)
-    )
-    send, recv, local = refs.pop(0), refs.pop(0), refs.pop(0)
-    if has_small:
-        small_held, small_got, small_send, small_recv = refs
-    r, s, z, c = place()
-    mate, along_x, along_y, along_z = peers_of(r, s, z, c)
-    across_x, across_y = along_x[0], along_y[0]
-    diagonal = (3 - r, s)
-    rx, ry = lax.rem(r, 2), lax.div(r, 2)
-    greet([mate, along_x, along_y, diagonal] + along_z)
-    live = []
-
-    def remote(m, slot, src, dst, device):
-        copy = pltpu.make_async_remote_copy(
-            src_ref=src,
-            dst_ref=dst,
-            send_sem=send.at[m, slot],
-            recv_sem=recv.at[m, slot],
-            device_id=device,
-            device_id_type=MESH,
-        )
-        copy.start()
-        live.append(copy)
-        return copy
-
-    at_c, at_one, at_two, at_z, at_end, at_out = {}, {}, {}, {}, {}, {}
-
-    def begin(m):
-        part = held[m].shape[3]
-        at_c[m] = []
-        for q in range(4):
-            columns = pl.ds(q * part, part)
-            far = remote(m, q, grads[m].at[:, 1 - c, :, columns], held[m].at[q], mate)
-            near = pltpu.make_async_copy(
-                grads[m].at[:, c, :, columns], own[m].at[q], local.at[m, q]
-            )
-            near.start()
-            at_c[m].append((far, near))
-
-    small_copies = []
-
-    def small_exchange(slot, device):
-        copy = pltpu.make_async_remote_copy(
-            src_ref=small_held.at[slot],
-            dst_ref=small_got.at[slot],
-            send_sem=small_send.at[slot],
-            recv_sem=small_recv.at[slot],
-            device_id=device,
-            device_id_type=MESH,
-        )
-        copy.start()
-        small_copies.append(copy)
-        return copy
-
-    if has_small:
-        small_held[0] = small_in[...]
-        swap = small_exchange(0, mate)
-    begin(0)
-    if count > 1:
-        begin(1)
-    for tick in range(count + 4):
-        m = tick
-        if m < count:
-            _, _, depth, part = held[m].shape
-            half = depth // 2
-            for far, near in at_c[m]:
-                far.wait_recv()
-                near.wait()
-
-            def add_all(i, carry, m=m):
-                q, b = lax.div(i, 4), lax.rem(i, 4)
-                held[m][q, b] = held[m][q, b] + own[m][q, b]
-                return carry
-
-            lax.fori_loop(0, 16, add_all, 0)
-            at_one[m] = []
-            for other in range(2):
-                quarter = other * 2 + (1 - rx)
-                at_one[m].append(
-                    remote(
-                        m,
-                        4 + other,
-                        held[m].at[quarter, :, pl.ds(0, half)],
-                        first[m].at[0, other],
-                        along_x,
-                    )
-                )
-                quarter = (1 - ry) * 2 + other
-                at_one[m].append(
-                    remote(
-                        m,
-                        6 + other,
-                        held[m].at[quarter, :, pl.ds(half, half)],
-                        first[m].at[1, other],
-                        along_y,
-                    )
-                )
-        if tick + 2 < count:
-            begin(tick + 2)
-        m = tick - 1
-        if 0 <= m < count:
-            _, _, depth, part = held[m].shape
-            half = depth // 2
-            for copy in at_one[m]:
-                copy.wait_recv()
-
-            def add_one(i, carry, m=m, half=half):
-                other, b = lax.div(i, 4), lax.rem(i, 4)
-                qx = other * 2 + rx
-                held[m][qx, b, :half] = held[m][qx, b, :half] + first[m][0, other, b]
-                qy = ry * 2 + other
-                held[m][qy, b, half:] = held[m][qy, b, half:] + first[m][1, other, b]
-                return carry
-
-            lax.fori_loop(0, 8, add_one, 0)
-            at_two[m] = [
-                remote(
-                    m,
-                    8,
-                    held[m].at[(1 - ry) * 2 + rx, :, pl.ds(0, half)],
-                    second[m].at[0],
-                    along_y,
-                ),
-                remote(
-                    m,
-                    9,
-                    held[m].at[ry * 2 + (1 - rx), :, pl.ds(half, half)],
-                    second[m].at[1],
-                    along_x,
-                ),
-            ]
-        if has_small and tick == 1:
-            swap.wait_recv()
-            small_held[1] = small_held[0] + small_got[0]
-            swap = small_exchange(1, along_x)
-        m = tick - 2
-        if 0 <= m < count:
-            _, _, depth, part = held[m].shape
-            half = depth // 2
-            for copy in at_two[m]:
-                copy.wait_recv()
-
-            def add_two(b, carry, m=m, half=half):
-                held[m][r, b, :half] = held[m][r, b, :half] + second[m][0, b]
-                held[m][r, b, half:] = held[m][r, b, half:] + second[m][1, b]
-                return carry
-
-            lax.fori_loop(0, 4, add_two, 0)
-            at_z[m] = [
-                remote(
-                    m,
-                    9 + k,
-                    held[m].at[r, lax.rem(z + k, 4)],
-                    third[m].at[k - 1],
-                    along_z[k - 1],
-                )
-                for k in (1, 2, 3)
-            ]
-        if has_small and tick == 2:
-            swap.wait_recv()
-            small_held[2] = small_held[1] + small_got[1]
-            swap = small_exchange(2, along_y)
-        m = tick - 3
-        if 0 <= m < count:
-            for copy in at_z[m]:
-                copy.wait_recv()
-            mine = held[m][r, z].astype(jnp.float32)
-            for k in range(3):
-                mine = mine + third[m][k].astype(jnp.float32)
-            final[m][r] = mine.astype(jnp.bfloat16)
-            at_end[m] = [
-                remote(m, 13 + i, final[m].at[r], final[m].at[r], device)
-                for i, device in enumerate((along_x, along_y, diagonal))
-            ]
-        if has_small and tick == 3:
-            swap.wait_recv()
-            small_held[3] = small_held[2] + small_got[2]
-            spread = []
-            for k in (1, 2, 3):
-                copy = pltpu.make_async_remote_copy(
-                    src_ref=small_held.at[3],
-                    dst_ref=small_got.at[2 + k],
-                    send_sem=small_send.at[2 + k],
-                    recv_sem=small_recv.at[2 + k],
-                    device_id=along_z[k - 1],
-                    device_id_type=MESH,
-                )
-                copy.start()
-                small_copies.append(copy)
-                spread.append(copy)
-        m = tick - 4
-        if 0 <= m < count:
-            for copy in at_end[m]:
-                copy.wait_recv()
-            out = pltpu.make_async_copy(final[m], outs[m], local.at[m, 4])
-            out.start()
-            at_out[m] = out
-    if has_small:
-        for copy in spread:
-            copy.wait_recv()
-        small_got[6] = small_held[3]
-        total = None
-        for source in range(4):
-            k = lax.rem(z + 4 - source, 4)
-            slot = jnp.where(k == 0, 6, 2 + k)
-            term = small_got[slot]
-            total = term if total is None else total + term
-        small_out[...] = total
-        for copy in small_copies:
-            copy.wait_send()
-    for m in range(count):
-        at_out[m].wait()
-    for copy in live:
-        copy.wait_send()
-
-
-def reduce_all(grads, small, axis_size, tag):
-    if axis_size != 8 or lax.axis_size("rows") != 4:
-        blocks = [
-            lax.psum(lax.psum_scatter(g, "seq", scatter_dimension=0, tiled=True), "rows")
-            for g in grads
-        ]
-        if small is not None:
-            small = lax.psum(small, ("rows", "seq"))
-        return [b.astype(jnp.float32) for b in blocks], small
-    count = len(grads)
-    shapes = [(g.shape[0] // axis_size, g.shape[1] // 4) for g in grads]
-    views = [g.reshape(4, 2, k, 4 * n) for g, (k, n) in zip(grads, shapes)]
-    low = jnp.bfloat16
-    out_shape = [jax.ShapeDtypeStruct((4, k, n), low) for k, n in shapes]
-    out_specs = [ANY] * count
-    in_specs = [ANY] * count
-    scratch = [pltpu.VMEM((4, 4, k, n), low) for k, n in shapes]
-    scratch += [pltpu.VMEM((4, 4, k, n), low) for k, n in shapes]
-    scratch += [pltpu.VMEM((2, 2, 4, k // 2, n), low) for k, n in shapes]
-    scratch += [pltpu.VMEM((2, 4, k // 2, n), low) for k, n in shapes]
-    scratch += [pltpu.VMEM((3, k, n), low) for k, n in shapes]
-    scratch += [pltpu.VMEM((4, k, n), low) for k, n in shapes]
-    scratch += [
-        pltpu.SemaphoreType.DMA((count, 16)),
-        pltpu.SemaphoreType.DMA((count, 16)),
-        pltpu.SemaphoreType.DMA((count, 5)),
-    ]
-    args = list(views)
-    if small is not None:
-        args.append(small)
-        in_specs.append(VMEM)
-        out_shape.append(jax.ShapeDtypeStruct(small.shape, small.dtype))
-        out_specs.append(VMEM)
-        scratch += [
-            pltpu.VMEM((4,) + small.shape, small.dtype),
-            pltpu.VMEM((7,) + small.shape, small.dtype),
-            pltpu.SemaphoreType.DMA((6,)),
-            pltpu.SemaphoreType.DMA((6,)),
-        ]
-    results = pl.pallas_call(
-        functools.partial(reduce_kernel, count, small is not None),
-        out_shape=tuple(out_shape),
-        in_specs=in_specs,
-        out_specs=tuple(out_specs),
-        scratch_shapes=scratch,
-        compiler_params=pltpu.CompilerParams(
-            collective_id=tag, has_side_effects=True, vmem_limit_bytes=60 * 1024 * 1024
-        ),
-        name="reduce_grads",
-    )(*args)
-    blocks = [
-        b.transpose(1, 0, 2).reshape(k, 4 * n).astype(jnp.float32)
-        for b, (k, n) in zip(results[:count], shapes)
-    ]
-    return blocks, (results[count] if small is not None else None)
-
-
-def scan_kernel(reverse, a_ref, b_ref, p_ref, h_ref):
-    steps, width = a_ref.shape[1:]
-    tiles = steps // 8
-    spot = lax.broadcasted_iota(jnp.int32, (8, width), 0)
-
-    def shift(values, distance, fill):
-        if reverse:
-            moved = pltpu.roll(values, 8 - distance, 0)
-            return jnp.where(spot >= 8 - distance, fill, moved)
-        moved = pltpu.roll(values, distance, 0)
-        return jnp.where(spot < distance, fill, moved)
-
-    def tile(i, carry):
-        carry_a, carry_b = carry
-        t = tiles - 1 - i if reverse else i
-        rows = pl.ds(pl.multiple_of(t * 8, 8), 8)
-        a, b = a_ref[0, rows, :], b_ref[0, rows, :]
-        for distance in (1, 2, 4):
-            b = b + a * shift(b, distance, 0.0)
-            a = a * shift(a, distance, 1.0)
-        b = b + a * carry_b
-        a = a * carry_a
-        p_ref[0, rows, :] = a
-        h_ref[0, rows, :] = b
-        edge = slice(0, 1) if reverse else slice(7, 8)
-        return a[edge], b[edge]
-
-    ones, zeros = jnp.ones((1, width), jnp.float32), jnp.zeros((1, width), jnp.float32)
-    lax.fori_loop(0, tiles, tile, (ones, zeros))
-
-
-def scan(a, b, reverse):
-    count, steps, width = a.shape
-    block = pl.BlockSpec((1, steps, 512), lambda i, j: (i, 0, j))
-    return pl.pallas_call(
-        functools.partial(scan_kernel, reverse),
-        grid=(count, width // 512),
-        in_specs=[block, block],
-        out_specs=(block, block),
-        out_shape=(jax.ShapeDtypeStruct(a.shape, a.dtype),) * 2,
-        name="scan_back" if reverse else "scan_ahead",
-    )(a, b)
 
 def gelu_parts(v):
     inner = 0.7978845608028654 * (v + 0.044715 * v * v * v)
@@ -582,10 +258,11 @@
             columns = at(column, 512)
             window = padded[row, pl.ds(pl.multiple_of(block * 32, 8), 40), columns]
             rows = pl.ds(pl.multiple_of(row * 128 + block * 32, 32), 32)
+            spot = pl.ds(pl.multiple_of(block * 32, 32), 32)
             total = conv_b[:, columns] + conv_w[0:1, columns] * window[8:]
             for k in (1, 2, 3):
                 shifted = pltpu.roll(window, k, 0)[8:]
-                total = total + conv_w[k : k + 1, columns] * (marks[rows, k : k + 1] * shifted)
+                total = total + conv_w[k : k + 1, columns] * (marks[row, spot, k : k + 1] * shifted)
             conv_out[rows, columns] = total
             conv_low[rows, columns] = total.astype(jnp.bfloat16)
 
@@ -620,7 +297,7 @@
                 results = []
                 for row in range(3):
                     rows = pl.ds(pl.multiple_of(row * 128 + t * 8, 8), 8)
-                    reset = marks[rows, 0:1]
+                    reset = marks[row, pl.ds(pl.multiple_of(t * 8, 8), 8), 0:1]
                     rate_gate = jax.nn.sigmoid(rate_pre[rows, columns] + rate_b[:, columns])
                     input_gate = jax.nn.sigmoid(input_pre[rows, columns] + input_b[:, columns])
                     log_rate = decay_scale[:, columns] * rate_gate
@@ -792,6 +469,712 @@
     )(*shards, tokens, marks, *vectors)
     return results[:8], results[8:]
 
+class Reduction:
+    def __init__(self, grads, outs, scratch, sems):
+        self.grads, self.outs = grads, outs
+        self.count = len(grads)
+        self.held, self.own, self.first, self.second, self.third, self.final = scratch
+        self.send, self.recv, self.local = sems
+        self.live = []
+        self.at_c, self.at_one, self.at_two, self.at_z, self.at_end, self.at_out = (
+            {} for _ in range(6)
+        )
+        r, s, z, c = place()
+        self.r, self.z, self.c = r, z, c
+        self.mate, self.along_x, self.along_y, self.along_z = peers_of(r, s, z, c)
+        self.diagonal = (3 - r, s)
+        self.rx, self.ry = lax.rem(r, 2), lax.div(r, 2)
+
+    def peers(self):
+        return [self.mate, self.along_x, self.along_y, self.diagonal] + self.along_z
+
+    def remote(self, m, slot, src, dst, device):
+        copy = pltpu.make_async_remote_copy(
+            src_ref=src,
+            dst_ref=dst,
+            send_sem=self.send.at[m, slot],
+            recv_sem=self.recv.at[m, slot],
+            device_id=device,
+            device_id_type=MESH,
+        )
+        copy.start()
+        self.live.append(copy)
+        return copy
+
+    def load(self, m, q):
+        part = self.held[m].shape[3]
+        near = pltpu.make_async_copy(
+            self.grads[m].at[:, self.c, :, pl.ds(q * part, part)],
+            self.own[m].at[q % 2],
+            self.local.at[m, q],
+        )
+        near.start()
+        return near
+
+    def begin(self, m):
+        part = self.held[m].shape[3]
+        far = [
+            self.remote(
+                m,
+                q,
+                self.grads[m].at[:, 1 - self.c, :, pl.ds(q * part, part)],
+                self.held[m].at[q],
+                self.mate,
+            )
+            for q in range(4)
+        ]
+        self.at_c[m] = (far, [self.load(m, 0), self.load(m, 1)])
+
+    def stage_core(self, m):
+        held, own = self.held[m], self.own[m]
+        half = held.shape[2] // 2
+        far, near = self.at_c[m]
+        for q in range(4):
+            far[q].wait_recv()
+            near[q].wait()
+
+            def add(b):
+                held[q, b] = held[q, b] + own[q % 2, b]
+
+            loop(4, add)
+            if q < 2:
+                near.append(self.load(m, q + 2))
+        self.at_one[m] = []
+        for other in range(2):
+            quarter = other * 2 + (1 - self.rx)
+            self.at_one[m].append(
+                self.remote(
+                    m,
+                    4 + other,
+                    held.at[quarter, :, pl.ds(0, half)],
+                    self.first[m].at[0, other],
+                    self.along_x,
+                )
+            )
+            quarter = (1 - self.ry) * 2 + other
+            self.at_one[m].append(
+                self.remote(
+                    m,
+                    6 + other,
+                    held.at[quarter, :, pl.ds(half, half)],
+                    self.first[m].at[1, other],
+                    self.along_y,
+                )
+            )
+
+    def stage_one(self, m):
+        held, first = self.held[m], self.first[m]
+        half = held.shape[2] // 2
+        for copy in self.at_one[m]:
+            copy.wait_recv()
+
+        def add(i):
+            other, b = lax.div(i, 4), lax.rem(i, 4)
+            qx = other * 2 + self.rx
+            held[qx, b, :half] = held[qx, b, :half] + first[0, other, b]
+            qy = self.ry * 2 + other
+            held[qy, b, half:] = held[qy, b, half:] + first[1, other, b]
+
+        loop(8, add)
+        self.at_two[m] = [
+            self.remote(
+                m,
+                8,
+                held.at[(1 - self.ry) * 2 + self.rx, :, pl.ds(0, half)],
+                self.second[m].at[0],
+                self.along_y,
+            ),
+            self.remote(
+                m,
+                9,
+                held.at[self.ry * 2 + (1 - self.rx), :, pl.ds(half, half)],
+                self.second[m].at[1],
+                self.along_x,
+            ),
+        ]
+
+    def stage_two(self, m):
+        held, second, r = self.held[m], self.second[m], self.r
+        half = held.shape[2] // 2
+        for copy in self.at_two[m]:
+            copy.wait_recv()
+
+        def add(b):
+            held[r, b, :half] = held[r, b, :half] + second[0, b]
+            held[r, b, half:] = held[r, b, half:] + second[1, b]
+
+        loop(4, add)
+        self.at_z[m] = [
+            self.remote(
+                m,
+                9 + k,
+                held.at[r, lax.rem(self.z + k, 4)],
+                self.third[m].at[k - 1],
+                self.along_z[k - 1],
+            )
+            for k in (1, 2, 3)
+        ]
+
+    def stage_z(self, m):
+        held, third, final, r = self.held[m], self.third[m], self.final[m], self.r
+        for copy in self.at_z[m]:
+            copy.wait_recv()
+        depth = held.shape[2]
+
+        def add(i):
+            rows = at(i, 32)
+            mine = held[r, self.z, rows, :].astype(jnp.float32)
+            for k in range(3):
+                mine = mine + third[k, rows, :].astype(jnp.float32)
+            final[r, rows, :] = mine.astype(jnp.bfloat16)
+
+        loop(depth // 32, add)
+        self.at_end[m] = [
+            self.remote(m, 13 + i, final.at[r], final.at[r], device)
+            for i, device in enumerate((self.along_x, self.along_y, self.diagonal))
+        ]
+
+    def stage_end(self, m):
+        for copy in self.at_end[m]:
+            copy.wait_recv()
+        out = pltpu.make_async_copy(self.final[m], self.outs[m], self.local.at[m, 4])
+        out.start()
+        self.at_out[m] = out
+
+    def tick(self, now):
+        stages = (self.stage_core, self.stage_one, self.stage_two, self.stage_z, self.stage_end)
+        for late, stage in enumerate(stages):
+            if 0 <= now - late < self.count:
+                stage(now - late)
+            if late == 0 and now + 2 < self.count:
+                self.begin(now + 2)
+
+    def ticks(self):
+        return self.count + 4
+
+    def close(self):
+        for m in range(self.count):
+            self.at_out[m].wait()
+        for copy in self.live:
+            copy.wait_send()
+
+
+REDUCTION_SEMS = 16
+
+
+def reduction_memory(shapes):
+    low = jnp.bfloat16
+    count = len(shapes)
+    scratch = [pltpu.VMEM((4, 4, k, n), low) for k, n in shapes]
+    scratch += [pltpu.VMEM((2, 4, k, n), low) for k, n in shapes]
+    scratch += [pltpu.VMEM((2, 2, 4, k // 2, n), low) for k, n in shapes]
+    scratch += [pltpu.VMEM((2, 4, k // 2, n), low) for k, n in shapes]
+    scratch += [pltpu.VMEM((3, k, n), low) for k, n in shapes]
+    scratch += [pltpu.VMEM((4, k, n), low) for k, n in shapes]
+    return scratch + [
+        pltpu.SemaphoreType.DMA((count, REDUCTION_SEMS)),
+        pltpu.SemaphoreType.DMA((count, REDUCTION_SEMS)),
+        pltpu.SemaphoreType.DMA((count, 5)),
+    ]
+
+
+def take_reduction(take, count):
+    scratch = [take(count) for _ in range(6)]
+    return scratch, take(3)
+
+
+def taker(refs):
+    refs = list(refs)
+
+    def take(n):
+        taken, refs[:n] = refs[:n], []
+        return taken
+
+    return take
+
+
+def split_rows(grad):
+    return grad.reshape(4, 2, grad.shape[0] // 8, grad.shape[1])
+
+
+def quarter_shape(grad):
+    return grad.shape[0] // 8, grad.shape[1] // 4
+
+
+def joined(block):
+    quarters, depth, part = block.shape
+    return block.transpose(1, 0, 2).reshape(depth, quarters * part).astype(jnp.float32)
+
+
+def reduce_kernel(count, *refs):
+    take = taker(refs)
+    grads = take(count)
+    (small_in,) = take(1)
+    outs = take(count)
+    (small_out,) = take(1)
+    reduction = Reduction(grads, outs, *take_reduction(take, count))
+    small_held, small_got, small_send, small_recv = take(4)
+    z = reduction.z
+    greet(reduction.peers())
+    small_copies = []
+
+    def swap_small(slot, source, device):
+        copy = pltpu.make_async_remote_copy(
+            src_ref=small_held.at[source],
+            dst_ref=small_got.at[slot],
+            send_sem=small_send.at[slot],
+            recv_sem=small_recv.at[slot],
+            device_id=device,
+            device_id_type=MESH,
+        )
+        copy.start()
+        small_copies.append(copy)
+        return copy
+
+    small_held[0] = small_in[...]
+    swap = swap_small(0, 0, reduction.mate)
+    reduction.begin(0)
+    if count > 1:
+        reduction.begin(1)
+    for now in range(reduction.ticks()):
+        reduction.tick(now)
+        if now < 2:
+            swap.wait_recv()
+            small_held[now + 1] = small_held[now] + small_got[now]
+            swap = swap_small(now + 1, now + 1, (reduction.along_x, reduction.along_y)[now])
+        if now == 2:
+            swap.wait_recv()
+            small_held[3] = small_held[2] + small_got[2]
+            spread = [swap_small(2 + k, 3, reduction.along_z[k - 1]) for k in (1, 2, 3)]
+    for copy in spread:
+        copy.wait_recv()
+    small_got[6] = small_held[3]
+    total = None
+    for source in range(4):
+        k = lax.rem(z + 4 - source, 4)
+        slot = jnp.where(k == 0, 6, 2 + k)
+        term = small_got[slot]
+        total = term if total is None else total + term
+    small_out[...] = total
+    for copy in small_copies:
+        copy.wait_send()
+    reduction.close()
+
+
+def reduce_all(grads, small, tag):
+    count = len(grads)
+    shapes = [quarter_shape(g) for g in grads]
+    results = pl.pallas_call(
+        functools.partial(reduce_kernel, count),
+        out_shape=tuple(jax.ShapeDtypeStruct((4, k, n), jnp.bfloat16) for k, n in shapes)
+        + (jax.ShapeDtypeStruct(small.shape, small.dtype),),
+        in_specs=[ANY] * count + [VMEM],
+        out_specs=(ANY,) * count + (VMEM,),
+        scratch_shapes=reduction_memory(shapes)
+        + [
+            pltpu.VMEM((4,) + small.shape, small.dtype),
+            pltpu.VMEM((7,) + small.shape, small.dtype),
+            pltpu.SemaphoreType.DMA((6,)),
+            pltpu.SemaphoreType.DMA((6,)),
+        ],
+        compiler_params=pltpu.CompilerParams(
+            collective_id=tag, has_side_effects=True, vmem_limit_bytes=60 * 1024 * 1024
+        ),
+        name="reduce_grads",
+    )(*[split_rows(g) for g in grads], small)
+    return [joined(b) for b in results[:count]], results[count]
+
+
+def backward_kernel(count, *refs):
+    take = taker(refs)
+    grads = take(count)
+    full_out, full_rate, full_input, full_branch, full_rec = take(5)
+    saved_states, saved_branch, saved_rate, saved_input, saved_conv, saved_rec = take(6)
+    resid_low, marks, tokens, grad_resid, normed, conv_low, mixed_in, carried = take(8)
+    conv_w, rate_b, input_b, decay_scale, gain1 = take(5)
+    outs = take(count)
+    d_out, d_rate, d_input, d_branch, d_rec, token_grad = take(6)
+    small, small_norm = take(2)
+    reduction = Reduction(grads, outs, *take_reduction(take, count))
+    ring, past, branch_pre, rate_pre, input_pre, conv_out = take(6)
+    flow, grads_conv, branch_low, rate_low, input_low, stage = take(6)
+    rim, ends, got, carry = take(4)
+    near_send, near_recv, load_sem, ring_sem, stage_sem = take(5)
+    r, s, z, c = place()
+    others = [(r, lax.rem(s + k, 8)) for k in range(1, 8)]
+    greet(others + [reduction.along_x, reduction.along_y, reduction.diagonal])
+    live = []
+
+    def near(slot, src, dst, device):
+        copy = pltpu.make_async_remote_copy(
+            src_ref=src,
+            dst_ref=dst,
+            send_sem=near_send.at[slot],
+            recv_sem=near_recv.at[slot],
+            device_id=device,
+            device_id_type=MESH,
+        )
+        copy.start()
+        live.append(copy)
+        return copy
+
+    def bring(slot, src, dst):
+        copy = pltpu.make_async_copy(src, dst, load_sem.at[slot])
+        copy.start()
+        return copy
+
+    tiles = []
+    for weight in (full_out, full_rate, full_input, full_branch, full_rec):
+        tiles.append([(weight, j) for j in range(weight.shape[0] // 512)])
+    out_tiles, rate_tiles, input_tiles, branch_tiles, rec_tiles = tiles
+    order = list(out_tiles)
+    for pair in zip(rate_tiles, input_tiles):
+        order += pair
+    for pair in zip(branch_tiles, rec_tiles):
+        order += pair
+    fetches = {}
+
+    def fetch(i):
+        if i < len(order):
+            weight, j = order[i]
+            copy = pltpu.make_async_copy(
+                weight.at[pl.ds(j * 512, 512)],
+                ring.at[i % 3, :, pl.ds(0, weight.shape[1])],
+                ring_sem.at[i % 3],
+            )
+            copy.start()
+            fetches[i] = copy
+
+    def back_tile(i, left, depth):
+        fetches[i].wait()
+        return lax.dot_general(
+            left[...],
+            ring[i % 3, :, pl.ds(0, depth)],
+            (((1,), (1,)), ((), ())),
+            preferred_element_type=jnp.float32,
+        )
+
+    staged = [None, None]
+    turn = [0]
+
+    def outer_product(left, right, target):
+        for strip in range(left.shape[1] // 512):
+            slot = turn[0] % 2
+            turn[0] += 1
+            if staged[slot] is not None:
+                staged[slot].wait()
+            rows = pl.ds(strip * 512, 512)
+            width = right.shape[1]
+
+            def one(j):
+                columns = at(j, 512)
+                stage[slot, :, columns] = lax.dot_general(
+                    left[:, rows],
+                    right[:, columns],
+                    (((0,), (0,)), ((), ())),
+                    preferred_element_type=jnp.float32,
+                ).astype(jnp.bfloat16)
+
+            loop(width // 512, one)
+            copy = pltpu.make_async_copy(
+                stage.at[slot, :, pl.ds(0, width)], target.at[rows], stage_sem.at[slot]
+            )
+            copy.start()
+            staged[slot] = copy
+
+    def block_of(i):
+        row, block = lax.div(i, 4), lax.rem(i, 4)
+        return row, block, pl.ds(pl.multiple_of(row * 128 + block * 32, 32), 32)
+
+    def folded(values):
+        return values[0:8] + values[8:16] + values[16:24] + values[24:32]
+
+    def gates(rows, columns, mark_rows):
+        rate_gate = jax.nn.sigmoid(rate_pre[rows, columns] + rate_b[:, columns])
+        log_rate = decay_scale[:, columns] * rate_gate
+        return rate_gate, log_rate, jnp.exp(log_rate)
+
+    def branch_back():
+        def one(i):
+            column, rest = lax.div(i, 12), lax.rem(i, 12)
+            row, block, rows = block_of(rest)
+            columns = at(column, 512)
+            act, slope = gelu_parts(branch_pre[rows, columns])
+            grad = flow[rows, columns]
+            state = past[row, pl.ds(pl.multiple_of(block * 32 + 8, 8), 32), columns]
+            flow[rows, columns] = grad * act
+            branch_low[rows, columns] = (grad * state * slope).astype(jnp.bfloat16)
+
+        loop(36, one)
+
+    def scan_back():
+        def one(column):
+            columns = at(column, 512)
+            spot = lax.broadcasted_iota(jnp.int32, (8, 512), 0)
+
+            def tile(i, state):
+                t = 15 - i
+                results = []
+                for row in range(3):
+                    rows = pl.ds(pl.multiple_of(row * 128 + t * 8, 8), 8)
+                    keep = 1.0 - marks[row, pl.ds(pl.multiple_of(t * 8, 8), 8), 0:1]
+                    _, _, pace = gates(rows, columns, None)
+                    decay = pace * keep
+                    follow, carry_a, carry_b = state[3 * row : 3 * row + 3]
+                    later = jnp.where(spot == 7, follow, pltpu.roll(decay, 7, 0))
+                    a, b = tile_scan(later, flow[rows, columns], True)
+                    b = b + a * carry_b
+                    a = a * carry_a
+                    branch_pre[rows, columns] = a
+                    flow[rows, columns] = b
+                    results += [decay[0:1], a[0:1], b[0:1]]
+                return tuple(results)
+
+            ones, zeros = jnp.ones((1, 512), jnp.float32), jnp.zeros((1, 512), jnp.float32)
+            last = lax.fori_loop(0, 16, tile, (ones, ones, zeros) * 3)
+            for row in range(3):
+                decay, a, b = last[3 * row : 3 * row + 3]
+                ends[row : row + 1, columns] = decay * a
+                ends[3 + row : 4 + row, columns] = decay * b
+
+        loop(3, one)
+        return [near(k, ends, got.at[k], others[k - 1]) for k in range(1, 8)]
+
+    def carry_back(copies):
+        for copy in copies:
+            copy.wait_recv()
+
+        def one(column):
+            columns = at(column, 512)
+            state = jnp.zeros((3, 512), jnp.float32)
+            for ahead in range(7, 0, -1):
+                k = 8 - ahead
+                after = got[k, 3:6, columns] + got[k, 0:3, columns] * state
+                state = jnp.where(s + ahead <= 7, after, state)
+            carry[0:3, columns] = state
+
+        loop(3, one)
+
+    def gates_back():
+        def one(column):
+            columns = at(column, 512)
+
+            def block_step(i, sums):
+                row, block, rows = block_of(i)
+                mark = pl.ds(pl.multiple_of(block * 32, 32), 32)
+                reset = marks[row, mark, 0:1]
+                keep = 1.0 - reset
+                rate_gate, log_rate, pace = gates(rows, columns, mark)
+                input_gate = jax.nn.sigmoid(input_pre[rows, columns] + input_b[:, columns])
+                power = pace * pace
+                root = jnp.sqrt(minus_expm1(2.0 * log_rate, power))
+                scale = reset + keep * root
+                conv = conv_out[rows, columns]
+                grad = flow[rows, columns] + branch_pre[rows, columns] * carry[
+                    pl.ds(row, 1), columns
+                ]
+                window = past[row, pl.ds(pl.multiple_of(block * 32, 8), 40), columns]
+                before = pltpu.roll(window, 1, 0)[8:]
+                grad_log = keep * grad * (before * pace - input_gate * conv * power / root)
+                decay_sum = rate_gate * grad_log
+                rate_grad = decay_scale[:, columns] * decay_sum * (1.0 - rate_gate)
+                direct = grad * scale * input_gate
+                input_grad = direct * conv * (1.0 - input_gate)
+                rate_low[rows, columns] = rate_grad.astype(jnp.bfloat16)
+                input_low[rows, columns] = input_grad.astype(jnp.bfloat16)
+                rate_pre[rows, columns] = direct
+                return (
+                    sums[0] + folded(decay_sum),
+                    sums[1] + folded(rate_grad),
+                    sums[2] + folded(input_grad),
+                )
+
+            zeros = jnp.zeros((8, 512), jnp.float32)
+            sums = lax.fori_loop(0, 12, block_step, (zeros,) * 3)
+            for spot, values in enumerate(sums):
+                small[5 + spot : 6 + spot, columns] = jnp.sum(values, axis=0, keepdims=True)
+
+        loop(3, one)
+
+    def conv_back(copy):
+        copy.wait_recv()
+        for row in range(3):
+            grads_conv[row, 128:136, :] = jnp.where(s < 7, rim[row], 0.0)
+
+        def one(column):
+            columns = at(column, 512)
+
+            def block_step(i, sums):
+                row, block, rows = block_of(i)
+                span = pl.ds(pl.multiple_of(block * 32, 8), 40)
+                ahead = grads_conv[row, span, columns]
+                behind = past[row, span, columns]
+                grad = ahead[:32]
+                total = conv_w[0:1, columns] * grad
+                new = [sums[0] + folded(grad * behind[8:])]
+                for k in (1, 2, 3):
+                    kept = ahead * marks[row, span, k : k + 1]
+                    total = total + conv_w[k : k + 1, columns] * pltpu.roll(kept, 40 - k, 0)[:32]
+                    new.append(
+                        sums[k] + folded(kept[:32] * pltpu.roll(behind, k, 0)[8:])
+                    )
+                new.append(sums[4] + folded(grad))
+                rate_low[rows, columns] = total.astype(jnp.bfloat16)
+                return tuple(new)
+
+            zeros = jnp.zeros((8, 512), jnp.float32)
+            sums = lax.fori_loop(0, 12, block_step, (zeros,) * 5)
+            for spot, values in enumerate(sums):
+                small[spot : spot + 1, columns] = jnp.sum(values, axis=0, keepdims=True)
+
+        loop(3, one)
+
+    def norm_back():
+        def one(i, total):
+            rows = at(i, 16)
+            values = tokens[rows, :].astype(jnp.float32)
+            scale = lax.rsqrt(jnp.mean(values * values, axis=-1, keepdims=True) + epsilon)
+            grad = input_pre[rows, pl.ds(0, 1024)]
+            back = grad * gain1[...]
+            mean = jnp.mean(values * back, axis=-1, keepdims=True)
+            result = grad_resid[rows, :] + scale * back - values * (scale * scale * scale * mean)
+            stage[0, rows, pl.ds(0, 1024)] = result.astype(jnp.bfloat16)
+            part = grad * values * scale
+            return total + part[0:8] + part[8:16]
+
+        if staged[0] is not None:
+            staged[0].wait()
+        total = lax.fori_loop(0, 24, one, jnp.zeros((8, 1024), jnp.float32))
+        small_norm[...] = jnp.sum(total, axis=0, keepdims=True)
+        copy = pltpu.make_async_copy(
+            stage.at[0, pl.ds(0, 384), pl.ds(0, 1024)], token_grad, stage_sem.at[0]
+        )
+        copy.start()
+        staged[0] = copy
+
+    reduction.begin(0)
+    reduction.begin(1)
+    loads = [
+        bring(0, saved_branch, branch_pre),
+        bring(1, saved_states, past.at[:, pl.ds(8, 128), :]),
+        bring(2, saved_rate, rate_pre),
+        bring(3, saved_input, input_pre),
+        bring(4, saved_conv, conv_out),
+    ]
+    for i in range(3):
+        fetch(i)
+    ends[...] = jnp.zeros_like(ends)
+    for row in range(3):
+        past[row, 0:8, :] = jnp.broadcast_to(carried[row : row + 1, :], (8, past.shape[2]))
+    for i in range(3):
+        flow[:, pl.ds(i * 512, 512)] = back_tile(i, resid_low, 1024)
+        fetch(i + 3)
+    reduction.tick(0)
+    loads[0].wait()
+    loads[1].wait()
+    branch_back()
+    loads[2].wait()
+    copies = scan_back()
+    outer_product(mixed_in, resid_low, d_out)
+    reduction.tick(1)
+    carry_back(copies)
+    loads[3].wait()
+    loads[4].wait()
+    gates_back()
+    loads.append(bring(5, saved_rec, past))
+    at_tile = 3
+    for j in range(3):
+        columns = pl.ds(j * 512, 512)
+        total = rate_pre[:, columns]
+        total = total + back_tile(at_tile, rate_low, 1536)
+        fetch(at_tile + 3)
+        total = total + back_tile(at_tile + 1, input_low, 1536)
+        fetch(at_tile + 4)
+        at_tile += 2
+        for row in range(3):
+            grads_conv[row, 0:128, columns] = total[row * 128 : (row + 1) * 128]
+    rim_copy = near(0, grads_conv.at[:, pl.ds(0, 8), :], rim, others[6])
+    reduction.tick(2)
+    outer_product(conv_low, rate_low, d_rate)
+    loads[5].wait()
+    conv_back(rim_copy)
+    for j in range(2):
+        columns = pl.ds(j * 512, 512)
+        total = back_tile(at_tile, branch_low, 1536)
+        fetch(at_tile + 3)
+        total = total + back_tile(at_tile + 1, rate_low, 1536)
+        fetch(at_tile + 4)
+        at_tile += 2
+        input_pre[:, columns] = total
+    reduction.tick(3)
+    outer_product(normed, rate_low, d_rec)
+    outer_product(conv_low, input_low, d_input)
+    reduction.tick(4)
+    outer_product(normed, branch_low, d_branch)
+    norm_back()
+    for now in range(5, reduction.ticks()):
+        reduction.tick(now)
+    for copy in staged:
+        copy.wait()
+    for copy in live:
+        copy.wait_send()
+    reduction.close()
+
+
+def backward_all(grads, fulls, saved, local, vectors):
+    low, full = jnp.bfloat16, jnp.float32
+    shape, memory = jax.ShapeDtypeStruct, pltpu.VMEM
+    shapes = [quarter_shape(g) for g in grads]
+    count = len(grads)
+    tok, model = local[0].shape
+    rec = fulls[0].shape[0]
+    out_shape = tuple(shape((4, k, n), low) for k, n in shapes) + (
+        shape((rec, model), low),
+        shape((rec, rec), low),
+        shape((rec, rec), low),
+        shape((model, rec), low),
+        shape((model, rec), low),
+        shape((tok, model), low),
+        shape((8, rec), full),
+        shape((1, model), full),
+    )
+    results = pl.pallas_call(
+        functools.partial(backward_kernel, count),
+        out_shape=out_shape,
+        in_specs=[ANY] * (count + 11) + [VMEM] * 13,
+        out_specs=(ANY,) * (count + 6) + (VMEM,) * 2,
+        scratch_shapes=reduction_memory(shapes)
+        + [
+            memory((3, 512, rec), low),
+            memory((3, 136, rec), full),
+            memory((tok, rec), full),
+            memory((tok, rec), full),
+            memory((tok, rec), full),
+            memory((tok, rec), full),
+            memory((tok, rec), full),
+            memory((3, 136, rec), full),
+            memory((tok, rec), low),
+            memory((tok, rec), low),
+            memory((tok, rec), low),
+            memory((2, 512, rec), low),
+            memory((3, 8, rec), full),
+            memory((8, rec), full),
+            memory((8, 8, rec), full),
+            memory((8, rec), full),
+            pltpu.SemaphoreType.DMA((8,)),
+            pltpu.SemaphoreType.DMA((8,)),
+            pltpu.SemaphoreType.DMA((6,)),
+            pltpu.SemaphoreType.DMA((3,)),
+            pltpu.SemaphoreType.DMA((2,)),
+        ],
+        compiler_params=pltpu.CompilerParams(
+            collective_id=1, has_side_effects=True, vmem_limit_bytes=62 * 1024 * 1024
+        ),
+        name="recurrent_backward",
+    )(*[split_rows(g) for g in grads], *fulls, *saved, *local, *vectors)
+    return [joined(b) for b in results[:count]], results[count:]
+
+
 def from_behind(block, axis, distance):
     devices = range(lax.axis_size(axis))
     route = [(i - distance, i) for i in devices if i - distance in devices]
@@ -1082,14 +1465,14 @@
     row_count, tok_count, model_width = tokens.shape
     rec_width = w_rec.shape[1]
     offset = lax.axis_index("seq") * tok_count
-    positions = offset - 3 + jnp.arange(tok_count + 3, dtype=jnp.int32)
+    positions = offset - 3 + jnp.arange(tok_count + 11, dtype=jnp.int32)
     marked = (
         jnp.any(positions[None, :, None] == bounds[:, None, :], axis=2) | (positions == 0)[None, :]
     )
     padded_resets = marked.astype(jnp.float32)
     resets = padded_resets[:, 3:]
     masks = conv_masks(padded_resets)
-    marks = jnp.stack((resets,) + masks + (resets,) * 4, axis=2).reshape(-1, 8)
+    marks = jnp.stack((resets,) + masks + (resets,) * 4, axis=2)
     flat_tokens = tokens.reshape(-1, model_width)
     decay_scale = (-8.0 * jax.nn.softplus(decay_param))[None]
     fulls, saved = forward_all(
@@ -1107,25 +1490,8 @@
         ),
     )
     full_rec, full_rate, full_input, full_branch, full_out, full_gate, full_up, full_down = fulls
-    normed, padded_all, conv_out, conv_low, rate_pre, input_pre = saved[:6]
+    normed, padded, conv_out, conv_low, rate_pre, input_pre = saved[:6]
     states, branch_pre, mixed_in, resid, carried, normed2 = saved[6:]
-    shape = (row_count, tok_count, rec_width)
-    conv_out, rate_pre, input_pre = (a.reshape(shape) for a in (conv_out, rate_pre, input_pre))
-    states = states.reshape(shape)
-    carry_in = carried[:3]
-    padded = padded_all[:, 5:, :]
-    inputs = flat_tokens.astype(jnp.float32)
-
-    def gates_of(rate_arg, input_arg, conv_arg, decay_arg, rate_arg_bias, input_arg_bias):
-        return gate_terms(
-            rate_arg, input_arg, conv_arg, decay_arg, rate_arg_bias, input_arg_bias, resets
-        )
-
-    decays, drives = gates_of(rate_pre, input_pre, conv_out, decay_param, rate_bias, input_bias)
-    ones_pair = jnp.ones((row_count, rec_width), jnp.float32)
-    zeros_pair = jnp.zeros((row_count, rec_width), jnp.float32)
-    earlier_states = jnp.concatenate([carry_in[:, None, :], states[:, :-1, :]], axis=1)
-    branch_act = jax.nn.gelu(branch_pre, approximate=True).reshape(states.shape)
     gate_pre = forward_product(normed2, full_gate)
     up_pre = forward_product(normed2, full_up)
     hidden = (jax.nn.gelu(gate_pre, approximate=True) * up_pre).astype(jnp.bfloat16)
@@ -1146,106 +1512,50 @@
     grad_resid_norm, grad_norm2 = pull_norm2(grad_normed2)
     grad_resid = cot_low.astype(jnp.float32) + grad_resid_norm
     resid_low = grad_resid.astype(jnp.bfloat16)
-    grad_out = outer(mixed_in, resid_low)
-    grad_mixed = back_product(resid_low, full_out).reshape(states.shape)
-    grad_states = grad_mixed * branch_act
-    _, pull_branch = jax.vjp(lambda pre_arg: jax.nn.gelu(pre_arg, approximate=True), branch_pre)
-    branch_low = pull_branch((grad_mixed * states).reshape(-1, rec_width))[0].astype(jnp.bfloat16)
-    next_decays = jnp.concatenate([decays[:, 1:, :], ones_pair[:, None, :]], axis=1)
-    suffix_decay, local_grads = scan(next_decays, grad_states, True)
-    element = (decays[:, 0] * suffix_decay[:, 0], decays[:, 0] * local_grads[:, 0])
-    carry_back = prefix(element, "seq", combine, (ones_pair, zeros_pair), True)[1]
-    state_grads = local_grads + suffix_decay * carry_back[:, None, :]
-    _, pull_gates = jax.vjp(
-        gates_of, rate_pre, input_pre, conv_out, decay_param, rate_bias, input_bias
-    )
-    grad_rate_pre, grad_input_pre, grad_conv_direct, grad_decay, grad_rate_bias, grad_input_bias = (
-        pull_gates((state_grads * earlier_states, state_grads))
-    )
-    rate_low = grad_rate_pre.astype(jnp.bfloat16).reshape(-1, rec_width)
-    input_low = grad_input_pre.astype(jnp.bfloat16).reshape(-1, rec_width)
-    grad_rate = outer(conv_low, rate_low)
-    grad_input = outer(conv_low, input_low)
-    grad_conv = grad_conv_direct + (
-        back_product(rate_low, full_rate) + back_product(input_low, full_input)
-    ).reshape(conv_out.shape)
-    _, pull_conv = jax.vjp(
-        lambda pad_arg, weight_arg, bias_arg: convolve(pad_arg, masks, weight_arg, bias_arg),
-        padded,
-        conv_weight,
-        conv_bias,
-    )
-    grad_padded, grad_conv_weight, grad_conv_bias = pull_conv(grad_conv)
-    rim_back = from_behind(grad_padded[:, :3, :], "seq", -1)
-    grad_rec = grad_padded[:, 3:, :] + jnp.concatenate(
-        [jnp.zeros((row_count, tok_count - 3, rec_width), jnp.float32), rim_back], axis=1
-    )
-    rec_low = grad_rec.astype(jnp.bfloat16).reshape(-1, rec_width)
-    grad_rec_w = outer(normed, rec_low)
-    grad_branch_w = outer(normed, branch_low)
-    grad_normed = back_product(branch_low, full_branch) + back_product(rec_low, full_rec)
-    _, pull_norm1 = jax.vjp(rms_norm, inputs, norm1_gain)
-    grad_inputs, grad_norm1 = pull_norm1(grad_normed)
-    token_grad = (grad_resid + grad_inputs).astype(jnp.bfloat16).reshape(tokens.shape)
     low = jnp.bfloat16
-    axis_size = 8
-    ff, _ = reduce_all(
-        [g.astype(low) for g in (grad_down, grad_gate, grad_up)], None, axis_size, 1
-    )
-    flat = jnp.concatenate(
+    ff, rest = backward_all(
+        [g.astype(low) for g in (grad_down, grad_gate, grad_up)],
+        (full_out, full_rate, full_input, full_branch, full_rec),
+        (
+            states.reshape(row_count, tok_count, rec_width),
+            branch_pre,
+            rate_pre,
+            input_pre,
+            conv_out,
+            padded,
+        ),
+        (resid_low, marks, flat_tokens, grad_resid, normed, conv_low, mixed_in, carried),
+        (conv_weight, rate_bias[None], input_bias[None], decay_scale, norm1_gain[None]),
+    )
+    rec_grads, (token_grad, sums, grad_norm1) = rest[:5], rest[5:]
+    small = jnp.concatenate(
         [
-            g.reshape(-1)
-            for g in (
-                grad_norm1,
-                grad_conv_weight,
-                grad_conv_bias,
-                grad_rate_bias,
-                grad_input_bias,
-                grad_decay,
-                grad_norm2,
-            )
+            sums.reshape(-1, model_width),
+            grad_norm1,
+            grad_norm2[None],
+            jnp.zeros((2, model_width), jnp.float32),
         ]
     )
-    size = flat.shape[0]
-    flat = jnp.pad(flat, (0, -size % 8192)).reshape(-1, 1024)
-    rec, flat = reduce_all(
-        [g.astype(low) for g in (grad_out, grad_rate, grad_input, grad_branch_w, grad_rec_w)],
-        flat,
-        axis_size,
-        2,
-    )
-    flat = flat.reshape(-1)
-    small, begin = [], 0
-    for like in (
-        grad_norm1,
-        grad_conv_weight,
-        grad_conv_bias,
-        grad_rate_bias,
-        grad_input_bias,
-        grad_decay,
-        grad_norm2,
-    ):
-        small.append(flat[begin : begin + like.size].reshape(like.shape))
-        begin += like.size
-    summed = (rec[3], rec[4], rec[1], rec[2], rec[0], ff[1], ff[2], ff[0])
+    rec, small = reduce_all(rec_grads, small, 2)
+    sums = small[:12].reshape(8, rec_width)
     return (
         mixed,
-        token_grad,
-        small[0],
-        summed[0],
-        summed[1],
-        small[1],
-        small[2],
-        summed[2],
-        small[3],
-        summed[3],
-        small[4],
-        small[5],
-        summed[4],
-        small[6],
-        summed[5],
-        summed[6],
-        summed[7],
+        token_grad.reshape(tokens.shape),
+        small[12],
+        rec[3],
+        rec[4],
+        sums[:4],
+        sums[4],
+        rec[1],
+        sums[6],
+        rec[2],
+        sums[7],
+        -8.0 * jax.nn.sigmoid(decay_param) * sums[5],
+        rec[0],
+        small[13],
+        ff[1],
+        ff[2],
+        ff[0],
     )
 
 

time: 600 us -> 485 us (0.81)
  matrix products: 79.1 us -> 43.4 us
  blocking collectives: 28.1 us -> 0 us
  other arithmetic: 32.7 us -> 8 us
  local copies, waits for them, and re-layouts: 43.5 us -> 22.6 us
    all_gather x2 -> x0, blocking collectives: 28.1 us -> none  [prefix(): gathered = jax.tree.map(lambda a: lax.all_gather(a, axis), part)]
    dot_general x8 -> x3, matrix products: 35.9 us -> 16.4 us  [outer(): lax.dot_general(left, right, (((0,), (0,)), ((), ())), preferred_element_...]
    dot_general x8 -> x3, matrix products: 30.4 us -> 13.3 us  [back_product(): lax.dot_general(grads, weight, (((1,), (1,)), ((), ())), preferred_elemen...]
    reduce_sum x3 -> x0, other arithmetic: 14.5 us -> none  [the longest x1 5.84 us: gate_terms(): input_gate = jax.nn.sigmoid(input_pre + input_bias)]
    unnamed x127 -> x56, local copies, waits for them, and re-layouts: 16.7 us -> 8.14 us
    convert_element_type x8, local copies, waits for them, and re-layouts: 12.9 us -> 6.58 us  [joined(): block.transpose(1, 0, 2).reshape(depth, quarters * part).astype(jnp.float32)]
    pallas_call x3 -> x2, Pallas kernels: 251 us -> 246 us  [the longest x1 129 us: backward_all(): pl.pallas_call(functools.partial(backward_kernel, count), out_shape=out_s...]
  transfers between devices with their start and end apart: 1 -> 0, of which waited for: 0 -> 0; matrix products, arithmetic and copies ran while one was open for 11% -> 0% of each run, Pallas kernels for 21% -> 0%
where the time goes in v3:
time: 485 us; the launch traced here: 475 us
  Pallas kernels  400 us (82%)
  matrix products  43.4 us (9%)
  local copies, waits for them, and re-layouts  22.6 us (5%)
  other arithmetic  8 us (2%)
    pallas_call x1, Pallas kernels, forward_all(): pl.pallas_call(forward_kernel, out_shape=fulls + saved, in_specs=[ANY] *...  154 us
    pallas_call x1, Pallas kernels, backward_all(): pl.pallas_call(functools.partial(backward_kernel, count), out_shape=out_s...  129 us
    pallas_call x1, Pallas kernels, reduce_all(): pl.pallas_call(functools.partial(reduce_kernel, count), out_shape=tuple((...  118 us
    dot_general x3, matrix products, outer(): lax.dot_general(left, right, (((0,), (0,)), ((), ())), preferred_element_...  16.4 us
    dot_general x3, matrix products, forward_product(): return jnp.dot(values, weight, preferred_element_type=jnp.float32)  13.8 us
    dot_general x3, matrix products, back_product(): lax.dot_general(grads, weight, (((1,), (1,)), ((), ())), preferred_elemen...  13.3 us

profile of v3, /device:TPU:0, one launch (start us, length us, event | category | flops | bytes accessed | tf_op | source)
XLA Modules:
  0.0 475.4 jit_solution(12699658379840486770)
XLA Ops:
  5.9 153.8 %recurrent_forward.1 = (bf16[1024,1536]{1,0:T(8,128)(2,1)}, bf16[1536,1536]{1,0:T(8,128)(2,1)}, bf16[1536,1536]{1,0:T(8,128)(2,1)}, bf16[1024,1536]{1,0:T(8,128)...) custom-call(bf16[128,1536]{1,0:T(8,128)(2,1)} %refs_0_.1, ...), custom_call_target="tpu_custom_call" | custom-call | tf_op jit(solution)/shard_map/recurrent_forward/pallas_call | solution.py:434
  159.7 5.0 %fusion.16 = f32[384,3072]{1,0:T(8,128)S(1)} fusion(bf16[384,1024]{1,0:T(8,128)(2,1)} %get-tuple-element.55, bf16[1024,3072]{1,0:T(8,128)(2,1)} %get-tuple-element.56), kind=kOutput, calls=%fused_computation.56 | convolution fusion | flops 2415919104 | bytes 11796480 | tf_op jit(solution)/shard_map/dot_general | solution.py:1234
  164.8 2.7 fusion.17
  167.5 7.5 %fusion.7 = (bf16[384,3072]{1,0:T(8,128)(2,1)S(1)}, bf16[384,3072]{1,0:T(8,128)(2,1)}, bf16[384,3072]{1,0:T(8,128)(2,1)}) fusion(f32[384,3072]{1,0:T(8,128)S(1)} %fusion.16, f32[384,3072]{1,0:T(8,128)S(1)} %fusion.17, bf16[3072,1024]{1,0:T(8,128)(2,1)S(1)} %bitcast.113, bf16[384,1024]{1,0:T(8,128)(2,1)S(1)} %bitcast.99), kind=kOutput, calls=%fused_computation.14 | convolution fusion | flops 2446589952 | bytes 23592960 | tf_op jit(solution)/shard_map/dot_general | solution.py:1244
  175.0 6.1 %add_convert_fusion = bf16[384,1024]{1,0:T(8,128)(2,1)} fusion(f32[384,1024]{1,0:T(8,128)S(1)} %copy-done, bf16[384,3072]{1,0:T(8,128)(2,1)} %get-tuple-element.203, bf16[3072,1024]{1,0:T(8,128)(2,1)S(1)} %bitcast.113), kind=kOutput, calls=%fused_computation.25 | convolution fusion | flops 2416705536 | bytes 11010048 | tf_op jit(solution)/shard_map/dot_general | solution.py:1234
  181.1 5.6 %convolution_convert_fusion.2 = bf16[3072,1024]{1,0:T(8,128)(2,1)} fusion(bf16[384,3072]{1,0:T(8,128)(2,1)S(1)} %copy-done.20, bf16[384,1024]{1,0:T(8,128)(2,1)S(1)} %bitcast.100), kind=kOutput, calls=%fused_computation.4 | convolution fusion | flops 2419064832 | bytes 9437184 | tf_op jit(solution)/shard_map/dot_general | solution.py:1238
  186.7 5.4 %convolution_convert_fusion.1 = bf16[1024,3072]{1,0:T(8,128)(2,1)} fusion(bf16[384,1024]{1,0:T(8,128)(2,1)S(1)} %copy-done.16, bf16[384,3072]{1,0:T(8,128)(2,1)S(1)} %copy-done.19), kind=kOutput, calls=%fused_computation.3 | convolution fusion | flops 2419064832 | bytes 9437184 | tf_op jit(solution)/shard_map/dot_general | solution.py:1238
  192.2 5.4 %convolution_convert_fusion = bf16[1024,3072]{1,0:T(8,128)(2,1)} fusion(bf16[384,1024]{1,0:T(8,128)(2,1)S(1)} %copy-done.16, bf16[384,3072]{1,0:T(8,128)(2,1)S(1)} %get-tuple-element.201), kind=kOutput, calls=%fused_computation.2 | convolution fusion | flops 2419064832 | bytes 9437184 | tf_op jit(solution)/shard_map/dot_general | solution.py:1238
  197.8 2.7 fusion.18
  200.5 3.0 multiply_reduce_fusion
  203.5 1.9 fusion.13
  205.5 128.5 %recurrent_backward.1 = (bf16[4,384,256]{2,1,0:T(8,128)(2,1)}, bf16[4,128,768]{2,1,0:T(8,128)(2,1)}, bf16[4,128,768]{2,1,0:T(8,128)(2,1)}, bf16[1536,1024]{1,0:T...) custom-call(bf16[4,2,384,1024]{3,2,1,0:T(8,128)(2,1)} %bitcast.81, ...), custom_call_target="tpu_custom_call" | custom-call | tf_op jit(solution)/shard_map/recurrent_backward/pallas_call | solution.py:1141
  334.9 1.4 maximum_maximum_fusion.refs_5_
  336.3 117.6 %reduce_grads.1 = (bf16[4,192,256]{2,1,0:T(8,128)(2,1)}, bf16[4,192,384]{2,1,0:T(8,128)(2,1)}, bf16[4,192,384]{2,1,0:T(8,128)(2,1)}, bf16[4,128,384]{2,1,0:T(8,1...) custom-call(bf16[4,2,192,1024]{3,2,1,0:T(8,128)(2,1)} %bitcast.91, bf16[4,2,192,1536]{3,2,1,0:T(8,128)(2,1)} %bitcast.87, ...), custom_call_target="tpu_custom_call" | custom-call | tf_op jit(solution)/shard_map/reduce_grads/pallas_call | solution.py:767
  453.8 1.4 fusion.15
  455.3 1.2 convert_bitcast_fusion.6
  458.2 1.2 copy.166
  460.9 1.2 copy.171
  462.0 1.2 copy.172
  464.8 1.4 convert_bitcast_fusion.1
  466.3 1.9 copy.162
  468.2 1.6 copy.167
  470.2 1.6 copy.168
  472.5 1.6 copy.169
  (90 shorter events, 13.0 us)
Async XLA Ops:
  0.7 2.8 copy-start.12
  0.7 3.4 copy-start.13
  0.7 4.0 copy-start.14
  0.7 4.6 copy-start.10
  159.7 5.1 %copy-start.15 = (bf16[1024,3072]{1,0:T(8,128)(2,1)S(1)}, bf16[1024,3072]{1,0:T(8,128)(2,1)}, u32[]{:S(2)}) copy-start(bf16[1024,3072]{1,0:T(8,128)(2,1)} %get-tuple-element.57) | copy-start | bytes 18874372
  159.7 5.1 %copy-start.16 = (bf16[384,1024]{1,0:T(8,128)(2,1)S(1)}, bf16[384,1024]{1,0:T(8,128)(2,1)}, u32[]{:S(2)}) copy-start(bf16[384,1024]{1,0:T(8,128)(2,1)} %get-tuple-element.55) | copy-start | bytes 2359300
  159.7 7.8 %slice-start.2 = ((s8[6291456]{0:T(1024)(128)(4,1)}), s8[4194304]{0:T(1024)(128)(4,1)S(1)}, s32[]{:S(2)}) async-start(s8[6291456]{0:T(1024)(128)(4,1)} %bitcast.112), calls=%async_computation.2 | async-start | bytes 8388608
  164.8 2.7 copy-start.1
  164.8 2.7 slice-start.3
  167.5 7.5 %copy-start = (f32[384,1024]{1,0:T(8,128)S(1)}, f32[384,1024]{1,0:T(8,128)}, u32[]{:S(2)}) copy-start(f32[384,1024]{1,0:T(8,128)} %get-tuple-element.54) | copy-start | bytes 4718596
  175.0 17.1 %copy-start.17 = (bf16[384,3072]{1,0:T(8,128)(2,1)}, bf16[384,3072]{1,0:T(8,128)(2,1)S(1)}, u32[]{:S(2)}) copy-start(bf16[384,3072]{1,0:T(8,128)(2,1)S(1)} %get-tuple-element.201) | copy-start | bytes 7077892
  175.0 6.1 %copy-start.20 = (bf16[384,3072]{1,0:T(8,128)(2,1)S(1)}, bf16[384,3072]{1,0:T(8,128)(2,1)}, u32[]{:S(2)}) copy-start(bf16[384,3072]{1,0:T(8,128)(2,1)} %get-tuple-element.203) | copy-start | bytes 7077892
  181.1 5.6 %copy-start.19 = (bf16[384,3072]{1,0:T(8,128)(2,1)S(1)}, bf16[384,3072]{1,0:T(8,128)(2,1)}, u32[]{:S(2)}) copy-start(bf16[384,3072]{1,0:T(8,128)(2,1)} %get-tuple-element.202) | copy-start | bytes 7077892
  186.7 11.0 %slice-start = ((s8[6291456]{0:T(1024)(128)(4,1)}), s8[4194304]{0:T(1024)(128)(4,1)S(1)}, s32[]{:S(2)}) async-start(s8[6291456]{0:T(1024)(128)(4,1)} %bitcast.110), calls=%async_computation | async-start | bytes 8388608
  192.2 5.6 %slice-start.1 = ((s8[6291456]{0:T(1024)(128)(4,1)}), s8[2097152]{0:T(1024)(128)(4,1)S(1)}, s32[]{:S(2)}) async-start(s8[6291456]{0:T(1024)(128)(4,1)} %bitcast.110), calls=%async_computation.1 | async-start | bytes 4194304
  197.7 2.8 copy-start.11
  197.8 2.8 copy-start.18
  456.8 2.6 copy-start.9
  456.8 3.9 copy-start.6
  456.8 3.9 copy-start.7
  460.9 2.9 copy-start.8
  462.0 2.8 copy-start.2
  462.0 2.8 copy-start.3
  472.5 1.6 copy-start.4
  (1 other events, 1.6 us)

commit v4 on v3

--- a/solution.py
+++ b/solution.py
@@ -86,9 +86,10 @@
         return taken
 
     shards = take(8)
-    tokens, marks, gain1, conv_w, conv_b, rate_b, input_b, decay_scale, gain2 = take(9)
+    cotangent, tokens, marks, gain1, conv_w, conv_b, rate_b, input_b, decay_scale, gain2 = take(10)
     fulls = take(8)
-    outs = take(12)
+    outs = take(11)
+    pair_normed2, pair_cotangent = take(2)
     (w_rec, w_rate, w_input, w_branch, w_out) = weights = take(5)
     normed, padded, conv_out, conv_low, rate_pre, input_pre = take(6)
     products, states, branch_pre, mixed_in, resid, normed2 = take(6)
@@ -98,6 +99,8 @@
     r, s, z, c = place()
     mate, along_x, along_y, along_z = peers_of(r, s, z, c)
     across_x, across_y = along_x[0], along_y[0]
+    parity = lax.rem(z, 2)
+    twin = (r, s + 2 - 4 * parity)
     others = [(r, lax.rem(s + k, 8)) for k in range(1, 8)]
     greet(others + [along_x, along_y])
     live, pending = [], []
@@ -136,33 +139,55 @@
         copy.start()
         pending.append(copy)
 
+    def rows_of(m, source, core, begin, length):
+        depth = shards[m].shape[0]
+        block = lax.div(source, 2) * 2 + core if m == 7 else source * 2 + core
+        return pl.ds(pl.multiple_of(block * depth + begin, 16), length)
+
     def region(m, source, quarter, begin, length):
-        depth, width = shards[m].shape
-        part = width // 4
-        row = pl.multiple_of((source * 2 + c) * depth + begin, 16)
+        part = fulls[m].shape[1] // 4
         column = pl.multiple_of(quarter * part, 128)
-        return fulls[m].at[pl.ds(row, length), pl.ds(column, part)]
+        return fulls[m].at[rows_of(m, source, c, begin, length), pl.ds(column, part)]
+
+    def turns(m):
+        return (2,) if m == 7 else (1, 2, 3)
 
     stage_own, stage_z, stage_x, stage_y, stage_d, stage_c = {}, {}, {}, {}, {}, {}
 
     def begin(m):
         depth, width = shards[m].shape
-        part = width // 4
-        rows = pl.ds(pl.multiple_of(s * depth, 16), depth)
-        own = pltpu.make_async_copy(shards[m], fulls[m].at[rows], local.at[m])
-        own.start()
-        column = pl.multiple_of(r * part, 128)
-        stage_z[m] = [
-            remote(
-                m,
-                k,
-                shards[m].at[:, pl.ds(column, part)],
-                region(m, z, r, 0, depth),
-                along_z[k - 1],
+        part = fulls[m].shape[1] // 4
+        rows = rows_of(m, z, c, 0, depth)
+        stage_z[m] = []
+        for k in turns(m):
+            column = r * part
+            if m in (5, 6):
+                half = lax.rem(parity + k, 2)
+                column = (half + 2 * lax.div(r, 2)) * (2 * part) + lax.rem(r, 2) * part
+            stage_z[m].append(
+                remote(
+                    m,
+                    k,
+                    shards[m].at[:, pl.ds(pl.multiple_of(column, 128), part)],
+                    region(m, z, r, 0, depth),
+                    along_z[k - 1],
+                )
             )
-            for k in (1, 2, 3)
-        ]
-        stage_own[m] = (own, remote(m, 0, shards[m], fulls[m].at[rows], mate))
+        pieces = [(shards[m], fulls[m].at[rows])]
+        if m in (5, 6):
+            strip = 2 * part
+            pieces = [
+                (
+                    shards[m].at[:, pl.ds(pl.multiple_of((parity + 2 * i) * strip, 128), strip)],
+                    fulls[m].at[rows, pl.ds(i * strip, strip)],
+                )
+                for i in range(2)
+            ]
+        stage_own[m] = []
+        for i, (src, dst) in enumerate(pieces):
+            own = pltpu.make_async_copy(src, dst, local.at[m, i])
+            own.start()
+            stage_own[m].append((own, remote(m, 19 * i, src, dst, mate)))
 
     def sources(k):
         return lax.rem(z + 4 - k, 4)
@@ -172,8 +197,8 @@
         if m < count:
             depth = shards[m].shape[0]
             stage_x[m], stage_y[m] = [], []
-            for k in (1, 2, 3):
-                stage_z[m][k - 1].wait_recv()
+            for i, k in enumerate(turns(m)):
+                stage_z[m][i].wait_recv()
                 piece = region(m, sources(k), r, 0, depth)
                 stage_x[m].append(remote(m, 3 + k, piece, piece, along_x))
                 stage_y[m].append(remote(m, 6 + k, piece, piece, along_y))
@@ -184,30 +209,29 @@
             depth = shards[m].shape[0]
             half = depth // 2
             stage_d[m] = []
-            for k in (1, 2, 3):
-                stage_x[m][k - 1].wait_recv()
+            for i, k in enumerate(turns(m)):
+                stage_x[m][i].wait_recv()
                 piece = region(m, sources(k), across_x, 0, half)
                 stage_d[m].append(remote(m, 9 + k, piece, piece, along_y))
-                stage_y[m][k - 1].wait_recv()
+                stage_y[m][i].wait_recv()
                 piece = region(m, sources(k), across_y, half, half)
                 stage_d[m].append(remote(m, 12 + k, piece, piece, along_x))
         m = now - 2
         if 0 <= m < count:
             depth = shards[m].shape[0]
             stage_c[m] = []
-            for k in (1, 2, 3):
-                stage_d[m][2 * k - 2].wait_recv()
-                stage_d[m][2 * k - 1].wait_recv()
-                rows = pl.ds(pl.multiple_of((sources(k) * 2 + c) * depth, 16), depth)
-                piece = fulls[m].at[rows]
+            for i, k in enumerate(turns(m)):
+                stage_d[m][2 * i].wait_recv()
+                stage_d[m][2 * i + 1].wait_recv()
+                piece = fulls[m].at[rows_of(m, sources(k), c, 0, depth)]
                 stage_c[m].append(remote(m, 15 + k, piece, piece, mate))
 
     loads = {}
 
     def arrive(m):
-        own, twin = stage_own[m]
-        own.wait()
-        twin.wait_recv()
+        for own, swapped in stage_own[m]:
+            own.wait()
+            swapped.wait_recv()
         for copy in stage_c[m]:
             copy.wait_recv()
         if m < 5:
@@ -372,8 +396,12 @@
             normed2[rows, :] = (values * scale * gain2[...]).astype(jnp.bfloat16)
 
         loop(12, one)
-        save(11, normed2, outs[11])
-
+        save(11, normed2, pair_normed2.at[pl.ds(0, tok)])
+        return near(8, normed2, pair_normed2.at[pl.ds(tok, tok)], twin)
+
+    tok = tokens.shape[0]
+    cotangent_copy = near(9, cotangent, pair_cotangent.at[pl.ds(tok, tok)], twin)
+    save(12, cotangent, pair_cotangent.at[pl.ds(0, tok)])
     carry_in[...] = jnp.zeros_like(carry_in)
     ends[...] = jnp.zeros_like(ends)
     begin(0)
@@ -400,18 +428,20 @@
     mix()
     arrive(4)
     tick(7)
-    out_product()
+    normed2_copy = out_product()
     tick(8)
     tick(9)
     for m in (5, 6, 7):
         arrive(m)
+    cotangent_copy.wait_recv()
+    normed2_copy.wait_recv()
     for copy in live:
         copy.wait_send()
     for copy in pending:
         copy.wait()
 
 
-def forward_all(shards, tokens, marks, vectors):
+def forward_all(shards, cotangent, tokens, marks, vectors):
     low, full = jnp.bfloat16, jnp.float32
     tok, model = tokens.shape
     rec = shards[0].shape[1]
@@ -428,14 +458,19 @@
         shape((tok, rec), low),
         shape((tok, model), full),
         shape((8, rec), full),
-        shape((tok, model), low),
-    )
-    fulls = tuple(shape((a.shape[0] * 8, a.shape[1]), low) for a in shards)
+        shape((2 * tok, model), low),
+        shape((2 * tok, model), low),
+    )
+    fulls = [shape((a.shape[0] * 8, a.shape[1]), low) for a in shards]
+    for m in (5, 6):
+        fulls[m] = shape((fulls[m].shape[0], fulls[m].shape[1] // 2), low)
+    fulls[7] = shape((fulls[7].shape[0] // 2, fulls[7].shape[1]), low)
+    fulls = tuple(fulls)
     results = pl.pallas_call(
         forward_kernel,
         out_shape=fulls + saved,
-        in_specs=[ANY] * 8 + [VMEM] * 9,
-        out_specs=(ANY,) * 20,
+        in_specs=[ANY] * 9 + [VMEM] * 9,
+        out_specs=(ANY,) * 21,
         scratch_shapes=[pltpu.VMEM(a.shape, low) for a in fulls[:5]]
         + [
             pltpu.VMEM((tok, model), low),
@@ -454,23 +489,24 @@
             pltpu.VMEM((8, rec), full),
             pltpu.VMEM((8, 8, rec), full),
             pltpu.VMEM((8, rec), full),
-            pltpu.SemaphoreType.DMA((8, 19)),
-            pltpu.SemaphoreType.DMA((8, 19)),
-            pltpu.SemaphoreType.DMA((8,)),
-            pltpu.SemaphoreType.DMA((8,)),
-            pltpu.SemaphoreType.DMA((8,)),
+            pltpu.SemaphoreType.DMA((8, 20)),
+            pltpu.SemaphoreType.DMA((8, 20)),
+            pltpu.SemaphoreType.DMA((8, 2)),
+            pltpu.SemaphoreType.DMA((10,)),
+            pltpu.SemaphoreType.DMA((10,)),
             pltpu.SemaphoreType.DMA((5,)),
-            pltpu.SemaphoreType.DMA((12,)),
+            pltpu.SemaphoreType.DMA((13,)),
         ],
         compiler_params=pltpu.CompilerParams(
             collective_id=0, has_side_effects=True, vmem_limit_bytes=60 * 1024 * 1024
         ),
         name="recurrent_forward",
-    )(*shards, tokens, marks, *vectors)
+    )(*shards, cotangent, tokens, marks, *vectors)
     return results[:8], results[8:]
 
 class Reduction:
-    def __init__(self, grads, outs, scratch, sems):
+    def __init__(self, kinds, grads, outs, scratch, sems):
+        self.kinds = kinds
         self.grads, self.outs = grads, outs
         self.count = len(grads)
         self.held, self.own, self.first, self.second, self.third, self.final = scratch
@@ -536,7 +572,7 @@
             def add(b):
                 held[q, b] = held[q, b] + own[q % 2, b]
 
-            loop(4, add)
+            loop(held.shape[1], add)
             if q < 2:
                 near.append(self.load(m, q + 2))
         self.at_one[m] = []
@@ -564,18 +600,18 @@
 
     def stage_one(self, m):
         held, first = self.held[m], self.first[m]
-        half = held.shape[2] // 2
+        count, half = held.shape[1], held.shape[2] // 2
         for copy in self.at_one[m]:
             copy.wait_recv()
 
         def add(i):
-            other, b = lax.div(i, 4), lax.rem(i, 4)
+            other, b = lax.div(i, count), lax.rem(i, count)
             qx = other * 2 + self.rx
             held[qx, b, :half] = held[qx, b, :half] + first[0, other, b]
             qy = self.ry * 2 + other
             held[qy, b, half:] = held[qy, b, half:] + first[1, other, b]
 
-        loop(8, add)
+        loop(2 * count, add)
         self.at_two[m] = [
             self.remote(
                 m,
@@ -603,32 +639,45 @@
             held[r, b, :half] = held[r, b, :half] + second[0, b]
             held[r, b, half:] = held[r, b, half:] + second[1, b]
 
-        loop(4, add)
-        self.at_z[m] = [
-            self.remote(
-                m,
-                9 + k,
-                held.at[r, lax.rem(self.z + k, 4)],
-                self.third[m].at[k - 1],
-                self.along_z[k - 1],
+        loop(held.shape[1], add)
+        rows = self.kinds[m] == "rows"
+        self.at_z[m] = []
+        for k in (2,) if rows else (1, 2, 3):
+            target = 1 - lax.div(self.z, 2) if rows else lax.rem(self.z + k, 4)
+            self.at_z[m].append(
+                self.remote(
+                    m,
+                    9 + k,
+                    held.at[r, target],
+                    self.third[m].at[0 if rows else k - 1],
+                    self.along_z[k - 1],
+                )
             )
-            for k in (1, 2, 3)
-        ]
 
     def stage_z(self, m):
         held, third, final, r = self.held[m], self.third[m], self.final[m], self.r
         for copy in self.at_z[m]:
             copy.wait_recv()
-        depth = held.shape[2]
+        kind, parity = self.kinds[m], lax.rem(self.z, 2)
+        own = lax.div(self.z, 2) if kind == "rows" else self.z
 
         def add(i):
             rows = at(i, 32)
-            mine = held[r, self.z, rows, :].astype(jnp.float32)
-            for k in range(3):
-                mine = mine + third[k, rows, :].astype(jnp.float32)
-            final[r, rows, :] = mine.astype(jnp.bfloat16)
-
-        loop(depth // 32, add)
+
+            def total(first, *terms):
+                values = first.astype(jnp.float32)
+                for k in terms:
+                    values = values + third[k, rows, :].astype(jnp.float32)
+                return values.astype(jnp.bfloat16)
+
+            mine = held[r, own, rows, :]
+            if kind == "columns":
+                final[r, parity, rows, :] = total(mine, 1)
+                final[r, 1 - parity, rows, :] = total(third[0, rows, :], 2)
+            else:
+                final[r, rows, :] = total(mine, *((0,) if kind == "rows" else (0, 1, 2)))
+
+        loop(held.shape[2] // 32, add)
         self.at_end[m] = [
             self.remote(m, 13 + i, final.at[r], final.at[r], device)
             for i, device in enumerate((self.along_x, self.along_y, self.diagonal))
@@ -662,15 +711,16 @@
 REDUCTION_SEMS = 16
 
 
-def reduction_memory(shapes):
+def reduction_memory(kinds, grads):
     low = jnp.bfloat16
-    count = len(shapes)
-    scratch = [pltpu.VMEM((4, 4, k, n), low) for k, n in shapes]
-    scratch += [pltpu.VMEM((2, 4, k, n), low) for k, n in shapes]
-    scratch += [pltpu.VMEM((2, 2, 4, k // 2, n), low) for k, n in shapes]
-    scratch += [pltpu.VMEM((2, 4, k // 2, n), low) for k, n in shapes]
-    scratch += [pltpu.VMEM((3, k, n), low) for k, n in shapes]
-    scratch += [pltpu.VMEM((4, k, n), low) for k, n in shapes]
+    count = len(grads)
+    shapes = [(2 if kind == "rows" else 4,) + quarter_shape(kind, g) for kind, g in zip(kinds, grads)]
+    scratch = [pltpu.VMEM((4, zs, k, n), low) for zs, k, n in shapes]
+    scratch += [pltpu.VMEM((2, zs, k, n), low) for zs, k, n in shapes]
+    scratch += [pltpu.VMEM((2, 2, zs, k // 2, n), low) for zs, k, n in shapes]
+    scratch += [pltpu.VMEM((2, zs, k // 2, n), low) for zs, k, n in shapes]
+    scratch += [pltpu.VMEM((zs - 1, k, n), low) for zs, k, n in shapes]
+    scratch += [pltpu.VMEM(a.shape, low) for a in reduced_shapes(kinds, grads)]
     return scratch + [
         pltpu.SemaphoreType.DMA((count, REDUCTION_SEMS)),
         pltpu.SemaphoreType.DMA((count, REDUCTION_SEMS)),
@@ -678,6 +728,14 @@
     ]
 
 
+def reduced_shapes(kinds, grads):
+    shapes = [(kind, quarter_shape(kind, g)) for kind, g in zip(kinds, grads)]
+    return tuple(
+        jax.ShapeDtypeStruct((4, 2, k, n) if kind == "columns" else (4, k, n), jnp.bfloat16)
+        for kind, (k, n) in shapes
+    )
+
+
 def take_reduction(take, count):
     scratch = [take(count) for _ in range(6)]
     return scratch, take(3)
@@ -693,17 +751,37 @@
     return take
 
 
-def split_rows(grad):
-    return grad.reshape(4, 2, grad.shape[0] // 8, grad.shape[1])
-
-
-def quarter_shape(grad):
-    return grad.shape[0] // 8, grad.shape[1] // 4
-
-
-def joined(block):
-    quarters, depth, part = block.shape
-    return block.transpose(1, 0, 2).reshape(depth, quarters * part).astype(jnp.float32)
+def split_rows(kind, grad):
+    zs = 2 if kind == "rows" else 4
+    return grad.reshape(zs, 2, grad.shape[0] // (2 * zs), grad.shape[1])
+
+
+def quarter_shape(kind, grad):
+    return grad.shape[0] // (4 if kind == "rows" else 8), grad.shape[1] // 4
+
+
+def finish_kernel(count, *refs):
+    for block, whole in zip(refs[:count], refs[count:]):
+        part = block.shape[-1]
+        for q in range(4):
+            if len(block.shape) == 4:
+                for half in range(2):
+                    column = ((half + 2 * (q // 2)) * 2 + q % 2) * part
+                    whole[:, column : column + part] = block[q, half].astype(jnp.float32)
+            else:
+                whole[:, q * part : (q + 1) * part] = block[q].astype(jnp.float32)
+
+
+def finish(blocks):
+    shapes = [(b.shape[-2], b.size // b.shape[-2]) for b in blocks]
+    return pl.pallas_call(
+        functools.partial(finish_kernel, len(blocks)),
+        out_shape=tuple(jax.ShapeDtypeStruct(a, jnp.float32) for a in shapes),
+        in_specs=[VMEM] * len(blocks),
+        out_specs=(VMEM,) * len(blocks),
+        compiler_params=pltpu.CompilerParams(vmem_limit_bytes=40 * 1024 * 1024),
+        name="widen_gradients",
+    )(*blocks)
 
 
 def reduce_kernel(count, *refs):
@@ -712,7 +790,7 @@
     (small_in,) = take(1)
     outs = take(count)
     (small_out,) = take(1)
-    reduction = Reduction(grads, outs, *take_reduction(take, count))
+    reduction = Reduction(("all",) * count, grads, outs, *take_reduction(take, count))
     small_held, small_got, small_send, small_recv = take(4)
     z = reduction.z
     greet(reduction.peers())
@@ -763,14 +841,14 @@
 
 def reduce_all(grads, small, tag):
     count = len(grads)
-    shapes = [quarter_shape(g) for g in grads]
+    kinds = ("all",) * count
     results = pl.pallas_call(
         functools.partial(reduce_kernel, count),
-        out_shape=tuple(jax.ShapeDtypeStruct((4, k, n), jnp.bfloat16) for k, n in shapes)
+        out_shape=reduced_shapes(kinds, grads)
         + (jax.ShapeDtypeStruct(small.shape, small.dtype),),
         in_specs=[ANY] * count + [VMEM],
         out_specs=(ANY,) * count + (VMEM,),
-        scratch_shapes=reduction_memory(shapes)
+        scratch_shapes=reduction_memory(kinds, grads)
         + [
             pltpu.VMEM((4,) + small.shape, small.dtype),
             pltpu.VMEM((7,) + small.shape, small.dtype),
@@ -781,27 +859,32 @@
             collective_id=tag, has_side_effects=True, vmem_limit_bytes=60 * 1024 * 1024
         ),
         name="reduce_grads",
-    )(*[split_rows(g) for g in grads], small)
-    return [joined(b) for b in results[:count]], results[count]
-
-
-def backward_kernel(count, *refs):
+    )(*[split_rows("all", g) for g in grads], small)
+    return results[:count], results[count]
+
+
+def backward_kernel(kinds, *refs):
     take = taker(refs)
+    count = len(kinds)
     grads = take(count)
+    part_mixed, part_normed2 = take(2)
     full_out, full_rate, full_input, full_branch, full_rec = take(5)
     saved_states, saved_branch, saved_rate, saved_input, saved_conv, saved_rec = take(6)
-    resid_low, marks, tokens, grad_resid, normed, conv_low, mixed_in, carried = take(8)
-    conv_w, rate_b, input_b, decay_scale, gain1 = take(5)
+    marks, tokens, cotangent, resid, normed, conv_low, mixed_in, carried = take(8)
+    conv_w, rate_b, input_b, decay_scale, gain1, gain2 = take(6)
     outs = take(count)
-    d_out, d_rate, d_input, d_branch, d_rec, token_grad = take(6)
-    small, small_norm = take(2)
-    reduction = Reduction(grads, outs, *take_reduction(take, count))
+    d_out, d_rate, d_input, d_branch, d_rec, token_grad, mixed = take(7)
+    small, small_norm, small_norm2 = take(3)
+    reduction = Reduction(kinds, grads, outs, *take_reduction(take, count))
     ring, past, branch_pre, rate_pre, input_pre, conv_out = take(6)
     flow, grads_conv, branch_low, rate_low, input_low, stage = take(6)
     rim, ends, got, carry = take(4)
+    own_parts, twin_parts, grad_resid, resid_low = take(4)
     near_send, near_recv, load_sem, ring_sem, stage_sem = take(5)
     r, s, z, c = place()
     others = [(r, lax.rem(s + k, 8)) for k in range(1, 8)]
+    parity = lax.rem(z, 2)
+    twin = (r, s + 2 - 4 * parity)
     greet(others + [reduction.along_x, reduction.along_y, reduction.diagonal])
     live = []
 
@@ -1029,6 +1112,36 @@
 
         loop(3, one)
 
+    def second_norm_back():
+        def one(i, total):
+            rows = at(i, 16)
+            grad = own_parts[1, rows, :].astype(jnp.float32) + twin_parts[1, rows, :].astype(
+                jnp.float32
+            )
+            values = resid[rows, :]
+            scale = lax.rsqrt(jnp.mean(values * values, axis=-1, keepdims=True) + epsilon)
+            back = grad * gain2[...]
+            mean = jnp.mean(values * back, axis=-1, keepdims=True)
+            result = cotangent[rows, :].astype(jnp.float32) + scale * back
+            result = result - values * (scale * scale * scale * mean)
+            grad_resid[rows, :] = result
+            resid_low[rows, :] = result.astype(jnp.bfloat16)
+            part = grad * values * scale
+            return total + part[0:8] + part[8:16]
+
+        total = lax.fori_loop(0, 24, one, jnp.zeros((8, 1024), jnp.float32))
+        small_norm2[...] = jnp.sum(total, axis=0, keepdims=True)
+
+    def mix_back():
+        def one(i):
+            rows = at(i, 16)
+            total = own_parts[0, rows, :].astype(jnp.float32)
+            total = total + twin_parts[0, rows, :].astype(jnp.float32)
+            own_parts[0, rows, :] = (resid[rows, :] + total).astype(jnp.bfloat16)
+
+        loop(24, one)
+        return bring(8, own_parts.at[0], mixed)
+
     def norm_back():
         def one(i, total):
             rows = at(i, 16)
@@ -1052,8 +1165,15 @@
         copy.start()
         staged[0] = copy
 
+    tok = tokens.shape[0]
+    normed2_copy = near(8, part_normed2.at[pl.ds(tok, tok)], twin_parts.at[1], twin)
     reduction.begin(0)
     reduction.begin(1)
+    mixed_copy = near(9, part_mixed.at[pl.ds(tok, tok)], twin_parts.at[0], twin)
+    part_loads = [
+        bring(6, part_normed2.at[pl.ds(0, tok)], own_parts.at[1]),
+        bring(7, part_mixed.at[pl.ds(0, tok)], own_parts.at[0]),
+    ]
     loads = [
         bring(0, saved_branch, branch_pre),
         bring(1, saved_states, past.at[:, pl.ds(8, 128), :]),
@@ -1066,10 +1186,13 @@
     ends[...] = jnp.zeros_like(ends)
     for row in range(3):
         past[row, 0:8, :] = jnp.broadcast_to(carried[row : row + 1, :], (8, past.shape[2]))
+    reduction.tick(0)
+    part_loads[0].wait()
+    normed2_copy.wait_recv()
+    second_norm_back()
     for i in range(3):
         flow[:, pl.ds(i * 512, 512)] = back_tile(i, resid_low, 1024)
         fetch(i + 3)
-    reduction.tick(0)
     loads[0].wait()
     loads[1].wait()
     branch_back()
@@ -1112,8 +1235,12 @@
     reduction.tick(4)
     outer_product(normed, branch_low, d_branch)
     norm_back()
+    part_loads[1].wait()
+    mixed_copy.wait_recv()
+    mixed_save = mix_back()
     for now in range(5, reduction.ticks()):
         reduction.tick(now)
+    mixed_save.wait()
     for copy in staged:
         copy.wait()
     for copy in live:
@@ -1121,29 +1248,31 @@
     reduction.close()
 
 
-def backward_all(grads, fulls, saved, local, vectors):
+def backward_all(grads, parts, fulls, saved, local, vectors):
     low, full = jnp.bfloat16, jnp.float32
     shape, memory = jax.ShapeDtypeStruct, pltpu.VMEM
-    shapes = [quarter_shape(g) for g in grads]
+    kinds = ("rows", "columns", "columns")
     count = len(grads)
-    tok, model = local[0].shape
+    tok, model = local[1].shape
     rec = fulls[0].shape[0]
-    out_shape = tuple(shape((4, k, n), low) for k, n in shapes) + (
+    out_shape = reduced_shapes(kinds, grads) + (
         shape((rec, model), low),
         shape((rec, rec), low),
         shape((rec, rec), low),
         shape((model, rec), low),
         shape((model, rec), low),
         shape((tok, model), low),
+        shape((tok, model), low),
         shape((8, rec), full),
         shape((1, model), full),
+        shape((1, model), full),
     )
     results = pl.pallas_call(
-        functools.partial(backward_kernel, count),
+        functools.partial(backward_kernel, kinds),
         out_shape=out_shape,
-        in_specs=[ANY] * (count + 11) + [VMEM] * 13,
-        out_specs=(ANY,) * (count + 6) + (VMEM,) * 2,
-        scratch_shapes=reduction_memory(shapes)
+        in_specs=[ANY] * (count + 13) + [VMEM] * 14,
+        out_specs=(ANY,) * (count + 7) + (VMEM,) * 3,
+        scratch_shapes=reduction_memory(kinds, grads)
         + [
             memory((3, 512, rec), low),
             memory((3, 136, rec), full),
@@ -1161,9 +1290,13 @@
             memory((8, rec), full),
             memory((8, 8, rec), full),
             memory((8, rec), full),
-            pltpu.SemaphoreType.DMA((8,)),
-            pltpu.SemaphoreType.DMA((8,)),
-            pltpu.SemaphoreType.DMA((6,)),
+            memory((2, tok, model), low),
+            memory((2, tok, model), low),
+            memory((tok, model), full),
+            memory((tok, model), low),
+            pltpu.SemaphoreType.DMA((10,)),
+            pltpu.SemaphoreType.DMA((10,)),
+            pltpu.SemaphoreType.DMA((9,)),
             pltpu.SemaphoreType.DMA((3,)),
             pltpu.SemaphoreType.DMA((2,)),
         ],
@@ -1171,8 +1304,8 @@
             collective_id=1, has_side_effects=True, vmem_limit_bytes=62 * 1024 * 1024
         ),
         name="recurrent_backward",
-    )(*[split_rows(g) for g in grads], *fulls, *saved, *local, *vectors)
-    return [joined(b) for b in results[:count]], results[count:]
+    )(*[split_rows(k, g) for k, g in zip(kinds, grads)], *parts, *fulls, *saved, *local, *vectors)
+    return results[:count], results[count:]
 
 
 def from_behind(block, axis, distance):
@@ -1477,6 +1610,7 @@
     decay_scale = (-8.0 * jax.nn.softplus(decay_param))[None]
     fulls, saved = forward_all(
         (w_rec, w_rate, w_input, w_branch, w_out, w_gate, w_up, w_down),
+        cotangent.reshape(-1, model_width),
         flat_tokens,
         marks,
         (
@@ -1489,32 +1623,30 @@
             norm2_gain[None],
         ),
     )
-    full_rec, full_rate, full_input, full_branch, full_out, full_gate, full_up, full_down = fulls
+    full_rec, full_rate, full_input, full_branch, full_out, half_gate, half_up, half_down = fulls
     normed, padded, conv_out, conv_low, rate_pre, input_pre = saved[:6]
-    states, branch_pre, mixed_in, resid, carried, normed2 = saved[6:]
-    gate_pre = forward_product(normed2, full_gate)
-    up_pre = forward_product(normed2, full_up)
+    states, branch_pre, mixed_in, resid, carried, pair_normed2, pair_cotangent = saved[6:]
+    gate_pre = forward_product(pair_normed2, half_gate)
+    up_pre = forward_product(pair_normed2, half_up)
     hidden = (jax.nn.gelu(gate_pre, approximate=True) * up_pre).astype(jnp.bfloat16)
-    mixed = (resid + forward_product(hidden, full_down)).astype(jnp.bfloat16).reshape(tokens.shape)
-    cot_low = cotangent.reshape(-1, model_width)
-    grad_down = outer(hidden, cot_low)
-    grad_hidden = back_product(cot_low, full_down)
+    part_mixed = forward_product(hidden, half_down).astype(jnp.bfloat16)
+    grad_down = outer(hidden, pair_cotangent)
+    grad_hidden = back_product(pair_cotangent, half_down)
     _, pull_mlp = jax.vjp(
         lambda gate_arg, up_arg: jax.nn.gelu(gate_arg, approximate=True) * up_arg, gate_pre, up_pre
     )
     grad_gate_pre, grad_up_pre = pull_mlp(grad_hidden)
     gate_low = grad_gate_pre.astype(jnp.bfloat16)
     up_low = grad_up_pre.astype(jnp.bfloat16)
-    grad_gate = outer(normed2, gate_low)
-    grad_up = outer(normed2, up_low)
-    grad_normed2 = back_product(gate_low, full_gate) + back_product(up_low, full_up)
-    _, pull_norm2 = jax.vjp(rms_norm, resid, norm2_gain)
-    grad_resid_norm, grad_norm2 = pull_norm2(grad_normed2)
-    grad_resid = cot_low.astype(jnp.float32) + grad_resid_norm
-    resid_low = grad_resid.astype(jnp.bfloat16)
+    grad_gate = outer(pair_normed2, gate_low)
+    grad_up = outer(pair_normed2, up_low)
+    part_normed2 = (back_product(gate_low, half_gate) + back_product(up_low, half_up)).astype(
+        jnp.bfloat16
+    )
     low = jnp.bfloat16
     ff, rest = backward_all(
         [g.astype(low) for g in (grad_down, grad_gate, grad_up)],
+        (part_mixed, part_normed2),
         (full_out, full_rate, full_input, full_branch, full_rec),
         (
             states.reshape(row_count, tok_count, rec_width),
@@ -1524,22 +1656,33 @@
             conv_out,
             padded,
         ),
-        (resid_low, marks, flat_tokens, grad_resid, normed, conv_low, mixed_in, carried),
-        (conv_weight, rate_bias[None], input_bias[None], decay_scale, norm1_gain[None]),
-    )
-    rec_grads, (token_grad, sums, grad_norm1) = rest[:5], rest[5:]
+        (
+            marks,
+            flat_tokens,
+            cotangent.reshape(-1, model_width),
+            resid,
+            normed,
+            conv_low,
+            mixed_in,
+            carried,
+        ),
+        (conv_weight, rate_bias[None], input_bias[None], decay_scale, norm1_gain[None], norm2_gain[None]),
+    )
+    rec_grads, (token_grad, mixed, sums, grad_norm1, grad_norm2) = rest[:5], rest[5:]
     small = jnp.concatenate(
         [
             sums.reshape(-1, model_width),
             grad_norm1,
-            grad_norm2[None],
+            grad_norm2,
             jnp.zeros((2, model_width), jnp.float32),
         ]
     )
     rec, small = reduce_all(rec_grads, small, 2)
+    blocks = finish(tuple(rec) + tuple(ff))
+    rec, ff = blocks[:5], blocks[5:]
     sums = small[:12].reshape(8, rec_width)
     return (
-        mixed,
+        mixed.reshape(tokens.shape),
         token_grad.reshape(tokens.shape),
         small[12],
         rec[3],

time: 485 us -> 442 us (0.911); the launches traced: 475 us -> 441 us
  Pallas kernels: 400 us -> 383 us
  local copies, waits for them, and re-layouts: 22.6 us -> 16 us
  matrix products: 43.4 us -> 37.2 us
    pallas_call x2 -> x3, Pallas kernels: 246 us -> 229 us  [the longest x1 117 us: reduce_all(): pl.pallas_call(functools.partial(reduce_kernel, count), out_shape=reduced...]
    convert_element_type x8 -> x0, local copies, waits for them, and re-layouts: 6.58 us -> none  [joined(): block.transpose(1, 0, 2).reshape(depth, quarters * part).astype(jnp.float32)]
where the time goes in v4:
time: 442 us; the launch traced here: 441 us
  Pallas kernels  383 us (87%)
  matrix products  37.2 us (8%)
  local copies, waits for them, and re-layouts  16 us (4%)
    pallas_call x1, Pallas kernels, forward_all(): pl.pallas_call(forward_kernel, out_shape=fulls + saved, in_specs=[ANY] *...  154 us
    pallas_call x1, Pallas kernels, reduce_all(): pl.pallas_call(functools.partial(reduce_kernel, count), out_shape=reduced...  117 us
    pallas_call x1, Pallas kernels, backward_all(): pl.pallas_call(functools.partial(backward_kernel, kinds), out_shape=out_s...  108 us
    dot_general x3, matrix products, back_product(): lax.dot_general(grads, weight, (((1,), (1,)), ((), ())), preferred_elemen...  13.4 us
    dot_general x3, matrix products, outer(): lax.dot_general(left, right, (((0,), (0,)), ((), ())), preferred_element_...  12.5 us
    dot_general x3, matrix products, forward_product(): return jnp.dot(values, weight, preferred_element_type=jnp.float32)  11.4 us

profile of v4, /device:TPU:0, one launch (start us, length us, event | category | flops | bytes accessed | tf_op | source)
XLA Modules:
  0.0 440.9 jit_solution(18169760714322922471)
XLA Ops:
  2.3 1.1 stack.23.refs_10_.refs_16_
  4.7 1.3 broadcast_in_dim.30.refs_14_.refs_25_
  6.0 1.3 broadcast_in_dim.31.refs_15_.refs_26_
  7.3 1.3 broadcast_in_dim.29.refs_13_
  8.6 154.0 %recurrent_forward.1 = (bf16[1024,1536]{1,0:T(8,128)(2,1)}, bf16[1536,1536]{1,0:T(8,128)(2,1)}, bf16[1536,1536]{1,0:T(8,128)(2,1)}, bf16[1024,1536]{1,0:T(8,128)...) custom-call(bf16[128,1536]{1,0:T(8,128)(2,1)} %refs_0_.1, ...), custom_call_target="tpu_custom_call" | custom-call | tf_op jit(solution)/shard_map/recurrent_forward/pallas_call | solution.py:469
  162.7 5.1 %fusion.12 = f32[768,1536]{1,0:T(8,128)S(1)} fusion(bf16[768,1024]{1,0:T(8,128)(2,1)} %get-tuple-element.65, bf16[1024,1536]{1,0:T(8,128)(2,1)} %get-tuple-element.67), kind=kOutput, calls=%fused_computation.38 | convolution fusion | flops 2415919104 | bytes 9437184 | tf_op jit(solution)/shard_map/dot_general | solution.py:1367
  167.8 2.6 fusion.11
  170.4 7.0 %multiply_convert_fusion = (bf16[768,1536]{1,0:T(8,128)(2,1)S(1)}, bf16[768,1536]{1,0:T(8,128)(2,1)S(1)}, bf16[768,1536]{1,0:T(8,128)(2,1)S(1)}) fusion(f32[768,1536]{1,0:T(8,128)S(1)} %fusion.11, f32[768,1536]{1,0:T(8,128)S(1)} %fusion.12, bf16[768,1024]{1,0:T(8,128)(2,1)S(1)} %copy-done.15, bf16[1536,1024]{1,0:T(8,128)(2,1)S(1)} %copy-done.12), kind=kOutput, calls=%fused_computation.9 | convolution fusion | flops 2446589952 | bytes 21233664 | tf_op jit(solution)/shard_map/dot_general | solution.py:1377
  177.5 2.6 fusion.13
  180.1 3.7 add_convert_fusion.refs_4_
  183.9 3.7 convolution_convert_fusion.3.refs_3_
  187.5 4.2 convolution_convert_fusion
  191.7 4.3 convolution_convert_fusion.1
  196.0 4.0 convolution_convert_fusion.2
  200.0 108.2 %recurrent_backward.1 = (bf16[4,384,256]{2,1,0:T(8,128)(2,1)}, bf16[4,2,128,384]{3,2,1,0:T(8,128)(2,1)}, bf16[4,2,128,384]{3,2,1,0:T(8,128)(2,1)}, bf16[1536,102...) custom-call(bf16[2,2,384,1024]{3,2,1,0:T(8,128)(2,1)} %bitcast.51, ...), custom_call_target="tpu_custom_call" | custom-call | tf_op jit(solution)/shard_map/recurrent_backward/pallas_call | solution.py:1270
  309.1 1.4 maximum_maximum_fusion.refs_5_
  310.5 117.1 %reduce_grads.1 = (bf16[4,192,256]{2,1,0:T(8,128)(2,1)}, bf16[4,192,384]{2,1,0:T(8,128)(2,1)}, bf16[4,192,384]{2,1,0:T(8,128)(2,1)}, bf16[4,128,384]{2,1,0:T(8,1...) custom-call(bf16[4,2,192,1024]{3,2,1,0:T(8,128)(2,1)} %bitcast.46, bf16[4,2,192,1536]{3,2,1,0:T(8,128)(2,1)} %bitcast.44, ...), custom_call_target="tpu_custom_call" | custom-call | tf_op jit(solution)/shard_map/reduce_grads/pallas_call | solution.py:845
  427.6 1.1 copy-done.3
  428.7 1.1 copy-done.4
  429.7 1.0 copy-done.5
  430.7 1.0 copy-done.6
  431.7 1.0 copy-done.7
  432.7 3.9 widen_gradients.1
  439.2 0.9 copy.87
  (52 shorter events, 7.2 us)
Async XLA Ops:
  162.6 5.1 %copy-start.14 = (bf16[1024,1536]{1,0:T(8,128)(2,1)S(1)}, bf16[1024,1536]{1,0:T(8,128)(2,1)}, u32[]{:S(2)}) copy-start(bf16[1024,1536]{1,0:T(8,128)(2,1)} %get-tuple-element.66) | copy-start | bytes 9437188
  162.6 5.1 %copy-start.16 = (bf16[768,1024]{1,0:T(8,128)(2,1)S(1)}, bf16[768,1024]{1,0:T(8,128)(2,1)}, u32[]{:S(2)}) copy-start(bf16[768,1024]{1,0:T(8,128)(2,1)} %get-tuple-element.65) | copy-start | bytes 4718596
  167.8 2.6 copy-start.12
  167.8 2.6 copy-start.15
  177.5 2.6 copy-start.13
  310.5 117.1 %copy-start = (bf16[4,384,256]{2,1,0:T(8,128)(2,1)S(1)}, bf16[4,384,256]{2,1,0:T(8,128)(2,1)}, u32[]{:S(2)}) copy-start(bf16[4,384,256]{2,1,0:T(8,128)(2,1)} %get-tuple-element.102.refs_5_) | copy-start | bytes 2359300
  310.5 117.1 %copy-start.1 = (bf16[4,2,128,384]{3,2,1,0:T(8,128)(2,1)S(1)}, bf16[4,2,128,384]{3,2,1,0:T(8,128)(2,1)}, u32[]{:S(2)}) copy-start(bf16[4,2,128,384]{3,2,1,0:T(8,128)(2,1)} %get-tuple-element.103.refs_6_) | copy-start | bytes 2359300
  310.5 117.1 %copy-start.2 = (bf16[4,2,128,384]{3,2,1,0:T(8,128)(2,1)S(1)}, bf16[4,2,128,384]{3,2,1,0:T(8,128)(2,1)}, u32[]{:S(2)}) copy-start(bf16[4,2,128,384]{3,2,1,0:T(8,128)(2,1)} %get-tuple-element.104.refs_7_) | copy-start | bytes 2359300
  310.5 128.7 %copy-start.9 = (bf16[384,1024]{1,0:T(8,128)(2,1)S(1)}, bf16[384,1024]{1,0:T(8,128)(2,1)}, u32[]{:S(2)}) copy-start(bf16[384,1024]{1,0:T(8,128)(2,1)} %get-tuple-element.86) | copy-start | bytes 2359300
  427.6 9.8 %copy-start.11 = (f32[1536]{0:T(1024)S(1)}, f32[1536]{0:T(1024)}, u32[]{:S(2)}) copy-start(f32[1536]{0:T(1024)} %param.29) | copy-start | bytes 18436
  427.6 1.1 copy-start.3
  428.7 1.1 copy-start.4
  429.7 1.0 copy-start.5
  430.7 1.0 copy-start.6
  431.7 1.0 copy-start.7
  432.7 3.9 copy-start.10
  432.7 7.3 %copy-start.8 = (bf16[384,1024]{1,0:T(8,128)(2,1)S(1)}, bf16[384,1024]{1,0:T(8,128)(2,1)}, u32[]{:S(2)}) copy-start(bf16[384,1024]{1,0:T(8,128)(2,1)} %get-tuple-element.87) | copy-start | bytes 2359300

commit v5 on v4

--- a/solution.py
+++ b/solution.py
@@ -78,6 +78,10 @@
     return pl.ds(pl.multiple_of(i * size, size), size)
 
 
+def split_vectors(ref):
+    return ref.at[0:4], ref.at[4:5], ref.at[5:6], ref.at[6:7], ref.at[7:8]
+
+
 def forward_kernel(*refs):
     refs = list(refs)
 
@@ -86,14 +90,16 @@
         return taken
 
     shards = take(8)
-    cotangent, tokens, marks, gain1, conv_w, conv_b, rate_b, input_b, decay_scale, gain2 = take(10)
+    cotangent, tokens, bounds, gains, vectors = take(5)
+    gain1, gain2 = gains.at[0:1], gains.at[1:2]
+    conv_w, conv_b, rate_b, input_b, decay_scale = split_vectors(vectors)
     fulls = take(8)
     outs = take(11)
-    pair_normed2, pair_cotangent = take(2)
+    pair_normed2, pair_cotangent, saved_marks = take(3)
     (w_rec, w_rate, w_input, w_branch, w_out) = weights = take(5)
     normed, padded, conv_out, conv_low, rate_pre, input_pre = take(6)
     products, states, branch_pre, mixed_in, resid, normed2 = take(6)
-    rim, ends, got, carry_in = take(4)
+    rim, ends, got, carry_in, marks = take(5)
     send, recv, local, near_send, near_recv, load_sem, save_sem = refs
     count = 8
     r, s, z, c = place()
@@ -260,6 +266,21 @@
         loop(12, one)
         save(0, normed, outs[0])
 
+    def mark():
+        place_of = lax.broadcasted_iota(jnp.int32, (144, 8), 0) + (s * 128 - 8)
+        column = lax.broadcasted_iota(jnp.int32, (136, 8), 1)
+        for row in range(3):
+            met = (place_of == bounds[row : row + 1, :]).astype(jnp.float32)
+            reset = jnp.max(met, axis=1, keepdims=True) + (place_of == 0).astype(jnp.float32)
+            keep = 1.0 - reset
+            second = keep * pltpu.roll(keep, 1, 0)
+            third = second * pltpu.roll(keep, 2, 0)
+            first, second, third = keep[8:], second[8:], third[8:]
+            values = jnp.where(column == 1, first, reset[8:])
+            values = jnp.where(column == 2, second, values)
+            marks[row] = jnp.where(column == 3, third, values)
+        save(11, marks, saved_marks)
+
     def rec_product():
         loads[0].wait()
 
@@ -396,7 +417,7 @@
             normed2[rows, :] = (values * scale * gain2[...]).astype(jnp.bfloat16)
 
         loop(12, one)
-        save(11, normed2, pair_normed2.at[pl.ds(0, tok)])
+        save(13, normed2, pair_normed2.at[pl.ds(0, tok)])
         return near(8, normed2, pair_normed2.at[pl.ds(tok, tok)], twin)
 
     tok = tokens.shape[0]
@@ -406,6 +427,7 @@
     ends[...] = jnp.zeros_like(ends)
     begin(0)
     begin(1)
+    mark()
     first_norm()
     tick(0)
     tick(1)
@@ -441,7 +463,7 @@
         copy.wait()
 
 
-def forward_all(shards, cotangent, tokens, marks, vectors):
+def forward_all(shards, cotangent, tokens, bounds, gains, vectors):
     low, full = jnp.bfloat16, jnp.float32
     tok, model = tokens.shape
     rec = shards[0].shape[1]
@@ -460,6 +482,7 @@
         shape((8, rec), full),
         shape((2 * tok, model), low),
         shape((2 * tok, model), low),
+        shape((3, 136, 8), full),
     )
     fulls = [shape((a.shape[0] * 8, a.shape[1]), low) for a in shards]
     for m in (5, 6):
@@ -469,8 +492,8 @@
     results = pl.pallas_call(
         forward_kernel,
         out_shape=fulls + saved,
-        in_specs=[ANY] * 9 + [VMEM] * 9,
-        out_specs=(ANY,) * 21,
+        in_specs=[VMEM] * 13,
+        out_specs=(ANY,) * 22,
         scratch_shapes=[pltpu.VMEM(a.shape, low) for a in fulls[:5]]
         + [
             pltpu.VMEM((tok, model), low),
@@ -489,19 +512,20 @@
             pltpu.VMEM((8, rec), full),
             pltpu.VMEM((8, 8, rec), full),
             pltpu.VMEM((8, rec), full),
+            pltpu.VMEM((3, 136, 8), full),
             pltpu.SemaphoreType.DMA((8, 20)),
             pltpu.SemaphoreType.DMA((8, 20)),
             pltpu.SemaphoreType.DMA((8, 2)),
             pltpu.SemaphoreType.DMA((10,)),
             pltpu.SemaphoreType.DMA((10,)),
             pltpu.SemaphoreType.DMA((5,)),
-            pltpu.SemaphoreType.DMA((13,)),
+            pltpu.SemaphoreType.DMA((14,)),
         ],
         compiler_params=pltpu.CompilerParams(
             collective_id=0, has_side_effects=True, vmem_limit_bytes=60 * 1024 * 1024
         ),
         name="recurrent_forward",
-    )(*shards, cotangent, tokens, marks, *vectors)
+    )(*shards, cotangent, tokens, bounds, gains, vectors)
     return results[:8], results[8:]
 
 class Reduction:
@@ -760,28 +784,57 @@
     return grad.shape[0] // (4 if kind == "rows" else 8), grad.shape[1] // 4
 
 
-def finish_kernel(count, *refs):
-    for block, whole in zip(refs[:count], refs[count:]):
-        part = block.shape[-1]
-        for q in range(4):
-            if len(block.shape) == 4:
-                for half in range(2):
-                    column = ((half + 2 * (q // 2)) * 2 + q % 2) * part
-                    whole[:, column : column + part] = block[q, half].astype(jnp.float32)
-            else:
-                whole[:, q * part : (q + 1) * part] = block[q].astype(jnp.float32)
-
-
-def finish(blocks):
-    shapes = [(b.shape[-2], b.size // b.shape[-2]) for b in blocks]
-    return pl.pallas_call(
-        functools.partial(finish_kernel, len(blocks)),
-        out_shape=tuple(jax.ShapeDtypeStruct(a, jnp.float32) for a in shapes),
-        in_specs=[VMEM] * len(blocks),
-        out_specs=(VMEM,) * len(blocks),
-        compiler_params=pltpu.CompilerParams(vmem_limit_bytes=40 * 1024 * 1024),
+def finish_kernel(count, plain, *refs):
+    take = taker(refs)
+    blocks, same = take(count), take(plain)
+    wholes, same_out = take(count), take(plain)
+    brought, wide, passed = take(count), take(count), take(plain)
+    sem_in, sem_out = take(2)
+    entries = [(a, b, i) for i, (a, b) in enumerate(zip(blocks + same, brought + passed))]
+    fetched = [pltpu.make_async_copy(a, b, sem_in.at[i]) for a, b, i in entries]
+    for copy in fetched:
+        copy.start()
+    written = []
+    for i in range(count + plain):
+        fetched[i].wait()
+        if i < count:
+            block, whole = brought[i], wide[i]
+            part = block.shape[-1]
+            for q in range(4):
+                for half in range(2 if len(block.shape) == 4 else 1):
+                    if len(block.shape) == 4:
+                        column = ((half + 2 * (q // 2)) * 2 + q % 2) * part
+                        values = block[q, half]
+                    else:
+                        column, values = q * part, block[q]
+                    whole[:, column : column + part] = values.astype(jnp.float32)
+            copy = pltpu.make_async_copy(whole, wholes[i], sem_out.at[i])
+        else:
+            copy = pltpu.make_async_copy(passed[i - count], same_out[i - count], sem_out.at[i])
+        copy.start()
+        written.append(copy)
+    for copy in written:
+        copy.wait()
+
+
+def finish(blocks, same):
+    shape = jax.ShapeDtypeStruct
+    whole = [(b.shape[-2], b.size // b.shape[-2]) for b in blocks]
+    count, plain = len(blocks), len(same)
+    results = pl.pallas_call(
+        functools.partial(finish_kernel, count, plain),
+        out_shape=tuple(shape(a, jnp.float32) for a in whole)
+        + tuple(shape(a.shape, a.dtype) for a in same),
+        in_specs=[ANY] * (count + plain),
+        out_specs=(ANY,) * (count + plain),
+        scratch_shapes=[pltpu.VMEM(b.shape, b.dtype) for b in blocks]
+        + [pltpu.VMEM(a, jnp.float32) for a in whole]
+        + [pltpu.VMEM(a.shape, a.dtype) for a in same]
+        + [pltpu.SemaphoreType.DMA((count + plain,))] * 2,
+        compiler_params=pltpu.CompilerParams(vmem_limit_bytes=62 * 1024 * 1024),
         name="widen_gradients",
-    )(*blocks)
+    )(*blocks, *same)
+    return results[:count], results[count:]
 
 
 def reduce_kernel(count, *refs):
@@ -866,16 +919,20 @@
 def backward_kernel(kinds, *refs):
     take = taker(refs)
     count = len(kinds)
-    grads = take(count)
-    part_mixed, part_normed2 = take(2)
+    grads = take(count - 1)
+    part_mixed, part_normed2, twin_normed2 = take(3)
     full_out, full_rate, full_input, full_branch, full_rec = take(5)
     saved_states, saved_branch, saved_rate, saved_input, saved_conv, saved_rec = take(6)
     marks, tokens, cotangent, resid, normed, conv_low, mixed_in, carried = take(8)
-    conv_w, rate_b, input_b, decay_scale, gain1, gain2 = take(6)
+    gains, vectors = take(2)
+    gain1, gain2 = gains.at[0:1], gains.at[1:2]
+    conv_w, _, rate_b, input_b, decay_scale = split_vectors(vectors)
     outs = take(count)
-    d_out, d_rate, d_input, d_branch, d_rec, token_grad, mixed = take(7)
-    small, small_norm, small_norm2 = take(3)
-    reduction = Reduction(kinds, grads, outs, *take_reduction(take, count))
+    d_rate, d_input, d_branch, d_rec, token_grad, mixed = take(6)
+    (small,) = take(1)
+    parts = take_reduction(take, count)
+    (d_out,) = take(1)
+    reduction = Reduction(kinds, grads + [d_out], outs, *parts)
     ring, past, branch_pre, rate_pre, input_pre, conv_out = take(6)
     flow, grads_conv, branch_low, rate_low, input_low, stage = take(6)
     rim, ends, got, carry = take(4)
@@ -883,8 +940,6 @@
     near_send, near_recv, load_sem, ring_sem, stage_sem = take(5)
     r, s, z, c = place()
     others = [(r, lax.rem(s + k, 8)) for k in range(1, 8)]
-    parity = lax.rem(z, 2)
-    twin = (r, s + 2 - 4 * parity)
     greet(others + [reduction.along_x, reduction.along_y, reduction.diagonal])
     live = []
 
@@ -941,12 +996,12 @@
     turn = [0]
 
     def outer_product(left, right, target):
-        for strip in range(left.shape[1] // 512):
+        for strip in range(left.shape[1] // 256):
             slot = turn[0] % 2
             turn[0] += 1
             if staged[slot] is not None:
                 staged[slot].wait()
-            rows = pl.ds(strip * 512, 512)
+            rows = pl.ds(strip * 256, 256)
             width = right.shape[1]
 
             def one(j):
@@ -964,6 +1019,23 @@
             )
             copy.start()
             staged[slot] = copy
+
+    def out_weight():
+        depth = d_out.shape[2]
+
+        def one(i):
+            source, column = lax.div(i, 2), lax.rem(i, 2)
+            columns = at(column, 512)
+            values = lax.dot_general(
+                mixed_in[:, at(source, 2 * depth)],
+                resid_low[:, columns],
+                (((0,), (0,)), ((), ())),
+                preferred_element_type=jnp.float32,
+            ).astype(jnp.bfloat16)
+            d_out[source, 0, :, columns] = values[:depth]
+            d_out[source, 1, :, columns] = values[depth:]
+
+        loop(8, one)
 
     def block_of(i):
         row, block = lax.div(i, 4), lax.rem(i, 4)
@@ -1130,7 +1202,7 @@
             return total + part[0:8] + part[8:16]
 
         total = lax.fori_loop(0, 24, one, jnp.zeros((8, 1024), jnp.float32))
-        small_norm2[...] = jnp.sum(total, axis=0, keepdims=True)
+        small[9:10, 0:1024] = jnp.sum(total, axis=0, keepdims=True)
 
     def mix_back():
         def one(i):
@@ -1151,27 +1223,22 @@
             back = grad * gain1[...]
             mean = jnp.mean(values * back, axis=-1, keepdims=True)
             result = grad_resid[rows, :] + scale * back - values * (scale * scale * scale * mean)
-            stage[0, rows, pl.ds(0, 1024)] = result.astype(jnp.bfloat16)
+            own_parts[1, rows, :] = result.astype(jnp.bfloat16)
             part = grad * values * scale
             return total + part[0:8] + part[8:16]
 
-        if staged[0] is not None:
-            staged[0].wait()
         total = lax.fori_loop(0, 24, one, jnp.zeros((8, 1024), jnp.float32))
-        small_norm[...] = jnp.sum(total, axis=0, keepdims=True)
-        copy = pltpu.make_async_copy(
-            stage.at[0, pl.ds(0, 384), pl.ds(0, 1024)], token_grad, stage_sem.at[0]
-        )
-        copy.start()
-        staged[0] = copy
+        small[8:9, 0:1024] = jnp.sum(total, axis=0, keepdims=True)
+        return bring(10, own_parts.at[1], token_grad)
 
     tok = tokens.shape[0]
-    normed2_copy = near(8, part_normed2.at[pl.ds(tok, tok)], twin_parts.at[1], twin)
+    twin = (r, s + 2 - 4 * lax.rem(z, 2))
     reduction.begin(0)
     reduction.begin(1)
-    mixed_copy = near(9, part_mixed.at[pl.ds(tok, tok)], twin_parts.at[0], twin)
+    mixed_copy = near(8, part_mixed.at[pl.ds(tok, tok)], twin_parts.at[0], twin)
     part_loads = [
         bring(6, part_normed2.at[pl.ds(0, tok)], own_parts.at[1]),
+        bring(9, twin_normed2, twin_parts.at[1]),
         bring(7, part_mixed.at[pl.ds(0, tok)], own_parts.at[0]),
     ]
     loads = [
@@ -1183,28 +1250,31 @@
     ]
     for i in range(3):
         fetch(i)
+    small[...] = jnp.zeros_like(small)
     ends[...] = jnp.zeros_like(ends)
     for row in range(3):
         past[row, 0:8, :] = jnp.broadcast_to(carried[row : row + 1, :], (8, past.shape[2]))
-    reduction.tick(0)
     part_loads[0].wait()
-    normed2_copy.wait_recv()
+    part_loads[1].wait()
     second_norm_back()
     for i in range(3):
         flow[:, pl.ds(i * 512, 512)] = back_tile(i, resid_low, 1024)
         fetch(i + 3)
+    reduction.tick(0)
+    out_weight()
     loads[0].wait()
     loads[1].wait()
     branch_back()
+    reduction.tick(1)
     loads[2].wait()
     copies = scan_back()
-    outer_product(mixed_in, resid_low, d_out)
-    reduction.tick(1)
+    reduction.tick(2)
     carry_back(copies)
     loads[3].wait()
     loads[4].wait()
     gates_back()
     loads.append(bring(5, saved_rec, past))
+    reduction.tick(3)
     at_tile = 3
     for j in range(3):
         columns = pl.ds(j * 512, 512)
@@ -1217,10 +1287,11 @@
         for row in range(3):
             grads_conv[row, 0:128, columns] = total[row * 128 : (row + 1) * 128]
     rim_copy = near(0, grads_conv.at[:, pl.ds(0, 8), :], rim, others[6])
-    reduction.tick(2)
+    reduction.tick(4)
     outer_product(conv_low, rate_low, d_rate)
     loads[5].wait()
     conv_back(rim_copy)
+    reduction.tick(5)
     for j in range(2):
         columns = pl.ds(j * 512, 512)
         total = back_tile(at_tile, branch_low, 1536)
@@ -1229,18 +1300,18 @@
         fetch(at_tile + 4)
         at_tile += 2
         input_pre[:, columns] = total
-    reduction.tick(3)
     outer_product(normed, rate_low, d_rec)
+    reduction.tick(6)
     outer_product(conv_low, input_low, d_input)
-    reduction.tick(4)
     outer_product(normed, branch_low, d_branch)
-    norm_back()
-    part_loads[1].wait()
+    token_save = norm_back()
+    part_loads[2].wait()
     mixed_copy.wait_recv()
     mixed_save = mix_back()
-    for now in range(5, reduction.ticks()):
+    for now in range(7, reduction.ticks()):
         reduction.tick(now)
     mixed_save.wait()
+    token_save.wait()
     for copy in staged:
         copy.wait()
     for copy in live:
@@ -1251,29 +1322,28 @@
 def backward_all(grads, parts, fulls, saved, local, vectors):
     low, full = jnp.bfloat16, jnp.float32
     shape, memory = jax.ShapeDtypeStruct, pltpu.VMEM
-    kinds = ("rows", "columns", "columns")
-    count = len(grads)
+    kinds = ("rows", "columns", "columns", "all")
+    count = len(kinds)
     tok, model = local[1].shape
     rec = fulls[0].shape[0]
-    out_shape = reduced_shapes(kinds, grads) + (
-        shape((rec, model), low),
+    all_grads = tuple(grads) + (shape((rec, model), low),)
+    out_shape = reduced_shapes(kinds, all_grads) + (
         shape((rec, rec), low),
         shape((rec, rec), low),
         shape((model, rec), low),
         shape((model, rec), low),
         shape((tok, model), low),
         shape((tok, model), low),
-        shape((8, rec), full),
-        shape((1, model), full),
-        shape((1, model), full),
+        shape((16, rec), full),
     )
     results = pl.pallas_call(
         functools.partial(backward_kernel, kinds),
         out_shape=out_shape,
-        in_specs=[ANY] * (count + 13) + [VMEM] * 14,
-        out_specs=(ANY,) * (count + 7) + (VMEM,) * 3,
-        scratch_shapes=reduction_memory(kinds, grads)
+        in_specs=[ANY] * (count + 13) + [VMEM] * 10,
+        out_specs=(ANY,) * (count + 6) + (VMEM,),
+        scratch_shapes=reduction_memory(kinds, all_grads)
         + [
+            memory((4, 2, rec // 8, model), low),
             memory((3, 512, rec), low),
             memory((3, 136, rec), full),
             memory((tok, rec), full),
@@ -1285,7 +1355,7 @@
             memory((tok, rec), low),
             memory((tok, rec), low),
             memory((tok, rec), low),
-            memory((2, 512, rec), low),
+            memory((2, 256, rec), low),
             memory((3, 8, rec), full),
             memory((8, rec), full),
             memory((8, 8, rec), full),
@@ -1294,9 +1364,9 @@
             memory((2, tok, model), low),
             memory((tok, model), full),
             memory((tok, model), low),
-            pltpu.SemaphoreType.DMA((10,)),
-            pltpu.SemaphoreType.DMA((10,)),
             pltpu.SemaphoreType.DMA((9,)),
+            pltpu.SemaphoreType.DMA((9,)),
+            pltpu.SemaphoreType.DMA((11,)),
             pltpu.SemaphoreType.DMA((3,)),
             pltpu.SemaphoreType.DMA((2,)),
         ],
@@ -1597,35 +1667,25 @@
 ):
     row_count, tok_count, model_width = tokens.shape
     rec_width = w_rec.shape[1]
-    offset = lax.axis_index("seq") * tok_count
-    positions = offset - 3 + jnp.arange(tok_count + 11, dtype=jnp.int32)
-    marked = (
-        jnp.any(positions[None, :, None] == bounds[:, None, :], axis=2) | (positions == 0)[None, :]
-    )
-    padded_resets = marked.astype(jnp.float32)
-    resets = padded_resets[:, 3:]
-    masks = conv_masks(padded_resets)
-    marks = jnp.stack((resets,) + masks + (resets,) * 4, axis=2)
     flat_tokens = tokens.reshape(-1, model_width)
-    decay_scale = (-8.0 * jax.nn.softplus(decay_param))[None]
+    gains = jnp.stack([norm1_gain, norm2_gain])
+    vectors = jnp.concatenate(
+        [
+            conv_weight,
+            jnp.stack([conv_bias, rate_bias, input_bias, -8.0 * jax.nn.softplus(decay_param)]),
+        ]
+    )
     fulls, saved = forward_all(
         (w_rec, w_rate, w_input, w_branch, w_out, w_gate, w_up, w_down),
         cotangent.reshape(-1, model_width),
         flat_tokens,
-        marks,
-        (
-            norm1_gain[None],
-            conv_weight,
-            conv_bias[None],
-            rate_bias[None],
-            input_bias[None],
-            decay_scale,
-            norm2_gain[None],
-        ),
+        bounds,
+        gains,
+        vectors,
     )
     full_rec, full_rate, full_input, full_branch, full_out, half_gate, half_up, half_down = fulls
     normed, padded, conv_out, conv_low, rate_pre, input_pre = saved[:6]
-    states, branch_pre, mixed_in, resid, carried, pair_normed2, pair_cotangent = saved[6:]
+    states, branch_pre, mixed_in, resid, carried, pair_normed2, pair_cotangent, marks = saved[6:]
     gate_pre = forward_product(pair_normed2, half_gate)
     up_pre = forward_product(pair_normed2, half_up)
     hidden = (jax.nn.gelu(gate_pre, approximate=True) * up_pre).astype(jnp.bfloat16)
@@ -1638,15 +1698,18 @@
     grad_gate_pre, grad_up_pre = pull_mlp(grad_hidden)
     gate_low = grad_gate_pre.astype(jnp.bfloat16)
     up_low = grad_up_pre.astype(jnp.bfloat16)
+    part_normed2 = (back_product(gate_low, half_gate) + back_product(up_low, half_up)).astype(
+        jnp.bfloat16
+    )
+    half = part_mixed.shape[0] // 2
+    twins = [(s, s + 2 - 4 * (s // 2 % 2)) for s in range(lax.axis_size("seq"))]
+    twin_normed2 = lax.ppermute(part_normed2[half:], "seq", twins)
     grad_gate = outer(pair_normed2, gate_low)
     grad_up = outer(pair_normed2, up_low)
-    part_normed2 = (back_product(gate_low, half_gate) + back_product(up_low, half_up)).astype(
-        jnp.bfloat16
-    )
     low = jnp.bfloat16
     ff, rest = backward_all(
         [g.astype(low) for g in (grad_down, grad_gate, grad_up)],
-        (part_mixed, part_normed2),
+        (part_mixed, part_normed2, twin_normed2),
         (full_out, full_rate, full_input, full_branch, full_rec),
         (
             states.reshape(row_count, tok_count, rec_width),
@@ -1666,39 +1729,31 @@
             mixed_in,
             carried,
         ),
-        (conv_weight, rate_bias[None], input_bias[None], decay_scale, norm1_gain[None], norm2_gain[None]),
-    )
-    rec_grads, (token_grad, mixed, sums, grad_norm1, grad_norm2) = rest[:5], rest[5:]
-    small = jnp.concatenate(
-        [
-            sums.reshape(-1, model_width),
-            grad_norm1,
-            grad_norm2,
-            jnp.zeros((2, model_width), jnp.float32),
-        ]
-    )
-    rec, small = reduce_all(rec_grads, small, 2)
-    blocks = finish(tuple(rec) + tuple(ff))
-    rec, ff = blocks[:5], blocks[5:]
-    sums = small[:12].reshape(8, rec_width)
+        (gains, vectors),
+    )
+    reduced, (token_grad, mixed, sums) = tuple(ff), rest[4:]
+    rec, sums = reduce_all(rest[:4], sums, 2)
+    (down, gate, up, out, rate, into, branch, recur), (mixed, token_grad) = finish(
+        reduced + tuple(rec), (mixed, token_grad)
+    )
     return (
         mixed.reshape(tokens.shape),
         token_grad.reshape(tokens.shape),
-        small[12],
-        rec[3],
-        rec[4],
+        sums[8, :model_width],
+        branch,
+        recur,
         sums[:4],
         sums[4],
-        rec[1],
+        rate,
         sums[6],
-        rec[2],
+        into,
         sums[7],
         -8.0 * jax.nn.sigmoid(decay_param) * sums[5],
-        rec[0],
-        small[13],
-        ff[1],
-        ff[2],
-        ff[0],
+        out,
+        sums[9, :model_width],
+        gate,
+        up,
+        down,
     )
 
 

time: 442 us -> 414 us (0.937)
  Pallas kernels: 383 us -> 361 us
  local copies, waits for them, and re-layouts: 16 us -> 8.94 us
    pallas_call x2, Pallas kernels: 158 us -> 144 us  [the longest x1 138 us: forward_all(): pl.pallas_call(forward_kernel, out_shape=fulls + saved, in_specs=[VMEM] *...]
    pallas_call x1, Pallas kernels: 117 us -> 108 us  [reduce_all(): pl.pallas_call(functools.partial(reduce_kernel, count), out_shape=reduced...]
    unnamed x36 -> x18, local copies, waits for them, and re-layouts: 6.92 us -> 0.92 us
    broadcast_in_dim x5 -> x0, local copies, waits for them, and re-layouts: 4.48 us -> none  [the longest x1 1.29 us: staged_body(): conv_bias[None]]
  transfers between devices with their start and end apart: 0 -> 1, of which waited for: 0 -> 1; matrix products, arithmetic and copies ran while one was open for 0% -> 4% of each run, Pallas kernels for 0% -> 0%
where the time goes in v5:
time: 414 us; the launch traced here: 413 us
  Pallas kernels  361 us (87%)
  matrix products  36.4 us (9%)
  local copies, waits for them, and re-layouts  8.94 us (2%)
    pallas_call x1, Pallas kernels, forward_all(): pl.pallas_call(forward_kernel, out_shape=fulls + saved, in_specs=[VMEM] *...  138 us
    pallas_call x1, Pallas kernels, backward_all(): pl.pallas_call(functools.partial(backward_kernel, kinds), out_shape=out_s...  109 us
    pallas_call x1, Pallas kernels, reduce_all(): pl.pallas_call(functools.partial(reduce_kernel, count), out_shape=reduced...  108 us
    dot_general x3, matrix products, back_product(): lax.dot_general(grads, weight, (((1,), (1,)), ((), ())), preferred_elemen...  12.6 us
    dot_general x3, matrix products, outer(): lax.dot_general(left, right, (((0,), (0,)), ((), ())), preferred_element_...  12.4 us
    dot_general x3, matrix products, forward_product(): return jnp.dot(values, weight, preferred_element_type=jnp.float32)  11.4 us
  transfers between devices with their start and end apart: 1, of which 1 were waited for; matrix products, arithmetic and copies ran while one was open for 4% of the time, Pallas kernels for 0%

profile of v5, /device:TPU:0, one launch (start us, length us, event | category | flops | bytes accessed | tf_op | source)
XLA Modules:
  0.0 413.2 jit_solution(13519925760030263649)
XLA Ops:
  0.7 0.7 stack.24
  1.4 0.7 stack.25
  2.8 0.7 fusion.7
  3.5 1.3 pad_maximum_fusion.refs_11_.refs_25_
  4.8 1.4 concatenate.3.refs_12_.refs_26_
  6.2 138.1 %recurrent_forward.1 = (bf16[1024,1536]{1,0:T(8,128)(2,1)}, bf16[1536,1536]{1,0:T(8,128)(2,1)}, bf16[1536,1536]{1,0:T(8,128)(2,1)}, bf16[1024,1536]{1,0:T(8,128)...) custom-call(bf16[128,1536]{1,0:T(8,128)(2,1)} %refs_0_.1, ...), custom_call_target="tpu_custom_call" | custom-call | tf_op jit(solution)/shard_map/recurrent_forward/pallas_call | solution.py:492
  144.3 5.1 %fusion.9 = f32[768,1536]{1,0:T(8,128)S(1)} fusion(bf16[768,1024]{1,0:T(8,128)(2,1)} %get-tuple-element.65, bf16[1024,1536]{1,0:T(8,128)(2,1)} %get-tuple-element.66), kind=kOutput, calls=%fused_computation.26 | convolution fusion | flops 2415919104 | bytes 9437184 | tf_op jit(solution)/shard_map/dot_general | solution.py:1437
  149.5 2.6 fusion.10
  152.1 7.3 %multiply_convert_fusion = (bf16[768,1536]{1,0:T(8,128)(2,1)}, bf16[768,1536]{1,0:T(8,128)(2,1)S(1)}, bf16[768,1536]{1,0:T(8,128)(2,1)S(1)}) fusion(f32[768,1536]{1,0:T(8,128)S(1)} %fusion.9, f32[768,1536]{1,0:T(8,128)S(1)} %fusion.10, bf16[768,1024]{1,0:T(8,128)(2,1)S(1)} %copy-done.6, bf16[1536,1024]{1,0:T(8,128)(2,1)S(1)} %copy-done.3), kind=kOutput, calls=%fused_computation.9 | convolution fusion | flops 2446589952 | bytes 21233664 | tf_op jit(solution)/shard_map/dot_general | solution.py:1447
  159.4 2.6 fusion.11
  162.1 2.6 add_convert_fusion.refs_4_
  164.8 2.2 collective-permute-start
  167.0 4.2 %convolution_convert_fusion = bf16[1024,1536]{1,0:T(8,128)(2,1)} fusion(bf16[768,1024]{1,0:T(8,128)(2,1)S(1)} %copy-done.7, bf16[768,1536]{1,0:T(8,128)(2,1)S(1)} %copy-done.8), kind=kOutput, calls=%fused_computation.12 | convolution fusion | flops 2417491968 | bytes 7077888 | tf_op jit(solution)/shard_map/dot_general | solution.py:1441
  171.2 4.2 %convolution_convert_fusion.1 = bf16[1024,1536]{1,0:T(8,128)(2,1)} fusion(bf16[768,1024]{1,0:T(8,128)(2,1)S(1)} %copy-done.7, bf16[768,1536]{1,0:T(8,128)(2,1)S(1)} %get-tuple-element.118), kind=kOutput, calls=%fused_computation.13 | convolution fusion | flops 2417491968 | bytes 7077888 | tf_op jit(solution)/shard_map/dot_general | solution.py:1441
  175.3 4.1 convolution_convert_fusion.2
  179.4 3.7 convolution_convert_fusion.3.refs_3_
  183.1 1.4 collective-permute-done.refs_5_
  184.4 0.9 copy-done.1
  185.3 109.2 %recurrent_backward.1 = (bf16[4,384,256]{2,1,0:T(8,128)(2,1)}, bf16[4,2,128,384]{3,2,1,0:T(8,128)(2,1)}, bf16[4,2,128,384]{3,2,1,0:T(8,128)(2,1)}, bf16[4,192,25...) custom-call(bf16[2,2,384,1024]{3,2,1,0:T(8,128)(2,1)} %bitcast.44, ...), custom_call_target="tpu_custom_call" | custom-call | tf_op jit(solution)/shard_map/recurrent_backward/pallas_call | solution.py:1339
  294.5 107.8 %reduce_grads.1 = (bf16[4,192,384]{2,1,0:T(8,128)(2,1)}, bf16[4,192,384]{2,1,0:T(8,128)(2,1)}, bf16[4,128,384]{2,1,0:T(8,128)(2,1)}, bf16[4,128,384]{2,1,0:T(8,128)(2,1)}, f32[16,1536]{1,0:T(8,128)}) custom-call(bf16[4,2,192,1536]{3,2,1,0:T(8,128)(2,1)} %bitcast.34, bf16[4,2,192,1536]{3,2,1,0:T(8,128)(2,1)} %bitcast.35, bf16[4,2,128,1536]{3,2,1,0:T(8,128)(2,1)} %bitcast.36, ...), custom_call_target="tpu_custom_call" | custom-call | tf_op jit(solution)/shard_map/reduce_grads/pallas_call | solution.py:898
  402.3 1.4 fusion.8
  403.7 1.4 slice.26
  405.2 1.6 slice_reduce_fusion
  407.4 5.6 %widen_gradients.1 = (f32[384,1024]{1,0:T(8,128)}, f32[128,3072]{1,0:T(8,128)}, f32[128,3072]{1,0:T(8,128)}, f32[192,1024]{1,0:T(8,128)}, f32[192,1536]{1,0:T(8,...) custom-call(bf16[4,384,256]{2,1,0:T(8,128)(2,1)} %get-tuple-element., ...), custom_call_target="tpu_custom_call" | custom-call | tf_op jit(solution)/shard_map/widen_gradients/pallas_call | solution.py:824
  (21 shorter events, 1.4 us)
Async XLA Ops:
  144.3 5.1 %copy-start.4 = (bf16[1024,1536]{1,0:T(8,128)(2,1)S(1)}, bf16[1024,1536]{1,0:T(8,128)(2,1)}, u32[]{:S(2)}) copy-start(bf16[1024,1536]{1,0:T(8,128)(2,1)} %get-tuple-element.67) | copy-start | bytes 9437188
  144.3 5.1 %copy-start.7 = (bf16[768,1024]{1,0:T(8,128)(2,1)S(1)}, bf16[768,1024]{1,0:T(8,128)(2,1)}, u32[]{:S(2)}) copy-start(bf16[768,1024]{1,0:T(8,128)(2,1)} %get-tuple-element.65) | copy-start | bytes 4718596
  149.4 2.6 copy-start.3
  149.5 2.6 copy-start.6
  152.1 7.3 %copy-start.5 = (bf16[1024,1536]{1,0:T(8,128)(2,1)S(1)}, bf16[1024,1536]{1,0:T(8,128)(2,1)}, u32[]{:S(2)}) copy-start(bf16[1024,1536]{1,0:T(8,128)(2,1)} %get-tuple-element.66) | copy-start | bytes 9437188
  159.4 2.6 copy-start.8
  164.7 6.5 %copy-start = (bf16[768,1024]{1,0:T(8,128)(2,1)}, bf16[768,1024]{1,0:T(8,128)(2,1)S(1)}, u32[]{:S(2)}) copy-start(bf16[768,1024]{1,0:T(8,128)(2,1)S(1)} %add_convert_fusion.refs_4_) | copy-start | bytes 4718596
  164.8 19.6 %collective-permute-start = (bf16[384,1024]{1,0:T(8,128)(2,1)S(1)}, bf16[384,1024]{1,0:T(8,128)(2,1)S(1)}, u32[]{:S(2)}, u32[]{:S(2)}) collective-permute-start(bf16[384,1024]{1,0:T(8,128)(2,1)S(1)} %slice.32), channel_id=1, source_target_pairs={{0,2},{1,3},{2,0},{3,1},{4,6},{5,7},{6,4},{7,5},{8,10},{9,11},{10,... | collective-permute-start | bytes 2359304 | tf_op jit(solution)/shard_map/ppermute | solution.py:1706
  184.4 0.9 copy-start.1
  294.5 112.3 %copy-start.2 = (f32[1536]{0:T(1024)S(1)}, f32[1536]{0:T(1024)}, u32[]{:S(2)}) copy-start(f32[1536]{0:T(1024)} %param.29) | copy-start | bytes 18436

commit v6 on v5

--- a/solution.py
+++ b/solution.py
@@ -529,8 +529,8 @@
     return results[:8], results[8:]
 
 class Reduction:
-    def __init__(self, kinds, grads, outs, scratch, sems):
-        self.kinds = kinds
+    def __init__(self, kinds, grads, outs, scratch, sems, swapped=()):
+        self.kinds, self.swapped = kinds, swapped
         self.grads, self.outs = grads, outs
         self.count = len(grads)
         self.held, self.own, self.first, self.second, self.third, self.final = scratch
@@ -573,6 +573,19 @@
 
     def begin(self, m):
         part = self.held[m].shape[3]
+        if m < len(self.swapped):
+            far = [
+                pltpu.make_async_copy(
+                    self.swapped[m].at[:, :, pl.ds(q * part, part)],
+                    self.held[m].at[q],
+                    self.local.at[m, 5 + q],
+                )
+                for q in range(4)
+            ]
+            for copy in far:
+                copy.start()
+            self.at_c[m] = (far, [self.load(m, 0), self.load(m, 1)])
+            return
         far = [
             self.remote(
                 m,
@@ -590,7 +603,10 @@
         half = held.shape[2] // 2
         far, near = self.at_c[m]
         for q in range(4):
-            far[q].wait_recv()
+            if m < len(self.swapped):
+                far[q].wait()
+            else:
+                far[q].wait_recv()
             near[q].wait()
 
             def add(b):
@@ -599,6 +615,41 @@
             loop(held.shape[1], add)
             if q < 2:
                 near.append(self.load(m, q + 2))
+        if self.kinds[m] == "early":
+            self.at_z[m] = [
+                self.remote(
+                    m,
+                    9 + k,
+                    held.at[:, lax.rem(self.z + k, 4)],
+                    self.third[m].at[k - 1],
+                    self.along_z[k - 1],
+                )
+                for k in (1, 2, 3)
+            ]
+        else:
+            self.send_one(m)
+
+    def sources(self, m):
+        return pl.ds(self.z, 1) if self.kinds[m] == "early" else pl.ds(0, self.held[m].shape[1])
+
+    def stage_early(self, m):
+        held, third, z = self.held[m], self.third[m], self.z
+        blocks = held.shape[2] // 32
+        for copy in self.at_z[m]:
+            copy.wait_recv()
+
+        def add(i):
+            q, rows = lax.div(i, blocks), at(lax.rem(i, blocks), 32)
+            values = held[q, z, rows, :].astype(jnp.float32)
+            for k in range(3):
+                values = values + third[k, q, rows, :].astype(jnp.float32)
+            held[q, z, rows, :] = values.astype(jnp.bfloat16)
+
+        loop(4 * blocks, add)
+        self.send_one(m)
+
+    def send_one(self, m):
+        held, half, sources = self.held[m], self.held[m].shape[2] // 2, self.sources(m)
         self.at_one[m] = []
         for other in range(2):
             quarter = other * 2 + (1 - self.rx)
@@ -606,7 +657,7 @@
                 self.remote(
                     m,
                     4 + other,
-                    held.at[quarter, :, pl.ds(0, half)],
+                    held.at[quarter, sources, pl.ds(0, half)],
                     self.first[m].at[0, other],
                     self.along_x,
                 )
@@ -616,38 +667,40 @@
                 self.remote(
                     m,
                     6 + other,
-                    held.at[quarter, :, pl.ds(half, half)],
+                    held.at[quarter, sources, pl.ds(half, half)],
                     self.first[m].at[1, other],
                     self.along_y,
                 )
             )
 
     def stage_one(self, m):
-        held, first = self.held[m], self.first[m]
-        count, half = held.shape[1], held.shape[2] // 2
+        held, first, sources = self.held[m], self.first[m], self.sources(m)
+        count, half = first.shape[2], held.shape[2] // 2
+        base = self.z if self.kinds[m] == "early" else 0
         for copy in self.at_one[m]:
             copy.wait_recv()
 
         def add(i):
             other, b = lax.div(i, count), lax.rem(i, count)
+            at_b = base + b
             qx = other * 2 + self.rx
-            held[qx, b, :half] = held[qx, b, :half] + first[0, other, b]
+            held[qx, at_b, :half] = held[qx, at_b, :half] + first[0, other, b]
             qy = self.ry * 2 + other
-            held[qy, b, half:] = held[qy, b, half:] + first[1, other, b]
+            held[qy, at_b, half:] = held[qy, at_b, half:] + first[1, other, b]
 
         loop(2 * count, add)
         self.at_two[m] = [
             self.remote(
                 m,
                 8,
-                held.at[(1 - self.ry) * 2 + self.rx, :, pl.ds(0, half)],
+                held.at[(1 - self.ry) * 2 + self.rx, sources, pl.ds(0, half)],
                 self.second[m].at[0],
                 self.along_y,
             ),
             self.remote(
                 m,
                 9,
-                held.at[self.ry * 2 + (1 - self.rx), :, pl.ds(half, half)],
+                held.at[self.ry * 2 + (1 - self.rx), sources, pl.ds(half, half)],
                 self.second[m].at[1],
                 self.along_x,
             ),
@@ -655,15 +708,21 @@
 
     def stage_two(self, m):
         held, second, r = self.held[m], self.second[m], self.r
-        half = held.shape[2] // 2
+        count, half = second.shape[1], held.shape[2] // 2
+        early = self.kinds[m] == "early"
+        base = self.z if early else 0
         for copy in self.at_two[m]:
             copy.wait_recv()
 
         def add(b):
-            held[r, b, :half] = held[r, b, :half] + second[0, b]
-            held[r, b, half:] = held[r, b, half:] + second[1, b]
-
-        loop(held.shape[1], add)
+            held[r, base + b, :half] = held[r, base + b, :half] + second[0, b]
+            held[r, base + b, half:] = held[r, base + b, half:] + second[1, b]
+
+        loop(count, add)
+        if early:
+            self.final[m][r] = held[r, self.z]
+            self.send_final(m)
+            return
         rows = self.kinds[m] == "rows"
         self.at_z[m] = []
         for k in (2,) if rows else (1, 2, 3):
@@ -702,6 +761,10 @@
                 final[r, rows, :] = total(mine, *((0,) if kind == "rows" else (0, 1, 2)))
 
         loop(held.shape[2] // 32, add)
+        self.send_final(m)
+
+    def send_final(self, m):
+        final, r = self.final[m], self.r
         self.at_end[m] = [
             self.remote(m, 13 + i, final.at[r], final.at[r], device)
             for i, device in enumerate((self.along_x, self.along_y, self.diagonal))
@@ -741,14 +804,18 @@
     shapes = [(2 if kind == "rows" else 4,) + quarter_shape(kind, g) for kind, g in zip(kinds, grads)]
     scratch = [pltpu.VMEM((4, zs, k, n), low) for zs, k, n in shapes]
     scratch += [pltpu.VMEM((2, zs, k, n), low) for zs, k, n in shapes]
-    scratch += [pltpu.VMEM((2, 2, zs, k // 2, n), low) for zs, k, n in shapes]
-    scratch += [pltpu.VMEM((2, zs, k // 2, n), low) for zs, k, n in shapes]
-    scratch += [pltpu.VMEM((zs - 1, k, n), low) for zs, k, n in shapes]
+    summed = [1 if kind == "early" else zs for kind, (zs, _, _) in zip(kinds, shapes)]
+    scratch += [pltpu.VMEM((2, 2, zs, k // 2, n), low) for zs, (_, k, n) in zip(summed, shapes)]
+    scratch += [pltpu.VMEM((2, zs, k // 2, n), low) for zs, (_, k, n) in zip(summed, shapes)]
+    scratch += [
+        pltpu.VMEM((3, 4, k, n) if kind == "early" else (zs - 1, k, n), low)
+        for kind, (zs, k, n) in zip(kinds, shapes)
+    ]
     scratch += [pltpu.VMEM(a.shape, low) for a in reduced_shapes(kinds, grads)]
     return scratch + [
         pltpu.SemaphoreType.DMA((count, REDUCTION_SEMS)),
         pltpu.SemaphoreType.DMA((count, REDUCTION_SEMS)),
-        pltpu.SemaphoreType.DMA((count, 5)),
+        pltpu.SemaphoreType.DMA((count, 9)),
     ]
 
 
@@ -837,13 +904,17 @@
     return results[:count], results[count:]
 
 
-def reduce_kernel(count, *refs):
+REC_KINDS = ("early", "all", "all", "all")
+
+
+def reduce_kernel(count, swaps, *refs):
     take = taker(refs)
     grads = take(count)
+    swapped = take(swaps)
     (small_in,) = take(1)
     outs = take(count)
     (small_out,) = take(1)
-    reduction = Reduction(("all",) * count, grads, outs, *take_reduction(take, count))
+    reduction = Reduction(REC_KINDS, grads, outs, *take_reduction(take, count), swapped)
     small_held, small_got, small_send, small_recv = take(4)
     z = reduction.z
     greet(reduction.peers())
@@ -864,19 +935,46 @@
 
     small_held[0] = small_in[...]
     swap = swap_small(0, 0, reduction.mate)
-    reduction.begin(0)
-    if count > 1:
-        reduction.begin(1)
-    for now in range(reduction.ticks()):
-        reduction.tick(now)
-        if now < 2:
-            swap.wait_recv()
-            small_held[now + 1] = small_held[now] + small_got[now]
-            swap = swap_small(now + 1, now + 1, (reduction.along_x, reduction.along_y)[now])
-        if now == 2:
-            swap.wait_recv()
-            small_held[3] = small_held[2] + small_got[2]
-            spread = [swap_small(2 + k, 3, reduction.along_z[k - 1]) for k in (1, 2, 3)]
+    begin, core, early = reduction.begin, reduction.stage_core, reduction.stage_early
+    one, two, over_z, end = (
+        reduction.stage_one,
+        reduction.stage_two,
+        reduction.stage_z,
+        reduction.stage_end,
+    )
+    begin(0)
+    begin(1)
+    core(0)
+    begin(2)
+    core(1)
+    begin(3)
+    core(2)
+    one(1)
+    swap.wait_recv()
+    small_held[1] = small_held[0] + small_got[0]
+    swap = swap_small(1, 1, reduction.along_x)
+    core(3)
+    one(2)
+    two(1)
+    swap.wait_recv()
+    small_held[2] = small_held[1] + small_got[1]
+    swap = swap_small(2, 2, reduction.along_y)
+    one(3)
+    early(0)
+    two(2)
+    swap.wait_recv()
+    small_held[3] = small_held[2] + small_got[2]
+    spread = [swap_small(2 + k, 3, reduction.along_z[k - 1]) for k in (1, 2, 3)]
+    over_z(1)
+    one(0)
+    two(3)
+    two(0)
+    over_z(2)
+    end(1)
+    over_z(3)
+    end(0)
+    end(2)
+    end(3)
     for copy in spread:
         copy.wait_recv()
     small_got[6] = small_held[3]
@@ -892,14 +990,14 @@
     reduction.close()
 
 
-def reduce_all(grads, small, tag):
+def reduce_all(grads, swapped, small, tag):
     count = len(grads)
-    kinds = ("all",) * count
+    kinds = REC_KINDS
     results = pl.pallas_call(
-        functools.partial(reduce_kernel, count),
+        functools.partial(reduce_kernel, count, len(swapped)),
         out_shape=reduced_shapes(kinds, grads)
         + (jax.ShapeDtypeStruct(small.shape, small.dtype),),
-        in_specs=[ANY] * count + [VMEM],
+        in_specs=[ANY] * (count + len(swapped)) + [VMEM],
         out_specs=(ANY,) * count + (VMEM,),
         scratch_shapes=reduction_memory(kinds, grads)
         + [
@@ -912,7 +1010,7 @@
             collective_id=tag, has_side_effects=True, vmem_limit_bytes=60 * 1024 * 1024
         ),
         name="reduce_grads",
-    )(*[split_rows("all", g) for g in grads], small)
+    )(*[split_rows("all", g) for g in grads], *swapped, small)
     return results[:count], results[count]
 
 
@@ -928,7 +1026,7 @@
     gain1, gain2 = gains.at[0:1], gains.at[1:2]
     conv_w, _, rate_b, input_b, decay_scale = split_vectors(vectors)
     outs = take(count)
-    d_rate, d_input, d_branch, d_rec, token_grad, mixed = take(6)
+    d_rate, d_input, d_branch, d_rec, token_grad, mixed, swap_rec, swap_rate = take(8)
     (small,) = take(1)
     parts = take_reduction(take, count)
     (d_out,) = take(1)
@@ -1036,6 +1134,25 @@
             d_out[source, 1, :, columns] = values[depth:]
 
         loop(8, one)
+
+    swaps = []
+
+    def swap_halves(first, source, target):
+        for slot in range(2):
+            if staged[slot] is not None:
+                staged[slot].wait()
+                staged[slot] = None
+        depth = target.shape[1]
+        for block in range(4):
+            row = pl.multiple_of((block * 2 + 1 - c) * depth, 16)
+            swaps.append(
+                near(
+                    first + block,
+                    source.at[pl.ds(row, depth)],
+                    target.at[block],
+                    reduction.mate,
+                )
+            )
 
     def block_of(i):
         row, block = lax.div(i, 4), lax.rem(i, 4)
@@ -1269,6 +1386,9 @@
     loads[2].wait()
     copies = scan_back()
     reduction.tick(2)
+    part_loads[2].wait()
+    mixed_copy.wait_recv()
+    mixed_save = mix_back()
     carry_back(copies)
     loads[3].wait()
     loads[4].wait()
@@ -1291,6 +1411,7 @@
     outer_product(conv_low, rate_low, d_rate)
     loads[5].wait()
     conv_back(rim_copy)
+    swap_halves(9, d_rate, swap_rate)
     reduction.tick(5)
     for j in range(2):
         columns = pl.ds(j * 512, 512)
@@ -1302,18 +1423,19 @@
         input_pre[:, columns] = total
     outer_product(normed, rate_low, d_rec)
     reduction.tick(6)
+    swap_halves(13, d_rec, swap_rec)
     outer_product(conv_low, input_low, d_input)
     outer_product(normed, branch_low, d_branch)
     token_save = norm_back()
-    part_loads[2].wait()
-    mixed_copy.wait_recv()
-    mixed_save = mix_back()
     for now in range(7, reduction.ticks()):
         reduction.tick(now)
+    for copy in swaps:
+        copy.wait_recv()
     mixed_save.wait()
     token_save.wait()
     for copy in staged:
-        copy.wait()
+        if copy is not None:
+            copy.wait()
     for copy in live:
         copy.wait_send()
     reduction.close()
@@ -1334,13 +1456,15 @@
         shape((model, rec), low),
         shape((tok, model), low),
         shape((tok, model), low),
+        shape((4, model // 8, rec), low),
+        shape((4, rec // 8, rec), low),
         shape((16, rec), full),
     )
     results = pl.pallas_call(
         functools.partial(backward_kernel, kinds),
         out_shape=out_shape,
         in_specs=[ANY] * (count + 13) + [VMEM] * 10,
-        out_specs=(ANY,) * (count + 6) + (VMEM,),
+        out_specs=(ANY,) * (count + 8) + (VMEM,),
         scratch_shapes=reduction_memory(kinds, all_grads)
         + [
             memory((4, 2, rec // 8, model), low),
@@ -1364,8 +1488,8 @@
             memory((2, tok, model), low),
             memory((tok, model), full),
             memory((tok, model), low),
-            pltpu.SemaphoreType.DMA((9,)),
-            pltpu.SemaphoreType.DMA((9,)),
+            pltpu.SemaphoreType.DMA((17,)),
+            pltpu.SemaphoreType.DMA((17,)),
             pltpu.SemaphoreType.DMA((11,)),
             pltpu.SemaphoreType.DMA((3,)),
             pltpu.SemaphoreType.DMA((2,)),
@@ -1731,9 +1855,10 @@
         ),
         (gains, vectors),
     )
-    reduced, (token_grad, mixed, sums) = tuple(ff), rest[4:]
-    rec, sums = reduce_all(rest[:4], sums, 2)
-    (down, gate, up, out, rate, into, branch, recur), (mixed, token_grad) = finish(
+    reduced, (token_grad, mixed, swap_rec, swap_rate, sums) = tuple(ff), rest[4:]
+    rate, into, branch, recur = rest[:4]
+    rec, sums = reduce_all((recur, rate, into, branch), (swap_rec, swap_rate), sums, 2)
+    (down, gate, up, out, recur, rate, into, branch), (mixed, token_grad) = finish(
         reduced + tuple(rec), (mixed, token_grad)
     )
     return (

time: 414 us -> 406 us (0.981)
  Pallas kernels: 361 us -> 352 us
    pallas_call x1, Pallas kernels: 108 us -> 99.4 us  [reduce_all(): pl.pallas_call(functools.partial(reduce_kernel, count, len(swapped)), out...]
where the time goes in v6:
time: 406 us; the launch traced here: 405 us
  Pallas kernels  352 us (87%)
  matrix products  36.4 us (9%)
  local copies, waits for them, and re-layouts  8.94 us (2%)
    pallas_call x1, Pallas kernels, forward_all(): pl.pallas_call(forward_kernel, out_shape=fulls + saved, in_specs=[VMEM] *...  138 us
    pallas_call x1, Pallas kernels, backward_all(): pl.pallas_call(functools.partial(backward_kernel, kinds), out_shape=out_s...  109 us
    pallas_call x1, Pallas kernels, reduce_all(): pl.pallas_call(functools.partial(reduce_kernel, count, len(swapped)), out...  99.4 us
    dot_general x3, matrix products, back_product(): lax.dot_general(grads, weight, (((1,), (1,)), ((), ())), preferred_elemen...  12.6 us
    dot_general x3, matrix products, outer(): lax.dot_general(left, right, (((0,), (0,)), ((), ())), preferred_element_...  12.4 us
    dot_general x3, matrix products, forward_product(): return jnp.dot(values, weight, preferred_element_type=jnp.float32)  11.4 us
  transfers between devices with their start and end apart: 1, of which 1 were waited for; matrix products, arithmetic and copies ran while one was open for 4% of the time, Pallas kernels for 0%

profile of v6, /device:TPU:0, one launch (start us, length us, event | category | flops | bytes accessed | tf_op | source)
XLA Modules:
  0.0 405.0 jit_solution(4017508885734663392)
XLA Ops:
  0.7 0.7 stack.24
  1.4 0.7 stack.25
  2.8 0.7 fusion.7
  3.5 1.3 pad_maximum_fusion.refs_11_.refs_25_
  4.8 1.4 concatenate.3.refs_12_.refs_26_
  6.2 138.1 %recurrent_forward.1 = (bf16[1024,1536]{1,0:T(8,128)(2,1)}, bf16[1536,1536]{1,0:T(8,128)(2,1)}, bf16[1536,1536]{1,0:T(8,128)(2,1)}, bf16[1024,1536]{1,0:T(8,128)...) custom-call(bf16[128,1536]{1,0:T(8,128)(2,1)} %refs_0_.1, ...), custom_call_target="tpu_custom_call" | custom-call | tf_op jit(solution)/shard_map/recurrent_forward/pallas_call | solution.py:492
  144.3 5.1 %fusion.9 = f32[768,1536]{1,0:T(8,128)S(1)} fusion(bf16[768,1024]{1,0:T(8,128)(2,1)} %get-tuple-element.67, bf16[1024,1536]{1,0:T(8,128)(2,1)} %get-tuple-element.68), kind=kOutput, calls=%fused_computation.26 | convolution fusion | flops 2415919104 | bytes 9437184 | tf_op jit(solution)/shard_map/dot_general | solution.py:1561
  149.5 2.6 fusion.10
  152.1 7.3 %multiply_convert_fusion = (bf16[768,1536]{1,0:T(8,128)(2,1)}, bf16[768,1536]{1,0:T(8,128)(2,1)S(1)}, bf16[768,1536]{1,0:T(8,128)(2,1)S(1)}) fusion(f32[768,1536]{1,0:T(8,128)S(1)} %fusion.9, f32[768,1536]{1,0:T(8,128)S(1)} %fusion.10, bf16[768,1024]{1,0:T(8,128)(2,1)S(1)} %copy-done.6, bf16[1536,1024]{1,0:T(8,128)(2,1)S(1)} %copy-done.3), kind=kOutput, calls=%fused_computation.9 | convolution fusion | flops 2446589952 | bytes 21233664 | tf_op jit(solution)/shard_map/dot_general | solution.py:1571
  159.4 2.6 fusion.11
  162.1 2.6 add_convert_fusion.refs_4_
  164.8 2.2 collective-permute-start
  167.0 4.2 %convolution_convert_fusion = bf16[1024,1536]{1,0:T(8,128)(2,1)} fusion(bf16[768,1024]{1,0:T(8,128)(2,1)S(1)} %copy-done.7, bf16[768,1536]{1,0:T(8,128)(2,1)S(1)} %copy-done.8), kind=kOutput, calls=%fused_computation.12 | convolution fusion | flops 2417491968 | bytes 7077888 | tf_op jit(solution)/shard_map/dot_general | solution.py:1565
  171.2 4.2 %convolution_convert_fusion.1 = bf16[1024,1536]{1,0:T(8,128)(2,1)} fusion(bf16[768,1024]{1,0:T(8,128)(2,1)S(1)} %copy-done.7, bf16[768,1536]{1,0:T(8,128)(2,1)S(1)} %get-tuple-element.122), kind=kOutput, calls=%fused_computation.13 | convolution fusion | flops 2417491968 | bytes 7077888 | tf_op jit(solution)/shard_map/dot_general | solution.py:1565
  175.3 4.1 %convolution_convert_fusion.2 = bf16[1536,1024]{1,0:T(8,128)(2,1)} fusion(bf16[768,1536]{1,0:T(8,128)(2,1)S(1)} %get-tuple-element.123, bf16[768,1024]{1,0:T(8,128)(2,1)S(1)} %copy-done.6), kind=kOutput, calls=%fused_computation.14 | convolution fusion | flops 2417491968 | bytes 7077888 | tf_op jit(solution)/shard_map/dot_general | solution.py:1565
  179.4 3.7 convolution_convert_fusion.3.refs_3_
  183.1 1.4 collective-permute-done.refs_5_
  184.4 0.9 copy-done.1
  185.3 109.3 %recurrent_backward.1 = (bf16[4,384,256]{2,1,0:T(8,128)(2,1)}, bf16[4,2,128,384]{3,2,1,0:T(8,128)(2,1)}, bf16[4,2,128,384]{3,2,1,0:T(8,128)(2,1)}, bf16[4,192,25...) custom-call(bf16[2,2,384,1024]{3,2,1,0:T(8,128)(2,1)} %bitcast.44, ...), custom_call_target="tpu_custom_call" | custom-call | tf_op jit(solution)/shard_map/recurrent_backward/pallas_call | solution.py:1463
  294.6 99.4 %reduce_grads.1 = (bf16[4,128,384]{2,1,0:T(8,128)(2,1)}, bf16[4,192,384]{2,1,0:T(8,128)(2,1)}, bf16[4,192,384]{2,1,0:T(8,128)(2,1)}, bf16[4,128,384]{2,1,0:T(8,128)(2,1)}, f32[16,1536]{1,0:T(8,128)}) custom-call(bf16[4,2,128,1536]{3,2,1,0:T(8,128)(2,1)} %bitcast.37, bf16[4,2,192,1536]{3,2,1,0:T(8,128)(2,1)} %bitcast.34, bf16[4,2,192,1536]{3,2,1,0:T(8,128)(2,1)} %bitcast.35, ...), custom_call_target="tpu_custom_call" | custom-call | tf_op jit(solution)/shard_map/reduce_grads/pallas_call | solution.py:996
  394.1 1.4 fusion.8
  395.5 1.4 slice.26
  396.9 1.6 slice_reduce_fusion
  399.1 5.6 %widen_gradients.1 = (f32[384,1024]{1,0:T(8,128)}, f32[128,3072]{1,0:T(8,128)}, f32[128,3072]{1,0:T(8,128)}, f32[192,1024]{1,0:T(8,128)}, f32[128,1536]{1,0:T(8,...) custom-call(bf16[4,384,256]{2,1,0:T(8,128)(2,1)} %get-tuple-element., ...), custom_call_target="tpu_custom_call" | custom-call | tf_op jit(solution)/shard_map/widen_gradients/pallas_call | solution.py:891
  (21 shorter events, 1.4 us)
Async XLA Ops:
  144.3 5.1 %copy-start.4 = (bf16[1024,1536]{1,0:T(8,128)(2,1)S(1)}, bf16[1024,1536]{1,0:T(8,128)(2,1)}, u32[]{:S(2)}) copy-start(bf16[1024,1536]{1,0:T(8,128)(2,1)} %get-tuple-element.69) | copy-start | bytes 9437188
  144.3 5.1 %copy-start.7 = (bf16[768,1024]{1,0:T(8,128)(2,1)S(1)}, bf16[768,1024]{1,0:T(8,128)(2,1)}, u32[]{:S(2)}) copy-start(bf16[768,1024]{1,0:T(8,128)(2,1)} %get-tuple-element.67) | copy-start | bytes 4718596
  149.4 2.6 copy-start.3
  149.5 2.6 copy-start.6
  152.1 7.3 %copy-start.5 = (bf16[1024,1536]{1,0:T(8,128)(2,1)S(1)}, bf16[1024,1536]{1,0:T(8,128)(2,1)}, u32[]{:S(2)}) copy-start(bf16[1024,1536]{1,0:T(8,128)(2,1)} %get-tuple-element.68) | copy-start | bytes 9437188
  159.4 2.6 copy-start.8
  164.7 6.5 %copy-start = (bf16[768,1024]{1,0:T(8,128)(2,1)}, bf16[768,1024]{1,0:T(8,128)(2,1)S(1)}, u32[]{:S(2)}) copy-start(bf16[768,1024]{1,0:T(8,128)(2,1)S(1)} %add_convert_fusion.refs_4_) | copy-start | bytes 4718596
  164.8 19.6 %collective-permute-start = (bf16[384,1024]{1,0:T(8,128)(2,1)S(1)}, bf16[384,1024]{1,0:T(8,128)(2,1)S(1)}, u32[]{:S(2)}, u32[]{:S(2)}) collective-permute-start(bf16[384,1024]{1,0:T(8,128)(2,1)S(1)} %slice.32), channel_id=1, source_target_pairs={{0,2},{1,3},{2,0},{3,1},{4,6},{5,7},{6,4},{7,5},{8,10},{9,11},{10,... | collective-permute-start | bytes 2359304 | tf_op jit(solution)/shard_map/ppermute | solution.py:1830
  184.4 0.9 copy-start.1
  294.6 103.9 %copy-start.2 = (f32[1536]{0:T(1024)S(1)}, f32[1536]{0:T(1024)}, u32[]{:S(2)}) copy-start(f32[1536]{0:T(1024)} %param.29) | copy-start | bytes 18436

commit v7 on v6

--- a/solution.py
+++ b/solution.py
@@ -536,9 +536,8 @@
         self.held, self.own, self.first, self.second, self.third, self.final = scratch
         self.send, self.recv, self.local = sems
         self.live = []
-        self.at_c, self.at_one, self.at_two, self.at_z, self.at_end, self.at_out = (
-            {} for _ in range(6)
-        )
+        self.at_c, self.at_one, self.at_two, self.at_z = {}, {}, {}, {}
+        self.at_end, self.at_last, self.at_out = {}, {}, {}
         r, s, z, c = place()
         self.r, self.z, self.c = r, z, c
         self.mate, self.along_x, self.along_y, self.along_z = peers_of(r, s, z, c)
@@ -765,14 +764,40 @@
 
     def send_final(self, m):
         final, r = self.final[m], self.r
+        targets = [self.along_x, self.along_y]
+        if m == self.count - 1:
+            targets.append(self.diagonal)
         self.at_end[m] = [
             self.remote(m, 13 + i, final.at[r], final.at[r], device)
-            for i, device in enumerate((self.along_x, self.along_y, self.diagonal))
+            for i, device in enumerate(targets)
         ]
 
     def stage_end(self, m):
         for copy in self.at_end[m]:
             copy.wait_recv()
+        if m == self.count - 1:
+            self.write(m)
+            return
+        final = self.final[m]
+
+        def part(quarter, which):
+            if self.kinds[m] == "columns":
+                return final.at[quarter, which]
+            half = final.shape[1] // 2
+            return final.at[quarter, pl.ds(which * half, half)]
+
+        from_x, from_y = part(self.along_x[0], 0), part(self.along_y[0], 1)
+        self.at_last[m] = [
+            self.remote(m, 15, from_x, from_x, self.along_y),
+            self.remote(m, 16, from_y, from_y, self.along_x),
+        ]
+
+    def stage_last(self, m):
+        for copy in self.at_last[m]:
+            copy.wait_recv()
+        self.write(m)
+
+    def write(self, m):
         out = pltpu.make_async_copy(self.final[m], self.outs[m], self.local.at[m, 4])
         out.start()
         self.at_out[m] = out
@@ -784,6 +809,8 @@
                 stage(now - late)
             if late == 0 and now + 2 < self.count:
                 self.begin(now + 2)
+        if 0 <= now - 5 < self.count - 1:
+            self.stage_last(now - 5)
 
     def ticks(self):
         return self.count + 4
@@ -795,7 +822,7 @@
             copy.wait_send()
 
 
-REDUCTION_SEMS = 16
+REDUCTION_SEMS = 17
 
 
 def reduction_memory(kinds, grads):
@@ -936,12 +963,8 @@
     small_held[0] = small_in[...]
     swap = swap_small(0, 0, reduction.mate)
     begin, core, early = reduction.begin, reduction.stage_core, reduction.stage_early
-    one, two, over_z, end = (
-        reduction.stage_one,
-        reduction.stage_two,
-        reduction.stage_z,
-        reduction.stage_end,
-    )
+    one, two, over_z = reduction.stage_one, reduction.stage_two, reduction.stage_z
+    end, last = reduction.stage_end, reduction.stage_last
     begin(0)
     begin(1)
     core(0)
@@ -973,8 +996,11 @@
     end(1)
     over_z(3)
     end(0)
+    last(1)
     end(2)
+    last(0)
     end(3)
+    last(2)
     for copy in spread:
         copy.wait_recv()
     small_got[6] = small_held[3]
@@ -1378,17 +1404,17 @@
         flow[:, pl.ds(i * 512, 512)] = back_tile(i, resid_low, 1024)
         fetch(i + 3)
     reduction.tick(0)
-    out_weight()
     loads[0].wait()
     loads[1].wait()
     branch_back()
-    reduction.tick(1)
     loads[2].wait()
     copies = scan_back()
-    reduction.tick(2)
+    out_weight()
+    reduction.tick(1)
     part_loads[2].wait()
     mixed_copy.wait_recv()
     mixed_save = mix_back()
+    reduction.tick(2)
     carry_back(copies)
     loads[3].wait()
     loads[4].wait()

time: 406 us -> 401 us (0.988)
  Pallas kernels: 352 us -> 346 us
    pallas_call x1, Pallas kernels: 99.4 us -> 94.4 us  [reduce_all(): pl.pallas_call(functools.partial(reduce_kernel, count, len(swapped)), out...]
where the time goes in v7:
time: 401 us; the launch traced here: 398 us
  Pallas kernels  346 us (86%)
  matrix products  36.4 us (9%)
  local copies, waits for them, and re-layouts  8.94 us (2%)
    pallas_call x1, Pallas kernels, forward_all(): pl.pallas_call(forward_kernel, out_shape=fulls + saved, in_specs=[VMEM] *...  138 us
    pallas_call x1, Pallas kernels, backward_all(): pl.pallas_call(functools.partial(backward_kernel, kinds), out_shape=out_s...  108 us
    pallas_call x1, Pallas kernels, reduce_all(): pl.pallas_call(functools.partial(reduce_kernel, count, len(swapped)), out...  94.4 us
    dot_general x3, matrix products, back_product(): lax.dot_general(grads, weight, (((1,), (1,)), ((), ())), preferred_elemen...  12.6 us
    dot_general x3, matrix products, outer(): lax.dot_general(left, right, (((0,), (0,)), ((), ())), preferred_element_...  12.4 us
    dot_general x3, matrix products, forward_product(): return jnp.dot(values, weight, preferred_element_type=jnp.float32)  11.4 us
  transfers between devices with their start and end apart: 1, of which 1 were waited for; matrix products, arithmetic and copies ran while one was open for 4% of the time, Pallas kernels for 0%

profile of v7, /device:TPU:0, one launch (start us, length us, event | category | flops | bytes accessed | tf_op | source)
XLA Modules:
  0.0 398.5 jit_solution(3640245284582806025)
XLA Ops:
  0.7 0.7 stack.24
  1.4 0.7 stack.25
  2.8 0.7 fusion.7
  3.5 1.3 pad_maximum_fusion.refs_11_.refs_25_
  4.8 1.4 concatenate.3.refs_12_.refs_26_
  6.2 138.1 %recurrent_forward.1 = (bf16[1024,1536]{1,0:T(8,128)(2,1)}, bf16[1536,1536]{1,0:T(8,128)(2,1)}, bf16[1536,1536]{1,0:T(8,128)(2,1)}, bf16[1024,1536]{1,0:T(8,128)...) custom-call(bf16[128,1536]{1,0:T(8,128)(2,1)} %refs_0_.1, ...), custom_call_target="tpu_custom_call" | custom-call | tf_op jit(solution)/shard_map/recurrent_forward/pallas_call | solution.py:492
  144.3 5.1 %fusion.9 = f32[768,1536]{1,0:T(8,128)S(1)} fusion(bf16[768,1024]{1,0:T(8,128)(2,1)} %get-tuple-element.67, bf16[1024,1536]{1,0:T(8,128)(2,1)} %get-tuple-element.68), kind=kOutput, calls=%fused_computation.26 | convolution fusion | flops 2415919104 | bytes 9437184 | tf_op jit(solution)/shard_map/dot_general | solution.py:1587
  149.5 2.6 fusion.10
  152.1 7.3 %multiply_convert_fusion = (bf16[768,1536]{1,0:T(8,128)(2,1)}, bf16[768,1536]{1,0:T(8,128)(2,1)S(1)}, bf16[768,1536]{1,0:T(8,128)(2,1)S(1)}) fusion(f32[768,1536]{1,0:T(8,128)S(1)} %fusion.9, f32[768,1536]{1,0:T(8,128)S(1)} %fusion.10, bf16[768,1024]{1,0:T(8,128)(2,1)S(1)} %copy-done.6, bf16[1536,1024]{1,0:T(8,128)(2,1)S(1)} %copy-done.3), kind=kOutput, calls=%fused_computation.9 | convolution fusion | flops 2446589952 | bytes 21233664 | tf_op jit(solution)/shard_map/dot_general | solution.py:1597
  159.4 2.6 fusion.11
  162.1 2.6 add_convert_fusion.refs_4_
  164.8 2.2 collective-permute-start
  167.0 4.2 %convolution_convert_fusion = bf16[1024,1536]{1,0:T(8,128)(2,1)} fusion(bf16[768,1024]{1,0:T(8,128)(2,1)S(1)} %copy-done.7, bf16[768,1536]{1,0:T(8,128)(2,1)S(1)} %copy-done.8), kind=kOutput, calls=%fused_computation.12 | convolution fusion | flops 2417491968 | bytes 7077888 | tf_op jit(solution)/shard_map/dot_general | solution.py:1591
  171.2 4.2 %convolution_convert_fusion.1 = bf16[1024,1536]{1,0:T(8,128)(2,1)} fusion(bf16[768,1024]{1,0:T(8,128)(2,1)S(1)} %copy-done.7, bf16[768,1536]{1,0:T(8,128)(2,1)S(1)} %get-tuple-element.122), kind=kOutput, calls=%fused_computation.13 | convolution fusion | flops 2417491968 | bytes 7077888 | tf_op jit(solution)/shard_map/dot_general | solution.py:1591
  175.3 4.1 %convolution_convert_fusion.2 = bf16[1536,1024]{1,0:T(8,128)(2,1)} fusion(bf16[768,1536]{1,0:T(8,128)(2,1)S(1)} %get-tuple-element.123, bf16[768,1024]{1,0:T(8,128)(2,1)S(1)} %copy-done.6), kind=kOutput, calls=%fused_computation.14 | convolution fusion | flops 2417491968 | bytes 7077888 | tf_op jit(solution)/shard_map/dot_general | solution.py:1591
  179.4 3.7 convolution_convert_fusion.3.refs_3_
  183.1 1.4 collective-permute-done.refs_5_
  184.4 0.9 copy-done.1
  185.3 107.8 %recurrent_backward.1 = (bf16[4,384,256]{2,1,0:T(8,128)(2,1)}, bf16[4,2,128,384]{3,2,1,0:T(8,128)(2,1)}, bf16[4,2,128,384]{3,2,1,0:T(8,128)(2,1)}, bf16[4,192,25...) custom-call(bf16[2,2,384,1024]{3,2,1,0:T(8,128)(2,1)} %bitcast.44, ...), custom_call_target="tpu_custom_call" | custom-call | tf_op jit(solution)/shard_map/recurrent_backward/pallas_call | solution.py:1489
  293.2 94.4 %reduce_grads.1 = (bf16[4,128,384]{2,1,0:T(8,128)(2,1)}, bf16[4,192,384]{2,1,0:T(8,128)(2,1)}, bf16[4,192,384]{2,1,0:T(8,128)(2,1)}, bf16[4,128,384]{2,1,0:T(8,128)(2,1)}, f32[16,1536]{1,0:T(8,128)}) custom-call(bf16[4,2,128,1536]{3,2,1,0:T(8,128)(2,1)} %bitcast.37, bf16[4,2,192,1536]{3,2,1,0:T(8,128)(2,1)} %bitcast.34, bf16[4,2,192,1536]{3,2,1,0:T(8,128)(2,1)} %bitcast.35, ...), custom_call_target="tpu_custom_call" | custom-call | tf_op jit(solution)/shard_map/reduce_grads/pallas_call | solution.py:1022
  387.6 1.4 fusion.8
  389.0 1.4 slice.26
  390.4 1.6 slice_reduce_fusion
  392.7 5.6 %widen_gradients.1 = (f32[384,1024]{1,0:T(8,128)}, f32[128,3072]{1,0:T(8,128)}, f32[128,3072]{1,0:T(8,128)}, f32[192,1024]{1,0:T(8,128)}, f32[128,1536]{1,0:T(8,...) custom-call(bf16[4,384,256]{2,1,0:T(8,128)(2,1)} %get-tuple-element., ...), custom_call_target="tpu_custom_call" | custom-call | tf_op jit(solution)/shard_map/widen_gradients/pallas_call | solution.py:918
  (21 shorter events, 1.4 us)
Async XLA Ops:
  144.3 5.1 %copy-start.4 = (bf16[1024,1536]{1,0:T(8,128)(2,1)S(1)}, bf16[1024,1536]{1,0:T(8,128)(2,1)}, u32[]{:S(2)}) copy-start(bf16[1024,1536]{1,0:T(8,128)(2,1)} %get-tuple-element.69) | copy-start | bytes 9437188
  144.3 5.1 %copy-start.7 = (bf16[768,1024]{1,0:T(8,128)(2,1)S(1)}, bf16[768,1024]{1,0:T(8,128)(2,1)}, u32[]{:S(2)}) copy-start(bf16[768,1024]{1,0:T(8,128)(2,1)} %get-tuple-element.67) | copy-start | bytes 4718596
  149.4 2.6 copy-start.3
  149.5 2.6 copy-start.6
  152.1 7.3 %copy-start.5 = (bf16[1024,1536]{1,0:T(8,128)(2,1)S(1)}, bf16[1024,1536]{1,0:T(8,128)(2,1)}, u32[]{:S(2)}) copy-start(bf16[1024,1536]{1,0:T(8,128)(2,1)} %get-tuple-element.68) | copy-start | bytes 9437188
  159.4 2.6 copy-start.8
  164.7 6.5 %copy-start = (bf16[768,1024]{1,0:T(8,128)(2,1)}, bf16[768,1024]{1,0:T(8,128)(2,1)S(1)}, u32[]{:S(2)}) copy-start(bf16[768,1024]{1,0:T(8,128)(2,1)S(1)} %add_convert_fusion.refs_4_) | copy-start | bytes 4718596
  164.8 19.6 %collective-permute-start = (bf16[384,1024]{1,0:T(8,128)(2,1)S(1)}, bf16[384,1024]{1,0:T(8,128)(2,1)S(1)}, u32[]{:S(2)}, u32[]{:S(2)}) collective-permute-start(bf16[384,1024]{1,0:T(8,128)(2,1)S(1)} %slice.32), channel_id=1, source_target_pairs={{0,2},{1,3},{2,0},{3,1},{4,6},{5,7},{6,4},{7,5},{8,10},{9,11},{10,... | collective-permute-start | bytes 2359304 | tf_op jit(solution)/shard_map/ppermute | solution.py:1856
  184.4 0.9 copy-start.1
  293.1 98.9 %copy-start.2 = (f32[1536]{0:T(1024)S(1)}, f32[1536]{0:T(1024)}, u32[]{:S(2)}) copy-start(f32[1536]{0:T(1024)} %param.29) | copy-start | bytes 18436

commit v8 on v7

--- a/solution.py
+++ b/solution.py
@@ -449,8 +449,8 @@
     carry_states(ends_copies)
     mix()
     arrive(4)
+    normed2_copy = out_product()
     tick(7)
-    normed2_copy = out_product()
     tick(8)
     tick(9)
     for m in (5, 6, 7):
@@ -1819,12 +1819,10 @@
     rec_width = w_rec.shape[1]
     flat_tokens = tokens.reshape(-1, model_width)
     gains = jnp.stack([norm1_gain, norm2_gain])
+    decay_scale = -8.0 * jax.nn.softplus(decay_param)
     vectors = jnp.concatenate(
-        [
-            conv_weight,
-            jnp.stack([conv_bias, rate_bias, input_bias, -8.0 * jax.nn.softplus(decay_param)]),
-        ]
-    )
+        [conv_weight.reshape(-1), conv_bias, rate_bias, input_bias, decay_scale]
+    ).reshape(8, rec_width)
     fulls, saved = forward_all(
         (w_rec, w_rate, w_input, w_branch, w_out, w_gate, w_up, w_down),
         cotangent.reshape(-1, model_width),

time: 401 us -> 400 us (level)
  no operation moved by 1% of the time
where the time goes in v8:
time: 400 us; the launch traced here: 398 us
  Pallas kernels  346 us (86%)
  matrix products  36.4 us (9%)
  local copies, waits for them, and re-layouts  8.93 us (2%)
    pallas_call x1, Pallas kernels, forward_all(): pl.pallas_call(forward_kernel, out_shape=fulls + saved, in_specs=[VMEM] *...  138 us
    pallas_call x1, Pallas kernels, backward_all(): pl.pallas_call(functools.partial(backward_kernel, kinds), out_shape=out_s...  108 us
    pallas_call x1, Pallas kernels, reduce_all(): pl.pallas_call(functools.partial(reduce_kernel, count, len(swapped)), out...  94.3 us
    dot_general x3, matrix products, back_product(): lax.dot_general(grads, weight, (((1,), (1,)), ((), ())), preferred_elemen...  12.6 us
    dot_general x3, matrix products, outer(): lax.dot_general(left, right, (((0,), (0,)), ((), ())), preferred_element_...  12.4 us
    dot_general x3, matrix products, forward_product(): return jnp.dot(values, weight, preferred_element_type=jnp.float32)  11.4 us
  transfers between devices with their start and end apart: 1, of which 1 were waited for; matrix products, arithmetic and copies ran while one was open for 4% of the time, Pallas kernels for 0%

profile of v8, /device:TPU:0, one launch (start us, length us, event | category | flops | bytes accessed | tf_op | source)
XLA Modules:
  0.0 398.4 jit_solution(10630508071217304836)
XLA Ops:
  0.7 0.8 reshape.79
  1.4 0.7 constant_dynamic-update-slice_fusion.2
  2.1 0.7 constant_dynamic-update-slice_fusion.1
  2.8 0.7 constant_dynamic-update-slice_fusion
  3.5 0.7 fusion.8
  4.9 1.3 pad_maximum_fusion.refs_11_.refs_25_
  6.2 138.1 %recurrent_forward.1 = (bf16[1024,1536]{1,0:T(8,128)(2,1)}, bf16[1536,1536]{1,0:T(8,128)(2,1)}, bf16[1536,1536]{1,0:T(8,128)(2,1)}, bf16[1024,1536]{1,0:T(8,128)...) custom-call(bf16[128,1536]{1,0:T(8,128)(2,1)} %refs_0_.1, ...), custom_call_target="tpu_custom_call" | custom-call | tf_op jit(solution)/shard_map/recurrent_forward/pallas_call | solution.py:492
  144.3 5.1 %fusion.10 = f32[768,1536]{1,0:T(8,128)S(1)} fusion(bf16[768,1024]{1,0:T(8,128)(2,1)} %get-tuple-element.67, bf16[1024,1536]{1,0:T(8,128)(2,1)} %get-tuple-element.68), kind=kOutput, calls=%fused_computation.31 | convolution fusion | flops 2415919104 | bytes 9437184 | tf_op jit(solution)/shard_map/dot_general | solution.py:1587
  149.5 2.6 fusion.11
  152.1 7.3 %multiply_convert_fusion = (bf16[768,1536]{1,0:T(8,128)(2,1)}, bf16[768,1536]{1,0:T(8,128)(2,1)S(1)}, bf16[768,1536]{1,0:T(8,128)(2,1)S(1)}) fusion(f32[768,1536]{1,0:T(8,128)S(1)} %fusion.10, f32[768,1536]{1,0:T(8,128)S(1)} %fusion.11, bf16[768,1024]{1,0:T(8,128)(2,1)S(1)} %copy-done.6, bf16[1536,1024]{1,0:T(8,128)(2,1)S(1)} %copy-done.3), kind=kOutput, calls=%fused_computation.9 | convolution fusion | flops 2446589952 | bytes 21233664 | tf_op jit(solution)/shard_map/dot_general | solution.py:1597
  159.4 2.6 fusion.12
  162.1 2.6 add_convert_fusion.refs_4_
  164.9 4.2 %convolution_convert_fusion = bf16[1024,1536]{1,0:T(8,128)(2,1)} fusion(bf16[768,1024]{1,0:T(8,128)(2,1)S(1)} %copy-done.7, bf16[768,1536]{1,0:T(8,128)(2,1)S(1)} %copy-done.8), kind=kOutput, calls=%fused_computation.12 | convolution fusion | flops 2417491968 | bytes 7077888 | tf_op jit(solution)/shard_map/dot_general | solution.py:1591
  169.1 4.1 %convolution_convert_fusion.1 = bf16[1024,1536]{1,0:T(8,128)(2,1)} fusion(bf16[768,1024]{1,0:T(8,128)(2,1)S(1)} %copy-done.7, bf16[768,1536]{1,0:T(8,128)(2,1)S(1)} %get-tuple-element.122), kind=kOutput, calls=%fused_computation.13 | convolution fusion | flops 2417491968 | bytes 7077888 | tf_op jit(solution)/shard_map/dot_general | solution.py:1591
  173.2 4.1 %convolution_convert_fusion.2 = bf16[1536,1024]{1,0:T(8,128)(2,1)} fusion(bf16[768,1536]{1,0:T(8,128)(2,1)S(1)} %get-tuple-element.123, bf16[768,1024]{1,0:T(8,128)(2,1)S(1)} %copy-done.6), kind=kOutput, calls=%fused_computation.14 | convolution fusion | flops 2417491968 | bytes 7077888 | tf_op jit(solution)/shard_map/dot_general | solution.py:1591
  177.3 3.7 convolution_convert_fusion.3.refs_3_
  180.9 3.5 collective-permute-done.refs_5_
  184.4 0.9 copy-done.1
  185.3 107.9 %recurrent_backward.1 = (bf16[4,384,256]{2,1,0:T(8,128)(2,1)}, bf16[4,2,128,384]{3,2,1,0:T(8,128)(2,1)}, bf16[4,2,128,384]{3,2,1,0:T(8,128)(2,1)}, bf16[4,192,25...) custom-call(bf16[2,2,384,1024]{3,2,1,0:T(8,128)(2,1)} %bitcast.44, ...), custom_call_target="tpu_custom_call" | custom-call | tf_op jit(solution)/shard_map/recurrent_backward/pallas_call | solution.py:1489
  293.2 94.3 %reduce_grads.1 = (bf16[4,128,384]{2,1,0:T(8,128)(2,1)}, bf16[4,192,384]{2,1,0:T(8,128)(2,1)}, bf16[4,192,384]{2,1,0:T(8,128)(2,1)}, bf16[4,128,384]{2,1,0:T(8,128)(2,1)}, f32[16,1536]{1,0:T(8,128)}) custom-call(bf16[4,2,128,1536]{3,2,1,0:T(8,128)(2,1)} %bitcast.37, bf16[4,2,192,1536]{3,2,1,0:T(8,128)(2,1)} %bitcast.34, bf16[4,2,192,1536]{3,2,1,0:T(8,128)(2,1)} %bitcast.35, ...), custom_call_target="tpu_custom_call" | custom-call | tf_op jit(solution)/shard_map/reduce_grads/pallas_call | solution.py:1022
  387.5 1.4 fusion.9
  389.0 1.4 slice.26
  390.4 1.6 slice_reduce_fusion
  392.6 5.6 %widen_gradients.1 = (f32[384,1024]{1,0:T(8,128)}, f32[128,3072]{1,0:T(8,128)}, f32[128,3072]{1,0:T(8,128)}, f32[192,1024]{1,0:T(8,128)}, f32[128,1536]{1,0:T(8,...) custom-call(bf16[4,384,256]{2,1,0:T(8,128)(2,1)} %get-tuple-element., ...), custom_call_target="tpu_custom_call" | custom-call | tf_op jit(solution)/shard_map/widen_gradients/pallas_call | solution.py:918
  (22 shorter events, 1.4 us)
Async XLA Ops:
  144.3 5.1 %copy-start.4 = (bf16[1024,1536]{1,0:T(8,128)(2,1)S(1)}, bf16[1024,1536]{1,0:T(8,128)(2,1)}, u32[]{:S(2)}) copy-start(bf16[1024,1536]{1,0:T(8,128)(2,1)} %get-tuple-element.69) | copy-start | bytes 9437188
  144.3 5.1 %copy-start.7 = (bf16[768,1024]{1,0:T(8,128)(2,1)S(1)}, bf16[768,1024]{1,0:T(8,128)(2,1)}, u32[]{:S(2)}) copy-start(bf16[768,1024]{1,0:T(8,128)(2,1)} %get-tuple-element.67) | copy-start | bytes 4718596
  149.4 2.6 copy-start.3
  149.4 2.6 copy-start.6
  152.1 7.3 %copy-start.5 = (bf16[1024,1536]{1,0:T(8,128)(2,1)S(1)}, bf16[1024,1536]{1,0:T(8,128)(2,1)}, u32[]{:S(2)}) copy-start(bf16[1024,1536]{1,0:T(8,128)(2,1)} %get-tuple-element.68) | copy-start | bytes 9437188
  159.4 2.6 copy-start.8
  164.7 4.4 %copy-start = (bf16[768,1024]{1,0:T(8,128)(2,1)}, bf16[768,1024]{1,0:T(8,128)(2,1)S(1)}, u32[]{:S(2)}) copy-start(bf16[768,1024]{1,0:T(8,128)(2,1)S(1)} %add_convert_fusion.refs_4_) | copy-start | bytes 4718596
  164.8 19.6 %collective-permute-start = (bf16[384,1024]{1,0:T(8,128)(2,1)S(1)}, bf16[384,1024]{1,0:T(8,128)(2,1)S(1)}, u32[]{:S(2)}, u32[]{:S(2)}) collective-permute-start(bf16[384,1024]{1,0:T(8,128)(2,1)S(1)} %slice.32), channel_id=1, source_target_pairs={{0,2},{1,3},{2,0},{3,1},{4,6},{5,7},{6,4},{7,5},{8,10},{9,11},{10,... | collective-permute-start | bytes 2359304 | tf_op jit(solution)/shard_map/ppermute | solution.py:1854
  184.4 0.9 copy-start.1
  293.2 98.8 %copy-start.2 = (f32[1536]{0:T(1024)S(1)}, f32[1536]{0:T(1024)}, u32[]{:S(2)}) copy-start(f32[1536]{0:T(1024)} %param.29) | copy-start | bytes 18436
